TPU v7x, 32 devices: a whole 2x2x4 slice. The times are simulated.
32 devices in a mesh: seq: 8 (over y, x, core), tensor: 4 (over z).
Axes of the slice: x: 2, y: 2, z: 4, core: 2. Of those that a mesh axis runs over, the one named last changes fastest.
Arguments:
- layer_input: bfloat16 [8, 2048, 2048], P('tensor', 'seq'), may hold values from -6 to 6
- segment_ids: int32 [8, 2048], replicated, may hold values from 0 to 3, never falling along the last dimension, each value on 1 to 1024 neighbouring positions
- cotangent: bfloat16 [8, 2048, 2048], P('tensor', 'seq'), may hold values from -6 to 6
- projections: bfloat16 [2048, 3, 2048], P('seq', None, 'tensor'), may hold values from -0.125 to 0.125
- output_weight: bfloat16 [2048, 2048], P('tensor', 'seq'), may hold values from -0.125 to 0.125
- up_weight: bfloat16 [2048, 8192], P('seq', 'tensor'), may hold values from -0.125 to 0.125
- down_weight: bfloat16 [8192, 2048], P('tensor', 'seq'), may hold values from -0.0625 to 0.0625
- norm_gains: bfloat16 [3, 2048], P(None, 'seq'), may hold values from 0.5 to 1.5
- hidden_gain: bfloat16 [4, 2048], P('tensor', 'seq'), may hold values from 0.5 to 1.5
- decays: float32 [6], replicated, may hold values from 0.8 to 0.99
- average_projections: float32 [2048, 3, 2048], P('seq', None, 'tensor'), may hold values from -6 to 6
- average_output: float32 [2048, 2048], P('tensor', 'seq'), may hold values from -6 to 6
- average_up: float32 [2048, 8192], P('seq', 'tensor'), may hold values from -6 to 6
- average_down: float32 [8192, 2048], P('tensor', 'seq'), may hold values from -6 to 6
- average_gains: float32 [3, 2048], P(None, 'seq'), may hold values from -6 to 6
- average_hidden: float32 [4, 2048], P('tensor', 'seq'), may hold values from -6 to 6
Outputs:
- layer_output: bfloat16 [8, 2048, 2048], P('tensor', 'seq')
- input_grad: float32 [8, 2048, 2048], P('tensor', 'seq')
- projections_grad: float32 [2048, 3, 2048], P('seq', None, 'tensor')
- output_weight_grad: float32 [2048, 2048], P('tensor', 'seq')
- up_weight_grad: float32 [2048, 8192], P('seq', 'tensor')
- down_weight_grad: float32 [8192, 2048], P('tensor', 'seq')
- gains_grad: float32 [3, 2048], P(None, 'seq')
- hidden_gain_grad: float32 [4, 2048], P('tensor', 'seq')
- new_average_projections: float32 [2048, 3, 2048], P('seq', None, 'tensor')
- new_average_output: float32 [2048, 2048], P('tensor', 'seq')
- new_average_up: float32 [2048, 8192], P('seq', 'tensor')
- new_average_down: float32 [8192, 2048], P('tensor', 'seq')
- new_average_gains: float32 [3, 2048], P(None, 'seq')
- new_average_hidden: float32 [4, 2048], P('tensor', 'seq')
Inputs may be any that keep to these rules, and one draw needn't show every extreme that they name: `segment_ids`: segment ids never fall along a sequence; each document has 1 to 1024 positions.
All inputs are finite; a program needn't handle non-finite values.
Results may differ from a plain program's by a relative error of at most 0.02.
Values may be sent and summed in bfloat16 or wider, within the bound.
No kernel may reach another device: no remote copies, remote signals or barrier semaphores. Data moves between devices by JAX's collectives and lax.ppermute only.
A program may use at most 448 MiB of HBM per device.

v0:
```python
from functools import partial

import jax
import jax.numpy as jnp
from jax import lax
from jax.sharding import PartitionSpec as P

HEAD_DIM = 64
SEQ_LEN = 2048
SCALE_BASE = 512


EPSILON = 1e-05
MASKED_SCORE = -1e30


def norm_rows(features, gain_row):
    row_mean = jnp.mean(features, axis=-1, keepdims=True)
    second = jnp.mean(features * features, axis=-1, keepdims=True)
    return (features - row_mean) * lax.rsqrt(second - row_mean * row_mean + EPSILON) * gain_row


def xpos_tables(positions):
    half_dim = HEAD_DIM // 2
    pair_index = jnp.arange(half_dim, dtype=jnp.float32)
    frequency = 10000.0 ** (-pair_index / half_dim)
    angles = positions[:, None] * frequency[None, :]
    zeta_base = (pair_index / half_dim + 0.4) / 1.4
    growth = zeta_base[None, :] ** ((positions[:, None] - SEQ_LEN // 2) / SCALE_BASE)
    return (jnp.cos(angles)[:, None, :], jnp.sin(angles)[:, None, :], growth[:, None, :])


def xpos_turn(features, cosine, sine_table, factor_row):
    half_dim = features.shape[-1] // 2
    lower_half = features[..., :half_dim]
    upper_half = features[..., half_dim:]
    return jnp.concatenate(
        [
            (lower_half * cosine - upper_half * sine_table) * factor_row,
            (upper_half * cosine + lower_half * sine_table) * factor_row,
        ],
        axis=-1,
    )


def xpos_back(features, cosine, sine_table, factor_row):
    half_dim = features.shape[-1] // 2
    lower_half = features[..., :half_dim] * factor_row
    upper_half = features[..., half_dim:] * factor_row
    return jnp.concatenate(
        [
            lower_half * cosine + upper_half * sine_table,
            upper_half * cosine - lower_half * sine_table,
        ],
        axis=-1,
    )


def to_heads(features, head_count):
    shaped = features.reshape(features.shape[0], features.shape[1], head_count, HEAD_DIM)
    return jnp.moveaxis(shaped, 2, 0)


def from_heads(features):
    merged = jnp.moveaxis(features, 0, 2)
    return merged.reshape(merged.shape[0], merged.shape[1], -1)


def share_rows(features):
    return lax.all_gather(features, "tensor", axis=0, tiled=True)


def spread_sum(features):
    return lax.psum_scatter(
        features.astype(jnp.bfloat16), "tensor", scatter_dimension=0, tiled=True
    ).astype(jnp.float32)


def row_totals(first_sum, second_sum):
    return lax.psum((first_sum, second_sum), "tensor")


def split_norm(features):
    columns = features.shape[-1] * lax.axis_size("tensor")
    row_sum, row_square = row_totals(
        jnp.sum(features, axis=-1), jnp.sum(features * features, axis=-1)
    )
    row_mean = (row_sum / columns)[..., None]
    second = (row_square / columns)[..., None]
    inverse = lax.rsqrt(second - row_mean * row_mean + EPSILON)
    return ((features - row_mean) * inverse, inverse)


def split_norm_back(scaled_grad, normed, inverse):
    columns = scaled_grad.shape[-1] * lax.axis_size("tensor")
    grad_sum, grad_cross = row_totals(
        jnp.sum(scaled_grad, axis=-1), jnp.sum(scaled_grad * normed, axis=-1)
    )
    return inverse * (
        scaled_grad - (grad_sum / columns)[..., None] - normed * (grad_cross / columns)[..., None]
    )


def probabilities(head_query, head_key, head_total, mask_rows, factor):
    scores = (
        jnp.einsum("sid,sjd->sij", head_query, head_key, preferred_element_type=jnp.float32)
        * factor
    )
    scores = jnp.where(mask_rows, scores, MASKED_SCORE)
    return jnp.exp(scores - head_total[..., None])


def on_device(
    layer_input,
    segment_ids,
    cotangent,
    projections,
    output_weight,
    up_weight,
    down_weight,
    norm_gains,
    hidden_gain,
    decays,
    average_projections,
    average_output,
    average_up,
    average_down,
    average_gains,
    average_hidden,
):
    full_proj, full_output, full_up, full_down, gains_all, hidden_all = (
        lax.all_gather(projections, "seq", axis=0, tiled=True),
        lax.all_gather(output_weight, "seq", axis=1, tiled=True),
        lax.all_gather(up_weight, "seq", axis=0, tiled=True),
        lax.all_gather(down_weight, "seq", axis=1, tiled=True),
        lax.all_gather(norm_gains, "seq", axis=1, tiled=True),
        lax.all_gather(hidden_gain, "seq", axis=1, tiled=True),
    )
    row_count = layer_input.shape[1]
    model_width = layer_input.shape[2]
    sequence_count = segment_ids.shape[0]
    full_length = segment_ids.shape[1]
    head_cols = full_proj.shape[2]
    heads_here = head_cols // HEAD_DIM
    factor = HEAD_DIM ** (-0.5)
    offset = lax.axis_index("seq") * row_count
    column_start = lax.axis_index("tensor") * head_cols
    own_places = offset + jnp.arange(row_count, dtype=jnp.int32)
    cosine, sine_table, growth = xpos_tables(own_places.astype(jnp.float32))
    all_places = jnp.arange(full_length, dtype=jnp.int32)
    own_segments = lax.dynamic_slice_in_dim(segment_ids, offset, row_count, 1)
    allowed = (own_places[None, :, None] >= all_places[None, None, :]) & (
        own_segments[:, :, None] == segment_ids[:, None, :]
    )
    gain_attn = gains_all[0].astype(jnp.float32)
    gain_inner = lax.dynamic_slice_in_dim(gains_all[1], column_start, head_cols, 0).astype(
        jnp.float32
    )
    gain_ffn = gains_all[2].astype(jnp.float32)
    gain_hidden = hidden_all[0].astype(jnp.float32)
    inputs = layer_input.astype(jnp.float32)
    normed_in = share_rows(norm_rows(inputs, gain_attn).astype(jnp.bfloat16))
    projected = jnp.einsum(
        "srd,dce->srce", normed_in, full_proj, preferred_element_type=jnp.float32
    )
    head_shape = (sequence_count, row_count, heads_here, HEAD_DIM)
    queries = xpos_turn(projected[:, :, 0].reshape(head_shape), cosine, sine_table, growth).astype(
        jnp.bfloat16
    )
    key_rows = xpos_turn(
        projected[:, :, 1].reshape(head_shape), cosine, sine_table, 1.0 / growth
    ).astype(jnp.bfloat16)
    key_rows = key_rows.reshape(sequence_count, row_count, head_cols)
    values = projected[:, :, 2].astype(jnp.bfloat16)
    all_keys, all_values = (
        lax.all_gather(key_rows, "seq", axis=1, tiled=True),
        lax.all_gather(values, "seq", axis=1, tiled=True),
    )
    query_heads = jnp.moveaxis(queries, 2, 0)
    key_heads = to_heads(all_keys, heads_here)
    value_heads = to_heads(all_values, heads_here)

    def attend_head(bundle):
        head_query, head_key, head_value = bundle
        scores = (
            jnp.einsum("sid,sjd->sij", head_query, head_key, preferred_element_type=jnp.float32)
            * factor
        )
        scores = jnp.where(allowed, scores, MASKED_SCORE)
        row_max = jnp.max(scores, axis=-1, keepdims=True)
        exponent = jnp.exp(scores - row_max)
        denominator = jnp.sum(exponent, axis=-1, keepdims=True)
        weights = (exponent / denominator).astype(jnp.bfloat16)
        result = jnp.einsum("sij,sjd->sid", weights, head_value, preferred_element_type=jnp.float32)
        return (result, (row_max + jnp.log(denominator))[..., 0])

    attended_heads, log_totals = lax.map(attend_head, (query_heads, key_heads, value_heads))
    attended = from_heads(attended_heads)
    inner_normed, inner_inverse = split_norm(attended)
    inner_rows = (inner_normed * gain_inner).astype(jnp.bfloat16)
    residual = inputs + spread_sum(
        jnp.einsum("srk,kd->srd", inner_rows, full_output, preferred_element_type=jnp.float32)
    )
    normed_mid = share_rows(norm_rows(residual, gain_ffn).astype(jnp.bfloat16))
    hidden = jnp.einsum("srd,df->srf", normed_mid, full_up, preferred_element_type=jnp.float32)
    activated = jax.nn.gelu(hidden, approximate=False)
    hidden_normed, hidden_inverse = split_norm(activated)
    squeezed = (hidden_normed * gain_hidden).astype(jnp.bfloat16)
    layer_output = (
        residual
        + spread_sum(
            jnp.einsum("srf,fd->srd", squeezed, full_down, preferred_element_type=jnp.float32)
        )
    ).astype(jnp.bfloat16)
    cotangents = cotangent.astype(jnp.float32)
    ffn_grad = share_rows(cotangent)
    down_grad = jnp.einsum("srf,srd->fd", squeezed, ffn_grad, preferred_element_type=jnp.float32)
    squeezed_grad = jnp.einsum(
        "srd,fd->srf", ffn_grad, full_down, preferred_element_type=jnp.float32
    )
    hidden_gain_grad = jnp.sum(squeezed_grad * hidden_normed, axis=(0, 1))
    activated_grad = split_norm_back(squeezed_grad * gain_hidden, hidden_normed, hidden_inverse)
    gelu_pullback = jax.vjp(partial(jax.nn.gelu, approximate=False), hidden)[1]
    hidden_grad = gelu_pullback(activated_grad)[0].astype(jnp.bfloat16)
    up_grad = jnp.einsum("srd,srf->df", normed_mid, hidden_grad, preferred_element_type=jnp.float32)
    mid_grad = spread_sum(
        jnp.einsum("srf,df->srd", hidden_grad, full_up, preferred_element_type=jnp.float32)
    )
    mid_pullback = jax.vjp(norm_rows, residual, gain_ffn)[1]
    residual_part, ffn_gain_grad = mid_pullback(mid_grad)
    residual_grad = cotangents + residual_part
    attn_grad = share_rows(residual_grad.astype(jnp.bfloat16))
    output_grad = jnp.einsum(
        "srk,srd->kd", inner_rows, attn_grad, preferred_element_type=jnp.float32
    )
    inner_grad = jnp.einsum(
        "srd,kd->srk", attn_grad, full_output, preferred_element_type=jnp.float32
    )
    inner_gain_grad = jnp.sum(inner_grad * inner_normed, axis=(0, 1))
    attended_grad = split_norm_back(inner_grad * gain_inner, inner_normed, inner_inverse).astype(
        jnp.bfloat16
    )
    grad_heads = to_heads(attended_grad, heads_here)

    def back_head(bundle):
        head_query, head_key, head_value, head_grad, head_total = bundle
        chances = probabilities(head_query, head_key, head_total, allowed, factor)
        product = jnp.einsum(
            "sid,sjd->sij", head_grad, head_value, preferred_element_type=jnp.float32
        )
        spread = jnp.sum(chances * product, axis=-1, keepdims=True)
        score_grad = (chances * (product - spread)).astype(jnp.bfloat16)
        query_grad = (
            jnp.einsum("sij,sjd->sid", score_grad, head_key, preferred_element_type=jnp.float32)
            * factor
        )
        key_grad = (
            jnp.einsum("sij,sid->sjd", score_grad, head_query, preferred_element_type=jnp.float32)
            * factor
        )
        value_grad = jnp.einsum(
            "sij,sid->sjd",
            chances.astype(jnp.bfloat16),
            head_grad,
            preferred_element_type=jnp.float32,
        )
        return (query_grad, key_grad, value_grad)

    query_grads, key_parts, value_parts = lax.map(
        back_head, (query_heads, key_heads, value_heads, grad_heads, log_totals)
    )
    key_grads, value_grads = (
        lax.psum_scatter(
            from_heads(key_parts).astype(jnp.bfloat16), "seq", scatter_dimension=1, tiled=True
        ).astype(jnp.float32),
        lax.psum_scatter(
            from_heads(value_parts).astype(jnp.bfloat16), "seq", scatter_dimension=1, tiled=True
        ).astype(jnp.float32),
    )
    query_raw = xpos_back(jnp.moveaxis(query_grads, 0, 2), cosine, sine_table, growth)
    key_raw = xpos_back(key_grads.reshape(head_shape), cosine, sine_table, 1.0 / growth)
    projected_grad = jnp.stack(
        [
            query_raw.reshape(sequence_count, row_count, head_cols),
            key_raw.reshape(sequence_count, row_count, head_cols),
            value_grads,
        ],
        axis=2,
    ).astype(jnp.bfloat16)
    proj_grad = jnp.einsum(
        "srd,srce->dce", normed_in, projected_grad, preferred_element_type=jnp.float32
    )
    input_part = spread_sum(
        jnp.einsum("srce,dce->srd", projected_grad, full_proj, preferred_element_type=jnp.float32)
    )
    input_pullback = jax.vjp(norm_rows, inputs, gain_attn)[1]
    input_norm_grad, attn_gain_grad = input_pullback(input_part)
    input_grad = residual_grad + input_norm_grad
    inner_full = lax.dynamic_update_slice_in_dim(
        jnp.zeros((model_width,), jnp.float32), inner_gain_grad, column_start, 0
    )
    gain_terms = jnp.stack([attn_gain_grad, inner_full, ffn_gain_grad])
    summed_grads = (
        lax.psum_scatter(
            proj_grad.astype(jnp.bfloat16), "seq", scatter_dimension=0, tiled=True
        ).astype(jnp.float32),
        lax.psum_scatter(
            output_grad.astype(jnp.bfloat16), "seq", scatter_dimension=1, tiled=True
        ).astype(jnp.float32),
        lax.psum_scatter(
            up_grad.astype(jnp.bfloat16), "seq", scatter_dimension=0, tiled=True
        ).astype(jnp.float32),
        lax.psum_scatter(
            down_grad.astype(jnp.bfloat16), "seq", scatter_dimension=1, tiled=True
        ).astype(jnp.float32),
        lax.psum_scatter(
            gain_terms.astype(jnp.bfloat16), "seq", scatter_dimension=1, tiled=True
        ).astype(jnp.float32),
        lax.psum_scatter(
            hidden_gain_grad[None, :].astype(jnp.bfloat16), "seq", scatter_dimension=1, tiled=True
        ).astype(jnp.float32),
    )
    gains_total = lax.psum(summed_grads[4], "tensor")
    final_grads = (
        summed_grads[0],
        summed_grads[1],
        summed_grads[2],
        summed_grads[3],
        gains_total,
        summed_grads[5],
    )
    averages = (
        average_projections,
        average_output,
        average_up,
        average_down,
        average_gains,
        average_hidden,
    )
    updated = tuple(
        (
            decays[member] * averages[member] + (1.0 - decays[member]) * final_grads[member]
            for member in range(6)
        )
    )
    return (
        layer_output,
        input_grad,
        final_grads[0],
        final_grads[1],
        final_grads[2],
        final_grads[3],
        final_grads[4],
        final_grads[5],
        updated[0],
        updated[1],
        updated[2],
        updated[3],
        updated[4],
        updated[5],
    )


def solution(mesh):
    return jax.shard_map(
        on_device,
        mesh=mesh,
        in_specs=(
            P("tensor", "seq", None),
            P(),
            P("tensor", "seq", None),
            P("seq", None, "tensor"),
            P("tensor", "seq"),
            P("seq", "tensor"),
            P("tensor", "seq"),
            P(None, "seq"),
            P("tensor", "seq"),
            P(),
            P("seq", None, "tensor"),
            P("tensor", "seq"),
            P("seq", "tensor"),
            P("tensor", "seq"),
            P(None, "seq"),
            P("tensor", "seq"),
        ),
        out_specs=(
            P("tensor", "seq", None),
            P("tensor", "seq", None),
            P("seq", None, "tensor"),
            P("tensor", "seq"),
            P("seq", "tensor"),
            P("tensor", "seq"),
            P(None, "seq"),
            P("tensor", "seq"),
            P("seq", None, "tensor"),
            P("tensor", "seq"),
            P("seq", "tensor"),
            P("tensor", "seq"),
            P(None, "seq"),
            P("tensor", "seq"),
        ),
        check_vma=False,
    )
```

profile of v0, /device:TPU:0, one launch (start us, length us, event | category | flops | bytes accessed | tf_op | source)
XLA Modules:
  0.0 3037.4 jit_solution(15116826409711250024)
XLA Ops:
  8.0 10.5 all_gather.36
  24.8 33.4 %all-gather.14.cloned.1.call-done = bf16[2048,3,512]{2,0,1:T(8,128)(2,1)} async-done(((bf16[256,3,512]{2,0,1:T(8,128)(2,1)}), bf16[2048,3,512]{2,0,1:T(8,128)(2,1)}) %all-gather.14.cloned.1.call-update) | async-done | bytes 6291472 | tf_op jit(solution)/shard_map/all_gather | solution.py:132
  58.2 151.8 %all-gather.12.cloned.1.call-done = bf16[8,256,2048]{2,1,0:T(8,128)(2,1)} async-done(((bf16[2,256,2048]{2,1,0:T(8,128)(2,1)}), bf16[8,256,2048]{2,1,0:T(8,128)(2,1)}) %all-gather.12.cloned.1.call-update) | async-done | bytes 8388624 | tf_op jit(solution)/shard_map/all_gather | solution.py:70
  210.0 17.1 fusion.66
  257.0 85.4 %all-gather.16.cloned.1.call-done = bf16[8,2048,512]{1,2,0:T(8,128)(2,1)} async-done(((bf16[8,256,512]{1,2,0:T(8,128)(2,1)}), bf16[8,2048,512]{1,2,0:T(8,128)(2,1)}) %all-gather.16.cloned.1.call-update) | async-done | bytes 16777232 | tf_op jit(solution)/shard_map/all_gather | solution.py:176
  342.3 14.5 copy.73
  356.8 77.7 %all-gather.30.cloned.1.call-done = bf16[8,2048,1,512]{3,1,2,0:T(8,128)(2,1)} async-done(((bf16[8,256,1,512]{3,1,2,0:T(8,128)(2,1)}), bf16[8,2048,1,512]{3,1,2,0:T(8,128)(2,1)}) %all-gather.30.cloned.1.call-update) | async-done | bytes 16777232 | tf_op jit(solution)/shard_map/all_gather | solution.py:177
  434.6 21.8 copy.71
  456.4 14.1 copy.74
  473.0 180.4 %while.28 = (s32[]{:T(128)}, f32[8,8,256,64]{2,3,0,1:T(8,128)}, f32[8,8,256]{2,1,0:T(8,128)}, bf16[8,8,256,64]{2,3,1,0:T(8,128)(2,1)S(1)}, bf16[8,8,2048,64]{2,3...) while((s32[]{:T(128)}, f32[8,8,256,64]{2,3,0,1:T(8,128)}, ...), condition=%wide.region_5.6_spmd.clone, body=%wide.region_2.5_spmd.clone.sunk | while | flops 1149237248 | bytes 57174628 | solution.py:197
  662.4 19.2 all-reduce.3
  681.7 10.7 convolution_convert_fusion
  693.3 141.2 %reduce-scatter.17.cloned.1.call-done = bf16[2,256,2048]{2,1,0:T(8,128)(2,1)} async-done(((bf16[8,256,2048]{2,1,0:T(8,128)(2,1)}), bf16[2,256,2048]{2,1,0:T(8,128)(2,1)}) %reduce-scatter.17.cloned.1.call-update) | async-done | bytes 2097168 | tf_op jit(solution)/shard_map/reduce_scatter | solution.py:74
  851.0 40.5 %all-gather.22.cloned.1.call-done = bf16[2048,2048]{1,0:T(8,128)(2,1)} async-done(((bf16[256,2048]{1,0:T(8,128)(2,1)}), bf16[2048,2048]{1,0:T(8,128)(2,1)}) %all-gather.22.cloned.1.call-update) | async-done | bytes 8388624 | tf_op jit(solution)/shard_map/all_gather | solution.py:134
  891.5 151.8 %all-gather.20.cloned.1.call-done = bf16[8,256,2048]{2,1,0:T(8,128)(2,1)} async-done(((bf16[2,256,2048]{2,1,0:T(8,128)(2,1)}), bf16[8,256,2048]{2,1,0:T(8,128)(2,1)}) %all-gather.20.cloned.1.call-update) | async-done | bytes 8388624 | tf_op jit(solution)/shard_map/all_gather | solution.py:70
  1043.3 29.0 fusion.106
  1072.4 43.2 %fusion.121 = (f32[8,256]{1,0:T(8,128)S(1)}, f32[8,256]{1,0:T(8,128)S(1)}, f32[8,256,2048]{2,1,0:T(8,128)}, f32[8,256,2048]{2,1,0:T(8,128)}) fusion(f32[8,256,2048]{2,1,0:T(8,128)S(1)} %get-tuple-element.335, u8[256,2048]{1,0:T(8,128)(4,1)S(1)} %get-tuple-element.211, u8[256,2048]{1,0:T(8,128)(4,1)S(1)} %get-tuple-element.212, ...), kind=kLoop, calls=%fused_computation.220 | loop fusion | flops 310374400 | bytes 51920896 | tf_op jit(solution)/shard_map/reduce_sum | solution.py:86
  1115.6 18.4 all-reduce.2
  1134.0 59.2 %all-gather.26.cloned.1.call-done = bf16[8,256,2048]{2,1,0:T(8,128)(2,1)} async-done(((bf16[2,256,2048]{2,1,0:T(8,128)(2,1)}), bf16[8,256,2048]{2,1,0:T(8,128)(2,1)}) %all-gather.26.cloned.1.call-update) | async-done | bytes 8388624 | tf_op jit(solution)/shard_map/all_gather | solution.py:70
  1193.3 56.0 %all-gather.24.cloned.1.call-done = bf16[2048,2048]{1,0:T(8,128)(2,1)} async-done(((bf16[2048,256]{1,0:T(8,128)(2,1)}), bf16[2048,2048]{1,0:T(8,128)(2,1)}) %all-gather.24.cloned.1.call-update) | async-done | bytes 8388624 | tf_op jit(solution)/shard_map/all_gather | solution.py:135
  1249.3 28.0 multiply_reduce_fusion.1
  1277.2 19.2 all-reduce.1
  1296.5 23.6 add_convert_fusion
  1323.4 21.3 fusion.78
  1344.8 141.8 %reduce-scatter.21.cloned.1.call-done = bf16[2,256,2048]{2,1,0:T(8,128)(2,1)} async-done(((bf16[8,256,2048]{2,1,0:T(8,128)(2,1)}), bf16[2,256,2048]{2,1,0:T(8,128)(2,1)}) %reduce-scatter.21.cloned.1.call-update) | async-done | bytes 2097168 | tf_op jit(solution)/shard_map/reduce_scatter | solution.py:74
  1495.1 150.3 %all-gather.28.cloned.1.call-done = bf16[8,256,2048]{2,1,0:T(8,128)(2,1)} async-done(((bf16[2,256,2048]{2,1,0:T(8,128)(2,1)}), bf16[8,256,2048]{2,1,0:T(8,128)(2,1)}) %all-gather.28.cloned.1.call-update) | async-done | bytes 8388624 | tf_op jit(solution)/shard_map/all_gather | solution.py:70
  1645.3 13.4 multiply_reduce_fusion.5
  1658.8 15.7 all-reduce
  1685.0 466.9 %while.29 = (s32[]{:T(128)}, f32[8,8,256,64]{2,3,0,1:T(8,128)}, bf16[8,8,2048,64]{2,3,0,1:T(8,128)(2,1)}, bf16[8,8,2048,64]{2,3,0,1:T(8,128)(2,1)}, bf16[8,8,256...) while((s32[]{:T(128)}, f32[8,8,256,64]{2,3,0,1:T(8,128)}, ...), condition=%wide.region_31.32_spmd.clone, body=%wide.region_29.31_spmd.clone.sunk | while | flops 2731669504 | bytes 193058032 | solution.py:269
  1685.1 9.7 fusion.161
  1695.5 15.2 multiply_reduce_fusion.10
  1710.7 15.0 multiply_convert_fusion.14
  1753.8 15.2 multiply_reduce_fusion.10
  1769.0 15.0 multiply_convert_fusion.14
  1801.6 9.7 fusion.161
  1812.0 15.2 multiply_reduce_fusion.10
  1827.3 15.0 multiply_convert_fusion.14
  1870.3 15.2 multiply_reduce_fusion.10
  1885.6 15.0 multiply_convert_fusion.14
  1928.6 15.2 multiply_reduce_fusion.10
  1943.9 15.0 multiply_convert_fusion.14
  1986.9 15.2 multiply_reduce_fusion.10
  2002.2 15.0 multiply_convert_fusion.14
  2045.3 15.2 multiply_reduce_fusion.10
  2060.5 15.0 multiply_convert_fusion.14
  2103.6 15.2 multiply_reduce_fusion.10
  2118.9 15.0 multiply_convert_fusion.14
  2152.1 23.2 copy.85
  2177.2 25.3 bitcast_convert_fusion
  2202.6 24.0 bitcast_convert_fusion.1
  2227.4 10.8 bitcast_convert_fusion.4
  2238.3 28.2 reduce-scatter.23.cloned.1.call-done
  2278.3 107.6 %reduce-scatter.25.cloned.1.call-done = bf16[8,256,512]{2,1,0:T(8,128)(2,1)} async-done(((bf16[8,2048,512]{2,1,0:T(8,128)(2,1)}), bf16[8,256,512]{2,1,0:T(8,128)(2,1)}) %reduce-scatter.25.cloned.1.call-update) | async-done | bytes 2097168 | tf_op jit(solution)/shard_map/reduce_scatter | solution.py:276
  2385.9 19.3 bitcast_convert_fusion.3
  2406.8 18.8 bitcast_convert_fusion.2
  2425.6 25.4 fusion.81
  2458.4 40.2 %reduce-scatter.35.cloned.1.call-done = bf16[2048,256]{1,0:T(8,128)(2,1)} async-done(((bf16[2048,2048]{1,0:T(8,128)(2,1)}), bf16[2048,256]{1,0:T(8,128)(2,1)}) %reduce-scatter.35.cloned.1.call-update) | async-done | bytes 1048592 | tf_op jit(solution)/shard_map/reduce_scatter | solution.py:313
  2502.8 70.4 %reduce-scatter.33.cloned.1.call-done = bf16[256,2048]{1,0:T(8,128)(2,1)} async-done(((bf16[2048,2048]{1,0:T(8,128)(2,1)}), bf16[256,2048]{1,0:T(8,128)(2,1)}) %reduce-scatter.33.cloned.1.call-update) | async-done | bytes 1048592 | tf_op jit(solution)/shard_map/reduce_scatter | solution.py:310
  2578.4 40.1 %reduce-scatter.31.cloned.1.call-done = bf16[512,256]{1,0:T(8,128)(2,1)} async-done(((bf16[512,2048]{1,0:T(8,128)(2,1)}), bf16[512,256]{1,0:T(8,128)(2,1)}) %reduce-scatter.31.cloned.1.call-update) | async-done | bytes 262160 | tf_op jit(solution)/shard_map/reduce_scatter | solution.py:307
  2621.2 62.5 %reduce-scatter.29.cloned.1.call-done = bf16[256,3,512]{2,0,1:T(8,128)(2,1)} async-done(((bf16[2048,3,512]{2,0,1:T(8,128)(2,1)}), bf16[256,3,512]{2,0,1:T(8,128)(2,1)}) %reduce-scatter.29.cloned.1.call-update) | async-done | bytes 786448 | tf_op jit(solution)/shard_map/reduce_scatter | solution.py:304
  2688.1 142.4 %reduce-scatter.27.cloned.1.call-done = bf16[2,256,2048]{2,1,0:T(8,128)(2,1)} async-done(((bf16[8,256,2048]{2,1,0:T(8,128)(2,1)}), bf16[2,256,2048]{2,1,0:T(8,128)(2,1)}) %reduce-scatter.27.cloned.1.call-update) | async-done | bytes 2097168 | tf_op jit(solution)/shard_map/reduce_scatter | solution.py:74
  2835.0 143.2 %reduce-scatter.19.cloned.1.call-done = bf16[2,256,2048]{2,1,0:T(8,128)(2,1)} async-done(((bf16[8,256,2048]{2,1,0:T(8,128)(2,1)}), bf16[2,256,2048]{2,1,0:T(8,128)(2,1)}) %reduce-scatter.19.cloned.1.call-update) | async-done | bytes 2097168 | tf_op jit(solution)/shard_map/reduce_scatter | solution.py:74
  2986.2 30.3 reduce-scatter.37.cloned.1.call-done
  3017.4 11.7 psum.71
  (418 shorter events, 523.2 us)
Async XLA Ops:
  7.2 51.0 %all-gather.14.cloned.1.call-start = ((), (), s32[]{:S(2)}) async-start(), calls=%async_computation.13 | async-start | bytes 7077888 | tf_op jit(solution)/shard_map/all_gather | solution.py:132
  7.9 202.1 %all-gather.12.cloned.1.call-start = ((), (), s32[]{:S(2)}) async-start(), calls=%async_computation.12 | async-start | bytes 10485760 | tf_op jit(solution)/shard_map/all_gather | solution.py:70
  24.2 318.1 %all-gather.16.cloned.1.call-start = ((), (), s32[]{:S(2)}) async-start(), calls=%async_computation.14 | async-start | bytes 18874368 | tf_op jit(solution)/shard_map/all_gather | solution.py:176
  24.6 220.5 %copy-start.22 = (f32[256,32]{0,1:T(8,128)}, f32[256,32]{0,1:T(8,128)S(1)}, u32[]{:S(2)}) copy-start(f32[256,32]{0,1:T(8,128)S(1)} %get-tuple-element.325) | copy-start | bytes 98308
  24.6 220.5 %copy-start.24 = (f32[256,32]{0,1:T(8,128)}, f32[256,32]{0,1:T(8,128)S(1)}, u32[]{:S(2)}) copy-start(f32[256,32]{0,1:T(8,128)S(1)} %get-tuple-element.326) | copy-start | bytes 98308
  24.7 220.4 %copy-start.26 = (f32[256,32]{0,1:T(8,128)}, f32[256,32]{0,1:T(8,128)S(1)}, u32[]{:S(2)}) copy-start(f32[256,32]{0,1:T(8,128)S(1)} %get-tuple-element.333) | copy-start | bytes 98308
  24.8 220.4 %copy-start.28 = (f32[256,32]{0,1:T(8,128)}, f32[256,32]{0,1:T(8,128)S(1)}, u32[]{:S(2)}) copy-start(f32[256,32]{0,1:T(8,128)S(1)} %get-tuple-element.334) | copy-start | bytes 98308
  250.8 183.7 %all-gather.30.cloned.1.call-start = ((), (), s32[]{:S(2)}) async-start(), calls=%async_computation.31 | async-start | bytes 18874368 | tf_op jit(solution)/shard_map/all_gather | solution.py:177
  254.7 427.0 %all-gather.18.cloned.1.call-start = ((), (), s32[]{:S(2)}) async-start(), calls=%async_computation.15 | async-start | bytes 2359296 | tf_op jit(solution)/shard_map/all_gather | solution.py:133
  255.3 579.2 %reduce-scatter.17.cloned.1.call-start = ((), (), s32[]{:S(2)}) async-start(), calls=%async_computation.16 | async-start | bytes 10485760 | tf_op jit(solution)/shard_map/reduce_scatter | solution.py:74
  692.4 142.0 %copy-start.1 = (bf16[2,256,2048]{2,1,0:T(8,128)(2,1)S(1)}, bf16[2,256,2048]{2,1,0:T(8,128)(2,1)}, u32[]{:S(2)}) copy-start(bf16[2,256,2048]{2,1,0:T(8,128)(2,1)} %param.20) | copy-start | bytes 6291460
  692.5 145.8 %copy-start.30 = (f32[1,2048]{1,0:T(1,128)S(1)}, f32[1,2048]{1,0:T(1,128)}, u32[]{:S(2)}) copy-start(f32[1,2048]{1,0:T(1,128)} %get-tuple-element.314) | copy-start | bytes 24580
  692.5 199.0 %all-gather.22.cloned.1.call-start = ((), (), s32[]{:S(2)}) async-start(), calls=%async_computation.18 | async-start | bytes 9437184 | tf_op jit(solution)/shard_map/all_gather | solution.py:134
  693.2 350.1 %all-gather.20.cloned.1.call-start = ((), (), s32[]{:S(2)}) async-start(), calls=%async_computation.17 | async-start | bytes 10485760 | tf_op jit(solution)/shard_map/all_gather | solution.py:70
  840.5 352.7 %all-gather.26.cloned.1.call-start = ((), (), s32[]{:S(2)}) async-start(), calls=%async_computation.21 | async-start | bytes 10485760 | tf_op jit(solution)/shard_map/all_gather | solution.py:70
  841.3 408.0 %all-gather.24.cloned.1.call-start = ((), (), s32[]{:S(2)}) async-start(), calls=%async_computation.19 | async-start | bytes 9437184 | tf_op jit(solution)/shard_map/all_gather | solution.py:135
  841.9 644.7 %reduce-scatter.21.cloned.1.call-start = ((), (), s32[]{:S(2)}) async-start(), calls=%async_computation.22 | async-start | bytes 10485760 | tf_op jit(solution)/shard_map/reduce_scatter | solution.py:74
  851.0 445.5 %copy-start.42 = (f32[1,2048]{1,0:T(1,128)}, f32[1,2048]{1,0:T(1,128)S(1)}, u32[]{:S(2)}) copy-start(f32[1,2048]{1,0:T(1,128)S(1)} %convert_element_type.241) | copy-start | bytes 24580
  1072.3 43.2 %copy-start.4 = (f32[8,256,2048]{2,1,0:T(8,128)}, f32[8,256,2048]{2,1,0:T(8,128)S(1)}, u32[]{:S(2)}) copy-start(f32[8,256,2048]{2,1,0:T(8,128)S(1)} %get-tuple-element.335) | copy-start | bytes 50331652
  1134.0 162.5 %copy-start.44 = (f32[8,256]{1,0:T(8,128)}, f32[8,256]{1,0:T(8,128)S(1)}, u32[]{:S(2)}) copy-start(f32[8,256]{1,0:T(8,128)S(1)} %get-tuple-element.317) | copy-start | bytes 24580
  1134.0 162.5 %copy-start.46 = (f32[8,256]{1,0:T(8,128)}, f32[8,256]{1,0:T(8,128)S(1)}, u32[]{:S(2)}) copy-start(f32[8,256]{1,0:T(8,128)S(1)} %get-tuple-element.318) | copy-start | bytes 24580
  1344.7 141.9 %copy-start.2 = (bf16[2,256,2048]{2,1,0:T(8,128)(2,1)S(1)}, bf16[2,256,2048]{2,1,0:T(8,128)(2,1)}, u32[]{:S(2)}) copy-start(bf16[2,256,2048]{2,1,0:T(8,128)(2,1)} %param.20) | copy-start | bytes 6291460
  1344.7 141.9 %copy-start.31 = (f32[1,2048]{1,0:T(1,128)S(1)}, f32[1,2048]{1,0:T(1,128)}, u32[]{:S(2)}) copy-start(f32[1,2048]{1,0:T(1,128)} %get-tuple-element.314) | copy-start | bytes 24580
  1344.7 141.9 %copy-start.36 = (f32[2,256]{1,0:T(2,128)S(1)}, f32[2,256]{1,0:T(2,128)}, u32[]{:S(2)}) copy-start(f32[2,256]{1,0:T(2,128)} %copy-done.35) | copy-start | bytes 6148
  1344.7 141.9 %copy-start.65 = (f32[2,256]{1,0:T(2,128)S(1)}, f32[2,256]{1,0:T(2,128)}, u32[]{:S(2)}) copy-start(f32[2,256]{1,0:T(2,128)} %copy-done.64) | copy-start | bytes 6148
  1344.7 146.5 %copy-start.41 = (f32[2,256]{1,0:T(2,128)S(1)}, f32[2,256]{1,0:T(2,128)}, u32[]{:S(2)}) copy-start(f32[2,256]{1,0:T(2,128)} %copy-done.40) | copy-start | bytes 6148
  1344.7 146.4 %copy-start.59 = (f32[2,256]{1,0:T(2,128)S(1)}, f32[2,256]{1,0:T(2,128)}, u32[]{:S(2)}) copy-start(f32[2,256]{1,0:T(2,128)} %copy-done.58) | copy-start | bytes 6148
  1344.7 300.6 %all-gather.28.cloned.1.call-start = ((), (), s32[]{:S(2)}) async-start(), calls=%async_computation.23 | async-start | bytes 10485760 | tf_op jit(solution)/shard_map/all_gather | solution.py:70
  1491.8 153.5 %copy-start.51 = (f32[8,256]{1,0:T(8,128)S(1)}, f32[8,256]{1,0:T(8,128)}, u32[]{:S(2)}) copy-start(f32[8,256]{1,0:T(8,128)} %copy-done.50) | copy-start | bytes 24580
  1491.8 153.5 %copy-start.54 = (f32[8,256]{1,0:T(8,128)S(1)}, f32[8,256]{1,0:T(8,128)}, u32[]{:S(2)}) copy-start(f32[8,256]{1,0:T(8,128)} %copy-done.53) | copy-start | bytes 24580
  1491.8 153.5 %copy-start.72 = (f32[1,512]{1,0:T(1,128)S(1)}, f32[1,512]{1,0:T(1,128)}, u32[]{:S(2)}) copy-start(f32[1,512]{1,0:T(1,128)} %dynamic-slice_convert_fusion) | copy-start | bytes 6148
  1494.8 771.7 %reduce-scatter.23.cloned.1.call-start = ((), (), s32[]{:S(2)}) async-start(), calls=%async_computation.24 | async-start | bytes 18874368 | tf_op jit(solution)/shard_map/reduce_scatter | solution.py:273
  2002.2 22.3 slice-start
  2002.2 22.3 slice-start.1
  2002.2 22.3 slice-start.2
  2118.9 22.3 slice-start.2
  2152.0 233.9 %reduce-scatter.25.cloned.1.call-start = ((), (), s32[]{:S(2)}) async-start(), calls=%async_computation.25 | async-start | bytes 18874368 | tf_op jit(solution)/shard_map/reduce_scatter | solution.py:276
  2175.3 280.9 %reduce-scatter.39.cloned.1.call-start = ((), (), s32[]{:S(2)}) async-start(), calls=%async_computation.33 | async-start | bytes 589824
  2177.2 321.4 %reduce-scatter.35.cloned.1.call-start = ((), (), s32[]{:S(2)}) async-start(), calls=%async_computation.30 | async-start | bytes 9437184 | tf_op jit(solution)/shard_map/reduce_scatter | solution.py:313
  2202.6 370.6 %reduce-scatter.33.cloned.1.call-start = ((), (), s32[]{:S(2)}) async-start(), calls=%async_computation.29 | async-start | bytes 9437184 | tf_op jit(solution)/shard_map/reduce_scatter | solution.py:310
  2226.7 391.9 %reduce-scatter.31.cloned.1.call-start = ((), (), s32[]{:S(2)}) async-start(), calls=%async_computation.28 | async-start | bytes 2359296 | tf_op jit(solution)/shard_map/reduce_scatter | solution.py:307
  2238.2 30.6 %copy-start.23 = (f32[256,32]{0,1:T(8,128)S(1)}, f32[256,32]{0,1:T(8,128)}, u32[]{:S(2)}) copy-start(f32[256,32]{0,1:T(8,128)} %copy-done.22) | copy-start | bytes 98308
  2238.2 30.6 %copy-start.25 = (f32[256,32]{0,1:T(8,128)S(1)}, f32[256,32]{0,1:T(8,128)}, u32[]{:S(2)}) copy-start(f32[256,32]{0,1:T(8,128)} %copy-done.24) | copy-start | bytes 98308
  2238.2 30.6 %copy-start.27 = (f32[256,32]{0,1:T(8,128)S(1)}, f32[256,32]{0,1:T(8,128)}, u32[]{:S(2)}) copy-start(f32[256,32]{0,1:T(8,128)} %copy-done.26) | copy-start | bytes 98308
  2238.2 30.6 %copy-start.29 = (f32[256,32]{0,1:T(8,128)S(1)}, f32[256,32]{0,1:T(8,128)}, u32[]{:S(2)}) copy-start(f32[256,32]{0,1:T(8,128)} %copy-done.28) | copy-start | bytes 98308
  2238.2 445.5 %reduce-scatter.29.cloned.1.call-start = ((), (), s32[]{:S(2)}) async-start(), calls=%async_computation.27 | async-start | bytes 7077888 | tf_op jit(solution)/shard_map/reduce_scatter | solution.py:304
  2405.2 425.3 %reduce-scatter.27.cloned.1.call-start = ((), (), s32[]{:S(2)}) async-start(), calls=%async_computation.26 | async-start | bytes 10485760 | tf_op jit(solution)/shard_map/reduce_scatter | solution.py:74
  2425.6 552.6 %reduce-scatter.19.cloned.1.call-start = ((), (), s32[]{:S(2)}) async-start(), calls=%async_computation.20 | async-start | bytes 10485760 | tf_op jit(solution)/shard_map/reduce_scatter | solution.py:74
  2451.1 47.5 %copy-start.16 = (f32[2048,256]{1,0:T(8,128)S(1)}, f32[2048,256]{1,0:T(8,128)}, u32[]{:S(2)}) copy-start(f32[2048,256]{1,0:T(8,128)} %param.33) | copy-start | bytes 6291460
  2451.1 565.4 %reduce-scatter.37.cloned.1.call-start = ((), (), s32[]{:S(2)}) async-start(), calls=%async_computation.32 | async-start | bytes 589824
  2502.8 75.6 %copy-start.70 = (bf16[2048]{0:T(1024)(128)(2,1)S(1)}, bf16[2048]{0:T(1024)(128)(2,1)}, u32[]{:S(2)}) copy-start(bf16[2048]{0:T(1024)(128)(2,1)} %get-tuple-element.215) | copy-start | bytes 12292
  2502.8 75.6 %copy-start.76 = (f32[512]{0:T(512)S(1)}, f32[512]{0:T(512)}, u32[]{:S(2)}) copy-start(f32[512]{0:T(512)} %get-tuple-element.213) | copy-start | bytes 6148
  2502.8 115.8 %copy-start.19 = (f32[512,256]{1,0:T(8,128)S(1)}, f32[512,256]{1,0:T(8,128)}, u32[]{:S(2)}) copy-start(f32[512,256]{1,0:T(8,128)} %param.31) | copy-start | bytes 1572868
  2578.3 252.2 %copy-start.3 = (bf16[2,256,2048]{2,1,0:T(8,128)(2,1)S(1)}, bf16[2,256,2048]{2,1,0:T(8,128)(2,1)}, u32[]{:S(2)}) copy-start(bf16[2,256,2048]{2,1,0:T(8,128)(2,1)} %param.20) | copy-start | bytes 6291460
  2578.3 252.2 %copy-start.34 = (f32[1,2048]{1,0:T(1,128)S(1)}, f32[1,2048]{1,0:T(1,128)}, u32[]{:S(2)}) copy-start(f32[1,2048]{1,0:T(1,128)} %copy-done.33) | copy-start | bytes 24580
  2578.3 252.2 %copy-start.39 = (f32[2,256]{1,0:T(2,128)S(1)}, f32[2,256]{1,0:T(2,128)}, u32[]{:S(2)}) copy-start(f32[2,256]{1,0:T(2,128)} %copy-done.38) | copy-start | bytes 6148
  2578.3 252.2 %copy-start.57 = (f32[2,256]{1,0:T(2,128)S(1)}, f32[2,256]{1,0:T(2,128)}, u32[]{:S(2)}) copy-start(f32[2,256]{1,0:T(2,128)} %copy-done.56) | copy-start | bytes 6148
  2621.2 213.8 %copy-start.49 = (f32[2,256]{1,0:T(2,128)S(1)}, f32[2,256]{1,0:T(2,128)}, u32[]{:S(2)}) copy-start(f32[2,256]{1,0:T(2,128)} %copy-done.48) | copy-start | bytes 6148
  2621.2 213.8 %copy-start.68 = (f32[2,256]{1,0:T(2,128)S(1)}, f32[2,256]{1,0:T(2,128)}, u32[]{:S(2)}) copy-start(f32[2,256]{1,0:T(2,128)} %copy-done.67) | copy-start | bytes 6148
  2621.2 357.1 %copy-start.32 = (f32[1,2048]{1,0:T(1,128)S(1)}, f32[1,2048]{1,0:T(1,128)}, u32[]{:S(2)}) copy-start(f32[1,2048]{1,0:T(1,128)} %get-tuple-element.314) | copy-start | bytes 24580
  2621.2 357.1 %copy-start.37 = (f32[2,256]{1,0:T(2,128)S(1)}, f32[2,256]{1,0:T(2,128)}, u32[]{:S(2)}) copy-start(f32[2,256]{1,0:T(2,128)} %copy-done.35) | copy-start | bytes 6148
  2621.2 357.1 %copy-start.61 = (f32[2,256]{1,0:T(2,128)S(1)}, f32[2,256]{1,0:T(2,128)}, u32[]{:S(2)}) copy-start(f32[2,256]{1,0:T(2,128)} %copy-done.60) | copy-start | bytes 6148
  2621.2 357.1 %copy-start.63 = (f32[2,256]{1,0:T(2,128)S(1)}, f32[2,256]{1,0:T(2,128)}, u32[]{:S(2)}) copy-start(f32[2,256]{1,0:T(2,128)} %copy-done.62) | copy-start | bytes 6148
  2978.2 50.9 %copy-start.75 = (f32[3,256]{1,0:T(4,128)S(1)}, f32[3,256]{1,0:T(4,128)}, u32[]{:S(2)}) copy-start(f32[3,256]{1,0:T(4,128)} %param.34) | copy-start | bytes 9220
  (69 other events, 661.7 us)
Sparse Core Ops, SparseCore 0:
  9.9 48.2 all-gather.13
  60.3 149.6 all-gather.11
  251.0 91.3 all-gather.15
  344.7 89.8 all-gather.29
  436.3 28.1 all-gather.17
  692.6 141.8 reduce-scatter.16
  836.3 55.1 all-gather.21
  893.6 149.6 all-gather.19
  1044.9 148.3 all-gather.25
  1195.0 54.1 all-gather.23
  1344.8 141.6 reduce-scatter.20
  1494.9 150.3 all-gather.27
  2152.1 114.3 reduce-scatter.22
  2269.9 115.9 reduce-scatter.24
  2389.4 34.1 reduce-scatter.38
  2427.2 71.2 reduce-scatter.34
  2501.9 71.2 reduce-scatter.32
  2577.3 41.2 reduce-scatter.30
  2621.9 61.7 reduce-scatter.28
  2686.0 144.4 reduce-scatter.26
  2833.0 145.2 reduce-scatter.18
  2981.6 34.8 reduce-scatter.36
where the time goes:
time: 3050 us; the launch traced here: 3040 us
  waiting for transfers between devices  1760 us (58%)
  matrix products  707 us (23%)
  other arithmetic  313 us (10%)
  local copies, waits for them, and re-layouts  134 us (4%)
  blocking collectives  104 us (3%)
    reduce_scatter x4, waiting for transfers between devices, spread_sum(): lax.psum_scatter(features.astype(jnp.bfloat16), 'tensor', scatter_dimensi...  569 us
    all_gather x4, waiting for transfers between devices, share_rows(): return lax.all_gather(features, 'tensor', axis=0, tiled=True)  513 us
    dot_general x8, matrix products, probabilities(): jnp.einsum('sid,sjd->sij', head_query, head_key, preferred_element_type=j...  122 us
    convert_element_type x8, other arithmetic, back_head(): score_grad = (chances * (product - spread)).astype(jnp.bfloat16)  120 us
    reduce_scatter x1, waiting for transfers between devices, on_device(): lax.psum_scatter(from_heads(value_parts).astype(jnp.bfloat16), 'seq', sca...  108 us
    all_gather x1, waiting for transfers between devices, on_device(): lax.all_gather(key_rows, 'seq', axis=1, tiled=True)  85.4 us
    dot_general x8, matrix products, back_head(): jnp.einsum('sid,sjd->sij', head_grad, head_value, preferred_element_type=...  77.8 us
    all_gather x1, waiting for transfers between devices, on_device(): lax.all_gather(values, 'seq', axis=1, tiled=True)  77.7 us
  transfers between devices with their start and end apart: 22, of which 20 were waited for; matrix products, arithmetic and copies ran while one was open for 17% of the time, Pallas kernels for 0%

commit v1 on v0

v1 whole, which is shorter than its diff:
```python
from functools import partial

import jax
import jax.numpy as jnp
import numpy as np
from jax import lax
from jax.experimental import pallas as pl
from jax.experimental.pallas import tpu as pltpu
from jax.sharding import PartitionSpec as P

HEAD_DIM = 64
HALF = HEAD_DIM // 2
SEQ_LEN = 2048
SCALE_BASE = 512
EPSILON = 1e-05
MASKED_SCORE = -1e30
FACTOR = HEAD_DIM ** (-0.5)
BF = jnp.bfloat16
F32 = jnp.float32
VMEM_LIMIT = 56 * 1024 * 1024


def swap(block, bit):
    size = lax.axis_size("seq")
    return lax.ppermute(block, "seq", [(i, i ^ bit) for i in range(size)])


def gather_rows(rows):
    size = lax.axis_size("seq")
    if size == 8:
        half = rows.shape[0] // 2
        across = swap(rows, 2)
        along = swap(rows, 4)
        corner_low = swap(across[:half], 4)
        corner_high = swap(along[half:], 2)
        even = jnp.concatenate([rows, across, along, corner_low, corner_high])
    else:
        even, bit = rows, 2
        while bit < size:
            even = jnp.concatenate([even, swap(even, bit)])
            bit *= 2
    return even, swap(even, 1)


def scatter_rows(even, odd, count):
    size = lax.axis_size("seq")
    total = even.astype(F32) + swap(odd, 1).astype(F32)
    if size == 8:
        half = count // 2
        own, across, along, corner = (total[i * count : (i + 1) * count] for i in range(4))
        low = swap(corner[:half].astype(BF), 4).astype(F32)
        high = swap(corner[half:].astype(BF), 2).astype(F32)
        across = jnp.concatenate([across[:half] + low, across[half:]]).astype(BF)
        along = jnp.concatenate([along[:half], along[half:] + high]).astype(BF)
        return own + swap(across, 2).astype(F32) + swap(along, 4).astype(F32)
    bit = size // 2
    while bit > 1:
        middle = total.shape[0] // 2
        total = total[:middle] + swap(total[middle:].astype(BF), bit).astype(F32)
        bit //= 2
    return total


def sum_blocks(stats):
    size = stats.shape[0]
    bit = 1
    while bit < size:
        shift = (bit & 1) * (size // 2) + (bit >> 1)
        other = swap(stats, bit)
        stats = stats + jnp.stack([other[i ^ shift] for i in range(size)])
        bit *= 2
    return stats


def row_norm(features):
    mean = jnp.mean(features, axis=-1, keepdims=True)
    second = jnp.mean(features * features, axis=-1, keepdims=True)
    inverse = lax.rsqrt(second - mean * mean + EPSILON)
    return (features - mean) * inverse, inverse


def row_norm_back(scaled, normed, inverse):
    return inverse * (
        scaled
        - jnp.mean(scaled, axis=-1, keepdims=True)
        - normed * jnp.mean(scaled * normed, axis=-1, keepdims=True)
    )


def dot(a, b, dims):
    return lax.dot_general(a, b, (dims, ((), ())), preferred_element_type=F32)


NN = ((1,), (0,))
NT = ((1,), (1,))
TN = ((0,), (0,))


def qkv_kernel(place, x_ref, w_ref, cq_ref, sq_ref, ck_ref, sk_ref, q_ref, k_ref, v_ref):
    cols = q_ref.shape[1]
    half = cols // 2
    full = dot(x_ref[...], w_ref[...], NT)
    q1, q2 = full[:, :half], full[:, half:cols]
    k1, k2 = full[:, cols : cols + half], full[:, cols + half : 2 * cols]
    cq, sq, ck, sk = cq_ref[...], sq_ref[...], ck_ref[...], sk_ref[...]
    q_ref[:, :half] = (q1 * cq - q2 * sq).astype(BF)
    q_ref[:, half:] = (q2 * cq + q1 * sq).astype(BF)
    k_ref[:, :half] = (k1 * ck - k2 * sk).astype(BF)
    k_ref[:, half:] = (k2 * ck + k1 * sk).astype(BF)
    v_ref[...] = full[:, 2 * cols :].astype(BF)


def project(place, rows, weights, tables, count):
    length, width = rows.shape
    size = length // count
    cols = weights.shape[0] // 3
    table = pl.BlockSpec((count, cols // 2), lambda i, place: (place[i], 0))
    out = pl.BlockSpec((count, cols), lambda i, place: (place[i], 0))
    return pl.pallas_call(
        qkv_kernel,
        grid_spec=pltpu.PrefetchScalarGridSpec(
            num_scalar_prefetch=1,
            grid=(size,),
            in_specs=[
                pl.BlockSpec((count, width), lambda i, place: (i, 0)),
                pl.BlockSpec((3 * cols, width), lambda i, place: (0, 0)),
                table,
                table,
                table,
                table,
            ],
            out_specs=[out, out, out],
        ),
        out_shape=[jax.ShapeDtypeStruct((length, cols), BF)] * 3,
        compiler_params=pltpu.CompilerParams(vmem_limit_bytes=VMEM_LIMIT),
        cost_estimate=pl.CostEstimate(
            flops=2 * length * width * 3 * cols,
            bytes_accessed=2 * (length * width + 3 * cols * width + 3 * length * cols),
            transcendentals=0,
        ),
        name="project",
    )(place, rows, weights, *tables)


def head_mask(shape, head, heads, turned):
    lane = lax.broadcasted_iota(jnp.int32, shape, 1)
    if turned:
        return (lane // HALF) % heads == head
    return lane // HEAD_DIM == head


def attend_kernel(first, q_ref, k_ref, v_ref, start_ref, o_ref, lse_ref, scores, vcat):
    i = pl.program_id(0)
    rows, cols = q_ref.shape
    heads = cols // HEAD_DIM
    blocks = k_ref.shape[0] // rows

    @pl.when(i == 0)
    def _():
        for b in range(blocks):
            value = v_ref[b * rows : (b + 1) * rows, :]
            for h in range(heads):
                vcat[b, h * rows : (h + 1) * rows, :] = jnp.where(
                    head_mask((rows, cols), h, heads, False), value, jnp.zeros_like(value)
                )

    query = q_ref[...]
    parts = [
        jnp.where(head_mask((rows, cols), h, heads, True), query, jnp.zeros_like(query))
        for h in range(heads)
    ]
    start = start_ref[...]
    low = first[i]
    place = i * rows + lax.broadcasted_iota(jnp.int32, (rows, rows), 0)
    lane = lax.broadcasted_iota(jnp.int32, (rows, rows), 1)

    def score_block(j, tops):
        column = j * rows + lane
        keep = (column <= place) & (column >= start)
        key = k_ref[pl.ds(pl.multiple_of(j * rows, rows), rows), :]
        new = []
        for h in range(heads):
            score = jnp.where(keep, dot(parts[h], key, NT), MASKED_SCORE)
            scores[j, h] = score
            new.append(jnp.maximum(tops[h], jnp.max(score, axis=1, keepdims=True)))
        return tuple(new)

    tops = lax.fori_loop(
        low, i + 1, score_block, tuple(jnp.full((rows, 1), MASKED_SCORE, F32) for _ in range(heads))
    )

    def value_block(j, carry):
        sums, total = carry
        chances, new = [], []
        for h in range(heads):
            chance = jnp.exp(scores[j, h] - tops[h])
            new.append(sums[h] + jnp.sum(chance, axis=1, keepdims=True))
            chances.append(chance.astype(BF))
        total = total + dot(jnp.concatenate(chances, axis=1), vcat[j], NN)
        return tuple(new), total

    sums, total = lax.fori_loop(
        low,
        i + 1,
        value_block,
        (tuple(jnp.zeros((rows, 1), F32) for _ in range(heads)), jnp.zeros((rows, cols), F32)),
    )
    scale = jnp.zeros((rows, cols), F32)
    for h in range(heads):
        scale = jnp.where(head_mask((rows, cols), h, heads, False), 1.0 / sums[h], scale)
        lse_ref[:, h : h + 1] = tops[h] + jnp.log(sums[h])
    o_ref[...] = total * scale


def attend(first, query, key, value, start_column, count):
    length, cols = query.shape
    heads = cols // HEAD_DIM
    size = length // count
    whole = pl.BlockSpec((length, cols), lambda i, first: (0, 0))
    return pl.pallas_call(
        attend_kernel,
        grid_spec=pltpu.PrefetchScalarGridSpec(
            num_scalar_prefetch=1,
            grid=(size,),
            in_specs=[
                pl.BlockSpec((count, cols), lambda i, first: (i, 0)),
                whole,
                whole,
                pl.BlockSpec((count, 1), lambda i, first: (i, 0)),
            ],
            out_specs=[
                pl.BlockSpec((count, cols), lambda i, first: (i, 0)),
                pl.BlockSpec((count, heads), lambda i, first: (i, 0)),
            ],
            scratch_shapes=[
                pltpu.VMEM((size, heads, count, count), F32),
                pltpu.VMEM((size, heads * count, cols), BF),
            ],
        ),
        out_shape=[
            jax.ShapeDtypeStruct((length, cols), F32),
            jax.ShapeDtypeStruct((length, heads), F32),
        ],
        compiler_params=pltpu.CompilerParams(vmem_limit_bytes=VMEM_LIMIT),
        cost_estimate=pl.CostEstimate(
            flops=4 * length * length * cols,
            bytes_accessed=10 * length * cols,
            transcendentals=heads * length * length // 4,
        ),
        name="attend",
    )(first, query, key, value, start_column)


def attend_back_kernel(
    first, spot, q_ref, k_ref, v_ref, do_ref, lse_ref, delta_ref, start_ref,
    cq_ref, sq_ref, ck_ref, sk_ref, out_ref, kcat, dk_ref, dv_ref,
):
    i = pl.program_id(0)
    rows, cols = q_ref.shape
    half = cols // 2
    heads = cols // HEAD_DIM
    blocks = k_ref.shape[0] // rows

    @pl.when(i == 0)
    def _():
        dk_ref[...] = jnp.zeros_like(dk_ref)
        dv_ref[...] = jnp.zeros_like(dv_ref)
        for b in range(blocks):
            key = k_ref[b * rows : (b + 1) * rows, :]
            for h in range(heads):
                kcat[b, h * rows : (h + 1) * rows, :] = jnp.where(
                    head_mask((rows, cols), h, heads, True), key, jnp.zeros_like(key)
                )

    query, grad = q_ref[...], do_ref[...]
    parts = [
        jnp.where(head_mask((rows, cols), h, heads, True), query, jnp.zeros_like(query))
        for h in range(heads)
    ]
    grads = [
        jnp.where(head_mask((rows, cols), h, heads, False), grad, jnp.zeros_like(grad))
        for h in range(heads)
    ]
    query_stack = jnp.concatenate(parts, axis=0)
    grad_stack = jnp.concatenate(grads, axis=0)
    start = start_ref[...]
    place = i * rows + lax.broadcasted_iota(jnp.int32, (rows, rows), 1)
    line = lax.broadcasted_iota(jnp.int32, (rows, rows), 0)

    def block(j, total):
        where = pl.ds(pl.multiple_of(j * rows, rows), rows)
        column = j * rows + line
        keep = (column <= place) & (column >= start)
        key, value = k_ref[where, :], v_ref[where, :]
        chances, slopes = [], []
        for h in range(heads):
            score = jnp.where(keep, dot(key, parts[h], NT), MASKED_SCORE)
            chance = jnp.exp(score - lse_ref[h : h + 1, :])
            product = dot(value, grads[h], NT)
            slopes.append((chance * (product - delta_ref[h : h + 1, :])).astype(BF))
            chances.append(chance.astype(BF))
        slope = jnp.concatenate(slopes, axis=1)
        dk_ref[where, :] += dot(slope, query_stack, NN)
        dv_ref[where, :] += dot(jnp.concatenate(chances, axis=1), grad_stack, NN)
        return total + dot(jnp.concatenate(slopes, axis=0), kcat[j], TN)

    total = lax.fori_loop(first[i], i + 1, block, jnp.zeros((rows, cols), F32))
    here = pl.ds(pl.multiple_of(i * rows, rows), rows)
    target = pl.ds(pl.multiple_of(spot[i] * rows, rows), rows)
    cq, sq = cq_ref[here, :], sq_ref[here, :]
    d1, d2 = total[:, :half], total[:, half:]
    out_ref[0, target, :half] = (d1 * cq + d2 * sq).astype(BF)
    out_ref[0, target, half:] = (d2 * cq - d1 * sq).astype(BF)

    @pl.when(i == pl.num_programs(0) - 1)
    def _():
        def finish(j, carry):
            where = pl.ds(pl.multiple_of(j * rows, rows), rows)
            goal = pl.ds(pl.multiple_of(spot[j] * rows, rows), rows)
            ck, sk = ck_ref[where, :], sk_ref[where, :]
            k1, k2 = dk_ref[where, :half], dk_ref[where, half:]
            out_ref[1, goal, :half] = (k1 * ck + k2 * sk).astype(BF)
            out_ref[1, goal, half:] = (k2 * ck - k1 * sk).astype(BF)
            out_ref[2, goal, :] = dv_ref[where, :].astype(BF)
            return carry

        lax.fori_loop(0, blocks, finish, 0)


def attend_back(first, spot, query, key, value, grad, lse, delta, start_row, tables, count):
    length, cols = query.shape
    heads = cols // HEAD_DIM
    size = length // count
    whole = pl.BlockSpec((length, cols), lambda i, *_: (0, 0))
    table = pl.BlockSpec((length, cols // 2), lambda i, *_: (0, 0))
    rows = pl.BlockSpec((count, cols), lambda i, *_: (i, 0))
    line = pl.BlockSpec((pl.squeezed, heads, count), lambda i, *_: (i, 0, 0))
    return pl.pallas_call(
        attend_back_kernel,
        grid_spec=pltpu.PrefetchScalarGridSpec(
            num_scalar_prefetch=2,
            grid=(size,),
            in_specs=[
                rows,
                whole,
                whole,
                rows,
                line,
                line,
                pl.BlockSpec((pl.squeezed, 1, count), lambda i, *_: (i, 0, 0)),
                table,
                table,
                table,
                table,
            ],
            out_specs=pl.BlockSpec((3, length, cols), lambda i, *_: (0, 0, 0)),
            scratch_shapes=[
                pltpu.VMEM((size, heads * count, cols), BF),
                pltpu.VMEM((length, cols), F32),
                pltpu.VMEM((length, cols), F32),
            ],
        ),
        out_shape=jax.ShapeDtypeStruct((3, length, cols), BF),
        compiler_params=pltpu.CompilerParams(vmem_limit_bytes=VMEM_LIMIT),
        cost_estimate=pl.CostEstimate(
            flops=10 * length * length * cols,
            bytes_accessed=20 * length * cols,
            transcendentals=heads * length * length // 4,
        ),
        name="attend_back",
    )(first, spot, query, key, value, grad, lse, delta, start_row, *tables)


def xpos_tables(heads, scale):
    positions = jnp.arange(SEQ_LEN, dtype=F32)
    pair_index = jnp.arange(HALF, dtype=F32)
    frequency = 10000.0 ** (-pair_index / HALF)
    angles = positions[:, None] * frequency[None, :]
    zeta_base = (pair_index / HALF + 0.4) / 1.4
    growth = zeta_base[None, :] ** ((positions[:, None] - SEQ_LEN // 2) / SCALE_BASE)
    cosine, sine = jnp.cos(angles), jnp.sin(angles)
    tables = (cosine * growth * scale, sine * growth * scale, cosine / growth, sine / growth)
    return tuple(jnp.tile(table, (1, heads)) for table in tables)


def on_device(
    layer_input,
    segment_ids,
    cotangent,
    projections,
    output_weight,
    up_weight,
    down_weight,
    norm_gains,
    hidden_gain,
    decays,
    average_projections,
    average_output,
    average_up,
    average_down,
    average_gains,
    average_hidden,
):
    size = lax.axis_size("seq")
    groups = lax.axis_size("tensor")
    me = lax.axis_index("seq")
    group = lax.axis_index("tensor")
    chunks, count, width = layer_input.shape
    length = segment_ids.shape[1]
    block_cols = projections.shape[2]
    heads = width // HEAD_DIM
    per_block = block_cols // HEAD_DIM
    mine = heads // size
    cols = mine * HEAD_DIM
    even_split = per_block % size == 0
    units = up_weight.shape[1] // size
    hidden_cols = units * groups
    hidden_total = hidden_cols * size

    gains_all = lax.all_gather(norm_gains, "seq", axis=1, tiled=True).astype(F32)
    gain_attn, gain_ffn = gains_all[0], gains_all[2]
    each = per_block // size if even_split else 1

    def to_order(rows):
        if not even_split:
            return rows
        shaped = rows.reshape((groups, size, each * HEAD_DIM) + rows.shape[1:])
        return jnp.swapaxes(shaped, 0, 1).reshape(rows.shape)

    def from_order(rows):
        if not even_split:
            return rows
        shaped = rows.reshape((size, groups, each * HEAD_DIM) + rows.shape[1:])
        return jnp.swapaxes(shaped, 0, 1).reshape(rows.shape)

    gain_inner = to_order(gains_all[1])
    gain_hidden = lax.all_gather(hidden_gain, "tensor", axis=0, tiled=True)
    gain_hidden = gain_hidden.astype(F32).reshape(hidden_cols)

    inputs = [layer_input[c].astype(F32) for c in range(chunks)]
    normed = [row_norm(rows) for rows in inputs]
    normed_in = [
        jnp.concatenate(gather_rows((normed[c][0] * gain_attn).astype(BF))) for c in range(chunks)
    ]

    turned = projections.transpose(1, 2, 0)
    if even_split:
        sent = turned.reshape(3, size, each * HEAD_DIM, count).transpose(1, 0, 2, 3)
        came = lax.all_to_all(sent, "seq", 0, 0, tiled=True)
        proj = lax.all_gather(came, "tensor", axis=0, tiled=False)
        proj = proj.transpose(2, 0, 3, 1, 4).reshape(3, cols, width)
    else:
        wide = lax.all_gather(turned, "tensor", axis=1, tiled=True)
        sent = wide.reshape(3, size, cols, count).transpose(1, 0, 2, 3)
        came = lax.all_to_all(sent, "seq", 0, 0, tiled=True)
        proj = came.transpose(1, 2, 0, 3).reshape(3, cols, width)
    turned_heads = proj[:2].reshape(2, mine, 2, HALF, width).transpose(0, 2, 1, 3, 4)
    proj = jnp.concatenate([turned_heads.reshape(2 * cols, width), proj[2]])

    full_output = lax.all_gather(
        lax.all_gather(output_weight, "tensor", axis=0, tiled=True), "seq", axis=1, tiled=True
    )
    full_output = to_order(full_output)

    sent = up_weight.reshape(count, size, units).transpose(1, 0, 2)
    came = lax.all_to_all(sent, "seq", 0, 0, tiled=True).reshape(width, units)
    up = lax.all_gather(came, "tensor", axis=0, tiled=False)
    up = up.transpose(1, 0, 2).reshape(width, hidden_cols)

    sent = down_weight.reshape(size, units, count)
    came = lax.all_to_all(sent, "seq", 0, 0, tiled=True)
    down = lax.all_gather(came.transpose(1, 0, 2).reshape(units, width), "tensor", axis=0, tiled=True)

    masks = np.concatenate([np.arange(0, size, 2), np.arange(1, size, 2)]).astype(np.int32)
    place = (jnp.asarray(masks) ^ me).astype(jnp.int32)
    blocks = jnp.arange(size, dtype=jnp.int32) ^ me
    spot = (blocks & 1) * (size // 2) + (blocks >> 1)
    tables_turn = xpos_tables(mine, FACTOR)
    segments = lax.dynamic_slice_in_dim(segment_ids, group * chunks, chunks, 0)
    starts = jnp.sum(
        (segments[:, None, :] < segments[:, :, None]).astype(jnp.int32), axis=2
    )
    firsts = starts.reshape(chunks, size, count)[:, :, 0] // count

    kept, residuals, normed_mid, gathered_mid = [], [], [], []
    for c in range(chunks):
        query, key, value = project(place, normed_in[c], proj, tables_turn, count)
        attended, lse = attend(firsts[c], query, key, value, starts[c][:, None], count)
        sent = attended.astype(BF).reshape(size, count, cols)
        came = lax.all_to_all(sent, "seq", 0, 0, tiled=True)
        rows = came.transpose(1, 0, 2).reshape(count, width).astype(F32)
        inner, inner_inverse = row_norm(rows)
        inner_rows = (inner * gain_inner).astype(BF)
        kept.append((query, key, value, attended, lse, inner, inner_inverse, inner_rows))
        residual = inputs[c] + dot(inner_rows, full_output, NN)
        residuals.append(residual)
        normed_mid.append(row_norm(residual))
        gathered_mid.append(
            jnp.concatenate(gather_rows((normed_mid[c][0] * gain_ffn).astype(BF)))
        )

    gathered_cot = [jnp.concatenate(gather_rows(cotangent[c])) for c in range(chunks)]
    middle = length // 2
    outputs, residual_grads, ffn_gain_grads, inner_gain_grads = [], [], [], []
    down_grad, up_grad, output_grad, hidden_gain_grad = 0.0, 0.0, 0.0, 0.0
    input_parts, proj_grad = [], 0.0
    for c in range(chunks):
        hidden = dot(gathered_mid[c], up, NN)
        activated, gelu_pullback = jax.vjp(partial(jax.nn.gelu, approximate=False), hidden)
        squeezed_grad = dot(gathered_cot[c], down, NT)
        scaled = squeezed_grad * gain_hidden
        stats = jnp.stack(
            [
                jnp.sum(activated, axis=1),
                jnp.sum(activated * activated, axis=1),
                jnp.sum(scaled, axis=1),
                jnp.sum(scaled * activated, axis=1),
            ]
        )
        stats = sum_blocks(stats.reshape(4, size, count).transpose(1, 0, 2)) / hidden_total
        stats = stats.transpose(1, 0, 2).reshape(4, length, 1)
        mean, second, scaled_mean, cross = stats
        inverse = lax.rsqrt(second - mean * mean + EPSILON)
        cross = inverse * (cross - mean * scaled_mean)
        hidden_normed = (activated - mean) * inverse
        squeezed = (hidden_normed * gain_hidden).astype(BF)
        hidden_gain_grad = hidden_gain_grad + jnp.sum(squeezed_grad * hidden_normed, axis=0)
        activated_grad = inverse * (scaled - scaled_mean - hidden_normed * cross)
        hidden_grad = gelu_pullback(activated_grad)[0].astype(BF)

        mid_grad = scatter_rows(
            dot(hidden_grad[:middle], up, NT), dot(hidden_grad[middle:], up, NT).astype(BF), count
        )
        outputs.append(
            residuals[c]
            + scatter_rows(
                dot(squeezed[:middle], down, NN), dot(squeezed[middle:], down, NN).astype(BF), count
            )
        )
        down_grad = down_grad + dot(squeezed, gathered_cot[c], TN)
        up_grad = up_grad + dot(gathered_mid[c], hidden_grad, TN)

        normal, inverse = normed_mid[c]
        ffn_gain_grads.append(jnp.sum(mid_grad * normal, axis=0))
        residual_grad = cotangent[c].astype(F32) + row_norm_back(
            mid_grad * gain_ffn, normal, inverse
        )
        residual_grads.append(residual_grad)
        attn_grad = residual_grad.astype(BF)
        query, key, value, attended, lse, inner, inner_inverse, inner_rows = kept[c]
        output_grad = output_grad + dot(inner_rows, attn_grad, TN)
        inner_grad = dot(attn_grad, full_output, NT)
        inner_gain_grads.append(jnp.sum(inner_grad * inner, axis=0))
        attended_grad = row_norm_back(inner_grad * gain_inner, inner, inner_inverse).astype(BF)
        sent = attended_grad.reshape(count, size, cols).transpose(1, 0, 2)
        grad = lax.all_to_all(sent, "seq", 0, 0, tiled=True).reshape(length, cols)
        delta = jnp.sum((grad.astype(F32) * attended).reshape(length, mine, HEAD_DIM), axis=2)
        projected_grad = attend_back(
            firsts[c],
            spot,
            query,
            key,
            value,
            grad,
            lse.reshape(size, count, mine).transpose(0, 2, 1),
            delta.reshape(size, count, mine).transpose(0, 2, 1),
            starts[c].reshape(size, 1, count),
            tables_turn,
            count,
        )
        projected_grad = projected_grad.transpose(1, 0, 2).reshape(length, 3 * cols)
        input_parts.append(
            scatter_rows(
                dot(projected_grad[:middle], proj, NN),
                dot(projected_grad[middle:], proj, NN).astype(BF),
                count,
            )
        )
        proj_grad = proj_grad + dot(projected_grad, normed_in[c], TN)

    input_grads, attn_gain_grads = [], []
    for c in range(chunks):
        normal, inverse = normed[c]
        attn_gain_grads.append(jnp.sum(input_parts[c] * normal, axis=0))
        input_grads.append(
            residual_grads[c] + row_norm_back(input_parts[c] * gain_attn, normal, inverse)
        )
    gain_terms = jnp.stack(
        [sum(attn_gain_grads), from_order(sum(inner_gain_grads)), sum(ffn_gain_grads)]
    )
    gains_grad = lax.psum(
        lax.psum_scatter(gain_terms, "seq", scatter_dimension=1, tiled=True), "tensor"
    )

    scatter = partial(lax.psum_scatter, axis_name="tensor", scatter_dimension=0, tiled=True)
    part = down_grad.astype(BF)
    part = scatter(part).reshape(units, size, count).transpose(1, 0, 2)
    down_final = lax.all_to_all(part, "seq", 0, 0, tiled=True).reshape(size * units, count)
    part = up_grad.astype(BF).reshape(width, groups, units).transpose(1, 0, 2)
    part = scatter(part).reshape(size, count, units)
    part = lax.all_to_all(part, "seq", 0, 0, tiled=True)
    up_final = part.transpose(1, 0, 2).reshape(count, size * units)
    part = from_order(output_grad.astype(BF)).reshape(width, size, count).transpose(1, 0, 2)
    part = lax.psum_scatter(part, "seq", scatter_dimension=0, tiled=True).reshape(width, count)
    output_final = scatter(part)
    part = proj_grad.astype(BF)
    turned_heads = part[: 2 * cols].reshape(2, 2, mine, HALF, width).transpose(0, 2, 1, 3, 4)
    part = jnp.concatenate([turned_heads.reshape(2, cols, width), part[None, 2 * cols :]])
    if even_split:
        part = part.reshape(3, groups, each * HEAD_DIM, width).transpose(1, 0, 2, 3)
        part = scatter(part.reshape(3 * cols, width))
        part = part.reshape(3, each * HEAD_DIM, size, count).transpose(2, 0, 1, 3)
        part = lax.all_to_all(part, "seq", 0, 0, tiled=True)
        proj_final = part.transpose(3, 1, 0, 2).reshape(count, 3, block_cols)
    else:
        part = lax.psum(part, "tensor").reshape(3, cols, size, count).transpose(2, 0, 1, 3)
        part = lax.all_to_all(part, "seq", 0, 0, tiled=True)
        part = part.transpose(3, 1, 0, 2).reshape(count, 3, width)
        proj_final = lax.dynamic_slice_in_dim(part, group * block_cols, block_cols, 2)
    hidden_final = lax.psum_scatter(
        hidden_gain_grad.reshape(groups, units), "tensor", scatter_dimension=0, tiled=True
    )

    grads = (
        proj_final.astype(F32),
        output_final.astype(F32),
        up_final.astype(F32),
        down_final.astype(F32),
        gains_grad.astype(F32),
        hidden_final.astype(F32),
    )
    averages = (
        average_projections,
        average_output,
        average_up,
        average_down,
        average_gains,
        average_hidden,
    )
    updated = tuple(
        decays[i] * averages[i] + (1.0 - decays[i]) * grads[i] for i in range(6)
    )
    return (jnp.stack(outputs).astype(BF), jnp.stack(input_grads)) + grads + updated


def solution(mesh):
    weights = (P("seq", None, "tensor"), P("tensor", "seq"), P("seq", "tensor"), P("tensor", "seq"))
    gains = (P(None, "seq"), P("tensor", "seq"))
    rows = P("tensor", "seq", None)
    return jax.shard_map(
        on_device,
        mesh=mesh,
        in_specs=(rows, P(), rows) + weights + gains + (P(),) + weights + gains,
        out_specs=(rows, rows) + weights + gains + weights + gains,
        check_vma=False,
    )
```

time: 3050 us -> 1350 us (0.44)
  waiting for transfers between devices: 1760 us -> 332 us
  matrix products: 707 us -> 312 us
  other arithmetic: 313 us -> 132 us
  Pallas kernels: 0 us -> 128 us
  local copies, waits for them, and re-layouts: 134 us -> 255 us
  starting transfers between devices: 2 us -> 92.1 us
  blocking collectives: 104 us -> 65.1 us
    reduce_scatter x10 -> x5, waiting for transfers between devices: 918 us -> 7.83 us  [the longest x1 7.77 us: on_device(): output_final = scatter(part)]
    all_gather x10 -> x5, waiting for transfers between devices: 806 us -> 13 us  [the longest x1 13 us: on_device(): lax.all_gather(output_weight, 'tensor', axis=0, tiled=True)]
    dot_general x68 -> x28, matrix products: 707 us -> 312 us  [dot(): return lax.dot_general(a, b, (dims, ((), ())), preferred_element_type=F32)]
    ppermute x0 -> x66, waiting for transfers between devices: none -> 246 us  [swap(): return lax.ppermute(block, 'seq', [(i, i ^ bit) for i in range(size)])]
    convert_element_type x17 -> x9, other arithmetic: 157 us -> 14.6 us  [the longest x2 4.38 us: on_device(): sent = attended.astype(BF).reshape(size, count, cols)]
    pallas_call x0 -> x6, Pallas kernels: none -> 128 us  [the longest x2 54.1 us: attend_back(): pl.pallas_call(attend_back_kernel, grid_spec=pltpu.PrefetchScalarGridSpec...]
    psum x5 -> x1, blocking collectives: 84.3 us -> 12 us  [on_device(): lax.psum(lax.psum_scatter(gain_terms, 'seq', scatter_dimension=1, tiled=T...]
    reduce_sum x14 -> x11, other arithmetic: 111 us -> 51.7 us  [the longest x2 31.5 us: on_device(): jnp.sum(squeezed_grad * hidden_normed, axis=0)]
  transfers between devices with their start and end apart: 22 -> 86, of which waited for: 20 -> 30; matrix products, arithmetic and copies ran while one was open for 17% -> 41% of each run, Pallas kernels for 0% -> 10%
where the time goes in v1:
time: 1350 us; the launch traced here: 1340 us
  waiting for transfers between devices  332 us (25%)
  matrix products  312 us (23%)
  local copies, waits for them, and re-layouts  255 us (19%)
  other arithmetic  132 us (10%)
  Pallas kernels  128 us (9%)
  starting transfers between devices  92.1 us (7%)
  blocking collectives  65.1 us (5%)
  between operations  20.2 us (1%)
    dot_general x28, matrix products, dot(): return lax.dot_general(a, b, (dims, ((), ())), preferred_element_type=F32)  312 us
    ppermute x66, waiting for transfers between devices, swap(): return lax.ppermute(block, 'seq', [(i, i ^ bit) for i in range(size)])  246 us
    unnamed x258, local copies, waits for them, and re-layouts  81 us
    ppermute x66, starting transfers between devices, swap(): return lax.ppermute(block, 'seq', [(i, i ^ bit) for i in range(size)])  55.7 us
    pallas_call x2, Pallas kernels, attend_back(): pl.pallas_call(attend_back_kernel, grid_spec=pltpu.PrefetchScalarGridSpec...  54.1 us
    unnamed x12, waiting for transfers between devices  46.7 us
    pallas_call x2, Pallas kernels, attend(): pl.pallas_call(attend_kernel, grid_spec=pltpu.PrefetchScalarGridSpec(num_...  46.1 us
    reduce_sum x2, other arithmetic, on_device(): jnp.sum(squeezed_grad * hidden_normed, axis=0)  31.5 us
  transfers between devices with their start and end apart: 86, of which 30 were waited for; matrix products, arithmetic and copies ran while one was open for 41% of the time, Pallas kernels for 10%

profile of v1, /device:TPU:0, one launch (start us, length us, event | category | flops | bytes accessed | tf_op | source)
XLA Modules:
  0.0 1336.8 jit_solution(8517848993279626157)
XLA Ops:
  9.5 17.8 %all_to_all.50 = bf16[8,3,64,256]{3,2,1,0:T(8,128)(2,1)} all-to-all(bf16[8,3,64,256]{3,2,1,0:T(8,128)(2,1)S(1)} %copy.341), channel_id=1, replica_groups=mesh['seq'=8,'tensor'=4] {'seq'}, dimensions={0} | all-to-all | bytes 1572864 | tf_op jit(solution)/shard_map/all_to_all | solution.py:449
  27.3 13.0 all-gather.8.cloned.1.call-done
  45.3 18.4 %all_gather.24 = bf16[3,2048]{1,0:T(4,128)(2,1)S(1)} all-gather(bf16[3,256]{1,0:T(4,128)(2,1)S(1)} %copy-done.97), channel_id=1, replica_groups=mesh['seq'=8,'tensor'=4] {'seq'}, dimensions={1}, use_global_device_ids=true | all-gather | bytes 13824 | tf_op jit(solution)/shard_map/all_gather | solution.py:420
  103.7 40.1 %collective-permute-done.25 = bf16[128,2048]{1,0:T(8,128)(2,1)S(1)} collective-permute-done((bf16[128,2048]{1,0:T(8,128)(2,1)S(1)}, bf16[128,2048]{1,0:T(8,128)(2,1)S(1)}, u32[]{:S(2)}, u32[]{:S(2)}) %collective-permute-start.25) | collective-permute-done | bytes 524320 | tf_op jit(solution)/shard_map/ppermute | solution.py:25
  146.4 47.7 %collective-permute-done.26 = bf16[128,2048]{1,0:T(8,128)(2,1)S(1)} collective-permute-done((bf16[128,2048]{1,0:T(8,128)(2,1)S(1)}, bf16[128,2048]{1,0:T(8,128)(2,1)S(1)}, u32[]{:S(2)}, u32[]{:S(2)}) %collective-permute-start.26) | collective-permute-done | bytes 524320 | tf_op jit(solution)/shard_map/ppermute | solution.py:25
  204.6 6.2 collective-permute-done.2
  275.0 13.7 %project.3 = (bf16[2048,256]{1,0:T(8,128)(2,1)}, bf16[2048,256]{1,0:T(8,128)(2,1)}, bf16[2048,256]{1,0:T(8,128)(2,1)}) custom-call(s32[8]{0:T(128)} %broadcast_xor_fusion.place, bf16[2048,2048]{1,0:T(8,128)(2,1)} %constant_dynamic-update-slice_fusion.38.x_ref, bf16[768,2048]{1,0:T(8,128)(2,1)} %pad_maximum_fusion.1.w_ref, f32[2048,128]{1,0:T(8,128)} %copy.345.cq_ref, ...), custom_call_target="tpu_custom_call" | custom-call | flops 6442450944 | bytes 14680064 | tf_op jit(solution)/shard_map/project/pallas_call | solution.py:119
  288.6 23.2 %attend.3 = (f32[2048,256]{1,0:T(8,128)}, f32[2048,4]{1,0:T(8,128)}) custom-call(s32[8]{0:T(128)} %get-tuple-element.362.first, bf16[2048,256]{1,0:T(8,128)(2,1)} %get-tuple-element.28.q_ref, bf16[2048,256]{1,0:T(8,128)(2,1)} %get-tuple-element.29.k_ref, bf16[2048,256]{1,0:T(8,128)(2,1)} %get-tuple-element.30.v_ref, s32[2048,1]{1,0:T(8,128)} %copy.361.start_ref), custom_call_target="tpu_custom_call" | custom-call | flops 4294967296 | bytes 5242880 | tf_op jit(solution)/shard_map/attend/pallas_call | solution.py:220
  323.2 13.7 %project.2 = (bf16[2048,256]{1,0:T(8,128)(2,1)}, bf16[2048,256]{1,0:T(8,128)(2,1)}, bf16[2048,256]{1,0:T(8,128)(2,1)}) custom-call(s32[8]{0:T(128)} %broadcast_xor_fusion.place, bf16[2048,2048]{1,0:T(8,128)(2,1)} %constant_dynamic-update-slice_fusion.5.x_ref, bf16[768,2048]{1,0:T(8,128)(2,1)} %pad_maximum_fusion.1.w_ref, f32[2048,128]{1,0:T(8,128)} %copy.345.cq_ref, ...), custom_call_target="tpu_custom_call" | custom-call | flops 6442450944 | bytes 14680064 | tf_op jit(solution)/shard_map/project/pallas_call | solution.py:119
  336.9 22.8 %attend.2 = (f32[2048,256]{1,0:T(8,128)}, f32[2048,4]{1,0:T(8,128)}) custom-call(s32[8]{0:T(128)} %get-tuple-element.361.first, bf16[2048,256]{1,0:T(8,128)(2,1)} %get-tuple-element.24.q_ref, bf16[2048,256]{1,0:T(8,128)(2,1)} %get-tuple-element.25.k_ref, bf16[2048,256]{1,0:T(8,128)(2,1)} %get-tuple-element.26.v_ref, s32[2048,1]{1,0:T(8,128)} %copy.349.start_ref), custom_call_target="tpu_custom_call" | custom-call | flops 4294967296 | bytes 5242880 | tf_op jit(solution)/shard_map/attend/pallas_call | solution.py:220
  376.4 8.0 all-to-all-done.1
  389.2 8.5 copy.352
  397.8 6.1 fusion.113
  409.8 16.9 %all-gather.1 = bf16[4,1,256]{2,1,0:T(2,128)(2,1)S(1)} all-gather(bf16[1,1,256]{2,1,0:T(2,128)(2,1)S(1)} %bitcast.444), channel_id=1, replica_groups=mesh['seq'=8,'tensor'=4] {'tensor'}, dimensions={0}, use_global_device_ids=true | all-gather | bytes 2560 | tf_op jit(solution)/shard_map/all_gather | solution.py:437
  428.2 6.6 collective-permute-done.28
  438.4 8.5 collective-permute-done.30
  448.3 18.0 %collective-permute-done.31 = bf16[128,2048]{1,0:T(8,128)(2,1)S(1)} collective-permute-done((bf16[128,2048]{1,0:T(8,128)(2,1)S(1)}, bf16[128,2048]{1,0:T(8,128)(2,1)S(1)}, u32[]{:S(2)}, u32[]{:S(2)}) %collective-permute-start.31) | collective-permute-done | bytes 524320 | tf_op jit(solution)/shard_map/ppermute | solution.py:25
  480.1 6.2 copy.355
  492.9 8.9 collective-permute-done.7
  504.1 13.1 fusion.147
  517.2 7.9 constant_dynamic-update-slice_fusion.49
  525.1 13.3 fusion.146
  543.2 11.5 fusion.145
  554.7 57.9 %multiply_reduce_fusion.7 = (f32[2048]{0:T(1024)S(1)}, f32[2048]{0:T(1024)S(1)}, f32[2048]{0:T(1024)S(1)}, f32[2048]{0:T(1024)S(1)}, f32[2048]{0:T(1024)S(1)}, /...) fusion(f32[1024]{0:T(1024)S(1)} %bitcast.428, ...), kind=kOutput, calls=%fused_computation.55 | convolution fusion | flops 8887713792 | bytes 79761408 | tf_op jit(solution)/shard_map/dot_general | solution.py:91
  624.1 17.7 %multiply_reduce_fusion = (f32[1024]{0:T(1024)}, bf16[2048,1024]{0,1:T(8,128)(2,1)}, bf16[2048,1024]{0,1:T(8,128)(2,1)}) fusion(f32[2048,1024]{0,1:T(8,128)} %copy-done.20, f32[2048,1024]{0,1:T(8,128)} %get-tuple-element.176, f32[2048]{0:T(1024)S(1)} %get-tuple-element.337, f32[2048]{0:T(1024)S(1)} %bitcast.419, f32[2048,1024]{0,1:T(8,128)} %get-tuple-element.177, ...), kind=kLoop, calls=%fused_computation.6 | loop fusion | flops 52427776 | bytes 41984000 | tf_op jit(solution)/shard_map/reduce_sum | solution.py:527
  641.8 14.6 %fusion.150 = f32[2048,1024]{0,1:T(8,128)} fusion(bf16[2048,1024]{0,1:T(8,128)(2,1)} %get-tuple-element.187, bf16[2048,2048]{1,0:T(8,128)(2,1)} %constant_dynamic-update-slice_fusion.49), kind=kOutput, calls=%fused_computation.408 | convolution fusion | flops 8589934592 | bytes 20971520 | tf_op jit(solution)/shard_map/dot_general | solution.py:91
  656.4 13.8 %multiply_reduce_fusion.1 = (f32[1024]{0:T(1024)S(1)}, bf16[2048,1024]{0,1:T(8,128)(2,1)}, bf16[2048,1024]{0,1:T(8,128)(2,1)}) fusion(f32[2048,1024]{0,1:T(8,128)} %get-tuple-element.377, f32[2048,1024]{0,1:T(8,128)} %get-tuple-element.174, f32[2048]{0:T(1024)S(1)} %get-tuple-element.335, f32[2048]{0:T(1024)S(1)} %bitcast.423, ...), kind=kLoop, calls=%fused_computation.7 | loop fusion | flops 52427776 | bytes 41984000 | tf_op jit(solution)/shard_map/reduce_sum | solution.py:527
  670.2 15.2 %add_convert_fusion.2 = bf16[2048,1024]{0,1:T(8,128)(2,1)} fusion(f32[2048,1024]{0,1:T(8,128)} %fusion.150, bf16[2048,1024]{0,1:T(8,128)(2,1)} %get-tuple-element.189, bf16[2048,2048]{1,0:T(8,128)(2,1)} %constant_dynamic-update-slice_fusion.16), kind=kOutput, calls=%fused_computation.9 | convolution fusion | flops 8594128896 | bytes 25165824 | tf_op jit(solution)/shard_map/dot_general | solution.py:91
  686.8 9.5 convolution_convert_fusion.4
  696.3 6.4 convolution_convert_fusion.2
  703.2 11.4 fusion.149
  714.6 6.2 convolution_convert_fusion.3
  720.8 6.1 convolution_convert_fusion.5
  727.5 12.9 add_convert_fusion.1
  740.5 12.3 fusion.142
  756.2 8.2 fusion.141
  770.2 10.3 fusion.140
  783.3 8.5 fusion.139
  797.3 9.6 collective-permute-done.21
  826.4 14.3 %collective-permute-done.58 = bf16[256,2048]{1,0:T(8,128)(2,1)S(1)} collective-permute-done((bf16[256,2048]{1,0:T(8,128)(2,1)S(1)}, bf16[256,2048]{1,0:T(8,128)(2,1)S(1)}, u32[]{:S(2)}, u32[]{:S(2)}) %collective-permute-start.58) | collective-permute-done | bytes 1048608 | tf_op jit(solution)/shard_map/ppermute | solution.py:25
  868.0 17.8 %collective-permute-done.48 = bf16[256,2048]{1,0:T(8,128)(2,1)} collective-permute-done((bf16[256,2048]{1,0:T(8,128)(2,1)}, bf16[256,2048]{1,0:T(8,128)(2,1)}, u32[]{:S(2)}, u32[]{:S(2)}) %collective-permute-start.48) | collective-permute-done | bytes 1048608 | tf_op jit(solution)/shard_map/ppermute | solution.py:25
  885.8 6.4 multiply_reduce_fusion.9
  892.2 14.3 %collective-permute-done.43 = bf16[256,2048]{1,0:T(8,128)(2,1)S(1)} collective-permute-done((bf16[256,2048]{1,0:T(8,128)(2,1)S(1)}, bf16[256,2048]{1,0:T(8,128)(2,1)S(1)}, u32[]{:S(2)}, u32[]{:S(2)}) %collective-permute-start.43) | collective-permute-done | bytes 1048608 | tf_op jit(solution)/shard_map/ppermute | solution.py:25
  911.1 8.4 fusion.74
  919.5 11.8 add_convert_fusion
  931.3 8.4 copy.393
  939.8 10.4 copy.427
  950.1 8.5 copy.394
  958.7 8.0 multiply_reduce_fusion.10
  966.8 8.2 multiply_reduce_fusion.11
  986.3 11.1 all-to-all-done.6
  1006.5 27.2 %attend_back.3 = bf16[3,2048,256]{2,1,0:T(8,128)(2,1)} custom-call(s32[8]{0:T(128)} %get-tuple-element.362.first, s32[8]{0:T(128)} %shift-right-arithmetic_add_fusion.spot, bf16[2048,256]{1,0:T(8,128)(2,1)} %get-tuple-element.28.q_ref, bf16[2048,256]{1,0:T(8,128)(2,1)} %get-tuple-element.29.k_ref, bf16[2048,256]{1,0:T(8,128)(2,1)} %get-tuple-element.30.v_ref, ...), custom_call_target="tpu_custom_call" | custom-call | flops 10737418240 | bytes 10485760 | tf_op jit(solution)/shard_map/attend_back/pallas_call | solution.py:338
  1043.1 8.0 convolution_convert_fusion
  1056.9 26.9 %attend_back.2 = bf16[3,2048,256]{2,1,0:T(8,128)(2,1)} custom-call(s32[8]{0:T(128)} %get-tuple-element.361.first, s32[8]{0:T(128)} %shift-right-arithmetic_add_fusion.spot, bf16[2048,256]{1,0:T(8,128)(2,1)} %get-tuple-element.24.q_ref, bf16[2048,256]{1,0:T(8,128)(2,1)} %get-tuple-element.25.k_ref, bf16[2048,256]{1,0:T(8,128)(2,1)} %get-tuple-element.26.v_ref, ...), custom_call_target="tpu_custom_call" | custom-call | flops 10737418240 | bytes 10485760 | tf_op jit(solution)/shard_map/attend_back/pallas_call | solution.py:338
  1090.3 6.6 convolution_convert_fusion.1
  1097.1 11.1 fusion.148
  1117.9 11.8 add_convert_fusion.5
  1148.7 6.6 fusion.144
  1201.1 6.1 collective-permute-done.63
  1207.2 21.4 %collective-permute-done.53 = bf16[256,2048]{1,0:T(8,128)(2,1)} collective-permute-done((bf16[256,2048]{1,0:T(8,128)(2,1)}, bf16[256,2048]{1,0:T(8,128)(2,1)}, u32[]{:S(2)}, u32[]{:S(2)}) %collective-permute-start.53) | collective-permute-done | bytes 1048608 | tf_op jit(solution)/shard_map/ppermute | solution.py:25
  1228.6 5.7 fusion.29
  1252.2 45.3 %reduce-scatter.19.cloned.1.call-done = f32[256,3]{1,0:T(8,128)} async-done(((f32[2048,3]{1,0:T(8,128)}), f32[256,3]{1,0:T(8,128)}) %reduce-scatter.19.cloned.1.call-update) | async-done | bytes 3088
  1298.4 12.0 all-reduce.1
  1319.3 7.8 reduce-scatter.13.cloned.1.call-done
  (623 shorter events, 421.9 us)
Async XLA Ops:
  7.2 33.1 %all-gather.8.cloned.1.call-start = ((), (), s32[]{:S(2)}) async-start(), calls=%async_computation.16 | async-start | bytes 1310720 | tf_op jit(solution)/shard_map/all_gather | solution.py:461
  7.9 247.7 %all-gather.16.cloned.1.call-start = ((), (), s32[]{:S(2)}) async-start(), calls=%async_computation.25 | async-start | bytes 3932160 | tf_op jit(solution)/shard_map/all_gather | solution.py:450
  27.3 361.9 %all-gather.10.cloned.1.call-start = ((), (), s32[]{:S(2)}) async-start(), calls=%async_computation.17 | async-start | bytes 9437184 | tf_op jit(solution)/shard_map/all_gather | solution.py:460
  41.6 29.8 %all-to-all-start.2 = ((bf16[8,256,256]{1,2,0:T(8,128)(2,1)}), bf16[8,256,256]{1,2,0:T(8,128)(2,1)S(1)}, u32[]{:S(2)}, u32[]{:S(2)}) async-start(bf16[8,256,256]{1,2,0:T(8,128)(2,1)} %bitcast.384), calls=%async_computation.2 | async-start | bytes 2097152 | tf_op jit(solution)/shard_map/all_to_all | solution.py:466
  45.3 434.8 %all-gather.12.cloned.1.call-start = ((), (), s32[]{:S(2)}) async-start(), calls=%async_computation.18 | async-start | bytes 5242880 | tf_op jit(solution)/shard_map/all_gather | solution.py:467
  67.3 26.3 %collective-permute-start.23 = (bf16[256,2048]{1,0:T(8,128)(2,1)}, bf16[256,2048]{1,0:T(8,128)(2,1)}, u32[]{:S(2)}, u32[]{:S(2)}) collective-permute-start(bf16[256,2048]{1,0:T(8,128)(2,1)} %get-tuple-element.237), channel_id=1, source_target_pairs={{0,8},{4,12},{8,0},{12,4},{16,24},{20,28},{24,16},{28,20},{1,9},{5... | collective-permute-start | bytes 3145736 | tf_op jit(solution)/shard_map/ppermute | solution.py:25
  67.9 27.4 %collective-permute-start.24 = (bf16[256,2048]{1,0:T(8,128)(2,1)}, bf16[256,2048]{1,0:T(8,128)(2,1)}, u32[]{:S(2)}, u32[]{:S(2)}) collective-permute-start(bf16[256,2048]{1,0:T(8,128)(2,1)} %get-tuple-element.237), channel_id=1, source_target_pairs={{0,16},{4,20},{8,24},{12,28},{16,0},{20,4},{24,8},{28,12},{1,17},{... | collective-permute-start | bytes 3145736 | tf_op jit(solution)/shard_map/ppermute | solution.py:25
  69.4 125.9 %collective-permute-start = (bf16[256,2048]{1,0:T(8,128)(2,1)}, bf16[256,2048]{1,0:T(8,128)(2,1)}, u32[]{:S(2)}, u32[]{:S(2)}) collective-permute-start(bf16[256,2048]{1,0:T(8,128)(2,1)} %get-tuple-element.181), channel_id=1, source_target_pairs={{0,8},{4,12},{8,0},{12,4},{16,24},{20,28},{24,16},{28,20},{1,9},{5... | collective-permute-start | bytes 3145736 | tf_op jit(solution)/shard_map/ppermute | solution.py:25
  70.0 127.1 %collective-permute-start.1 = (bf16[256,2048]{1,0:T(8,128)(2,1)}, bf16[256,2048]{1,0:T(8,128)(2,1)}, u32[]{:S(2)}, u32[]{:S(2)}) collective-permute-start(bf16[256,2048]{1,0:T(8,128)(2,1)} %get-tuple-element.181), channel_id=1, source_target_pairs={{0,16},{4,20},{8,24},{12,28},{16,0},{20,4},{24,8},{28,12},{1,17},{... | collective-permute-start | bytes 3145736 | tf_op jit(solution)/shard_map/ppermute | solution.py:25
  75.9 137.3 %collective-permute-start.33 = (bf16[256,2048]{1,0:T(8,128)(2,1)}, bf16[256,2048]{1,0:T(8,128)(2,1)S(1)}, u32[]{:S(2)}, u32[]{:S(2)}) collective-permute-start(bf16[256,2048]{1,0:T(8,128)(2,1)} %get-tuple-element.244), channel_id=1, source_target_pairs={{0,8},{4,12},{8,0},{12,4},{16,24},{20,28},{24,16},{28,20},{1,9},{5... | collective-permute-start | bytes 3145736 | tf_op jit(solution)/shard_map/ppermute | solution.py:25
  76.5 155.7 %all-to-all-start.3 = ((bf16[8,256,256]{2,1,0:T(8,128)(2,1)}), bf16[8,256,256]{2,1,0:T(8,128)(2,1)}, u32[]{:S(2)}, u32[]{:S(2)}) async-start(bf16[8,256,256]{2,1,0:T(8,128)(2,1)} %bitcast.403), calls=%async_computation.3 | async-start | bytes 2097152 | tf_op jit(solution)/shard_map/all_to_all | solution.py:471
  80.7 423.3 %all-gather.14.cloned.1.call-start = ((), (), s32[]{:S(2)}) async-start(), calls=%async_computation.19 | async-start | bytes 5242880 | tf_op jit(solution)/shard_map/all_gather | solution.py:472
  94.7 49.1 %collective-permute-start.25 = (bf16[128,2048]{1,0:T(8,128)(2,1)S(1)}, bf16[128,2048]{1,0:T(8,128)(2,1)S(1)}, u32[]{:S(2)}, u32[]{:S(2)}) collective-permute-start(bf16[128,2048]{1,0:T(8,128)(2,1)S(1)} %slice.648), channel_id=1, source_target_pairs={{0,16},{4,20},{8,24},{12,28},{16,0},{20,4},{24,8},{28,12},{1,17},{... | collective-permute-start | bytes 1572872 | tf_op jit(solution)/shard_map/ppermute | solution.py:25
  96.5 97.6 %collective-permute-start.26 = (bf16[128,2048]{1,0:T(8,128)(2,1)S(1)}, bf16[128,2048]{1,0:T(8,128)(2,1)S(1)}, u32[]{:S(2)}, u32[]{:S(2)}) collective-permute-start(bf16[128,2048]{1,0:T(8,128)(2,1)S(1)} %slice.649), channel_id=1, source_target_pairs={{0,8},{4,12},{8,0},{12,4},{16,24},{20,28},{24,16},{28,20},{1,9},{5... | collective-permute-start | bytes 1572872 | tf_op jit(solution)/shard_map/ppermute | solution.py:25
  143.8 90.7 %collective-permute-start.34 = (bf16[256,2048]{1,0:T(8,128)(2,1)}, bf16[256,2048]{1,0:T(8,128)(2,1)}, u32[]{:S(2)}, u32[]{:S(2)}) collective-permute-start(bf16[256,2048]{1,0:T(8,128)(2,1)} %get-tuple-element.244), channel_id=1, source_target_pairs={{0,16},{4,20},{8,24},{12,28},{16,0},{20,4},{24,8},{28,12},{1,17},{... | collective-permute-start | bytes 3145736 | tf_op jit(solution)/shard_map/ppermute | solution.py:25
  195.2 75.1 %collective-permute-start.27 = (bf16[1024,2048]{1,0:T(8,128)(2,1)}, bf16[1024,2048]{1,0:T(8,128)(2,1)}, u32[]{:S(2)}, u32[]{:S(2)}) collective-permute-start(bf16[1024,2048]{1,0:T(8,128)(2,1)} %get-tuple-element.290), channel_id=1, source_target_pairs={{0,4},{4,0},{8,12},{12,8},{16,20},{20,16},{24,28},{28,24},{1,5},{5... | collective-permute-start | bytes 12582920 | tf_op jit(solution)/shard_map/ppermute | solution.py:25
  210.8 27.1 %collective-permute-start.10 = (bf16[256,2048]{1,0:T(8,128)(2,1)}, bf16[256,2048]{1,0:T(8,128)(2,1)}, u32[]{:S(2)}, u32[]{:S(2)}) collective-permute-start(bf16[256,2048]{1,0:T(8,128)(2,1)} %get-tuple-element.245), channel_id=1, source_target_pairs={{0,8},{4,12},{8,0},{12,4},{16,24},{20,28},{24,16},{28,20},{1,9},{5... | collective-permute-start | bytes 3145736 | tf_op jit(solution)/shard_map/ppermute | solution.py:25
  213.2 105.3 %collective-permute-start.4 = (bf16[1024,2048]{1,0:T(8,128)(2,1)}, bf16[1024,2048]{1,0:T(8,128)(2,1)}, u32[]{:S(2)}, u32[]{:S(2)}) collective-permute-start(bf16[1024,2048]{1,0:T(8,128)(2,1)} %get-tuple-element.278), channel_id=1, source_target_pairs={{0,4},{4,0},{8,12},{12,8},{16,20},{20,16},{24,28},{28,24},{1,5},{5... | collective-permute-start | bytes 12582920 | tf_op jit(solution)/shard_map/ppermute | solution.py:25
  213.2 27.3 %collective-permute-start.11 = (bf16[256,2048]{1,0:T(8,128)(2,1)}, bf16[256,2048]{1,0:T(8,128)(2,1)}, u32[]{:S(2)}, u32[]{:S(2)}) collective-permute-start(bf16[256,2048]{1,0:T(8,128)(2,1)} %get-tuple-element.245), channel_id=1, source_target_pairs={{0,16},{4,20},{8,24},{12,28},{16,0},{20,4},{24,8},{28,12},{1,17},{... | collective-permute-start | bytes 3145736 | tf_op jit(solution)/shard_map/ppermute | solution.py:25
  237.9 131.1 %collective-permute-start.36 = (bf16[128,2048]{1,0:T(8,128)(2,1)}, bf16[128,2048]{1,0:T(8,128)(2,1)}, u32[]{:S(2)}, u32[]{:S(2)}) collective-permute-start(bf16[128,2048]{1,0:T(8,128)(2,1)} %slice.654), channel_id=1, source_target_pairs={{0,8},{4,12},{8,0},{12,4},{16,24},{20,28},{24,16},{28,20},{1,9},{5... | collective-permute-start | bytes 1572872 | tf_op jit(solution)/shard_map/ppermute | solution.py:25
  240.6 131.0 %collective-permute-start.12 = (bf16[128,2048]{1,0:T(8,128)(2,1)}, bf16[128,2048]{1,0:T(8,128)(2,1)}, u32[]{:S(2)}, u32[]{:S(2)}) collective-permute-start(bf16[128,2048]{1,0:T(8,128)(2,1)} %slice.623), channel_id=1, source_target_pairs={{0,16},{4,20},{8,24},{12,28},{16,0},{20,4},{24,8},{28,12},{1,17},{... | collective-permute-start | bytes 1572872 | tf_op jit(solution)/shard_map/ppermute | solution.py:25
  253.9 119.7 %collective-permute-start.13 = (bf16[128,2048]{1,0:T(8,128)(2,1)}, bf16[128,2048]{1,0:T(8,128)(2,1)}, u32[]{:S(2)}, u32[]{:S(2)}) collective-permute-start(bf16[128,2048]{1,0:T(8,128)(2,1)} %slice.624), channel_id=1, source_target_pairs={{0,8},{4,12},{8,0},{12,4},{16,24},{20,28},{24,16},{28,20},{1,9},{5... | collective-permute-start | bytes 1572872 | tf_op jit(solution)/shard_map/ppermute | solution.py:25
  314.9 49.8 %all-to-all-start.4 = ((bf16[8,256,256]{1,2,0:T(8,128)(2,1)}), bf16[8,256,256]{1,2,0:T(8,128)(2,1)S(1)}, u32[]{:S(2)}, u32[]{:S(2)}) async-start(bf16[8,256,256]{1,2,0:T(8,128)(2,1)} %copy.362), calls=%async_computation.4 | async-start | bytes 2097152 | tf_op jit(solution)/shard_map/all_to_all | solution.py:490
  369.0 742.4 %reduce-scatter.15.cloned.1.call-start = ((), (), s32[]{:S(2)}) async-start(), calls=%async_computation.23 | async-start | bytes 5242880 | tf_op jit(solution)/shard_map/reduce_scatter | solution.py:600
  371.2 99.4 %collective-permute-start.37 = (bf16[1024,2048]{1,0:T(8,128)(2,1)}, bf16[1024,2048]{1,0:T(8,128)(2,1)}, u32[]{:S(2)}, u32[]{:S(2)}) collective-permute-start(bf16[1024,2048]{1,0:T(8,128)(2,1)} %get-tuple-element.282), channel_id=1, source_target_pairs={{0,4},{4,0},{8,12},{12,8},{16,20},{20,16},{24,28},{28,24},{1,5},{5... | collective-permute-start | bytes 12582920 | tf_op jit(solution)/shard_map/ppermute | solution.py:25
  375.9 99.5 %collective-permute-start.14 = (bf16[1024,2048]{1,0:T(8,128)(2,1)}, bf16[1024,2048]{1,0:T(8,128)(2,1)}, u32[]{:S(2)}, u32[]{:S(2)}) collective-permute-start(bf16[1024,2048]{1,0:T(8,128)(2,1)} %get-tuple-element.286), channel_id=1, source_target_pairs={{0,4},{4,0},{8,12},{12,8},{16,20},{20,16},{24,28},{28,24},{1,5},{5... | collective-permute-start | bytes 12582920 | tf_op jit(solution)/shard_map/ppermute | solution.py:25
  408.6 26.2 %collective-permute-start.28 = (bf16[256,2048]{1,0:T(8,128)(2,1)S(1)}, bf16[256,2048]{1,0:T(8,128)(2,1)S(1)}, u32[]{:S(2)}, u32[]{:S(2)}) collective-permute-start(bf16[256,2048]{1,0:T(8,128)(2,1)S(1)} %get-tuple-element.183), channel_id=1, source_target_pairs={{0,8},{4,12},{8,0},{12,4},{16,24},{20,28},{24,16},{28,20},{1,9},{5... | collective-permute-start | bytes 3145736 | tf_op jit(solution)/shard_map/ppermute | solution.py:25
  409.2 26.2 %collective-permute-start.29 = (bf16[256,2048]{1,0:T(8,128)(2,1)S(1)}, bf16[256,2048]{1,0:T(8,128)(2,1)S(1)}, u32[]{:S(2)}, u32[]{:S(2)}) collective-permute-start(bf16[256,2048]{1,0:T(8,128)(2,1)S(1)} %get-tuple-element.183), channel_id=1, source_target_pairs={{0,16},{4,20},{8,24},{12,28},{16,0},{20,4},{24,8},{28,12},{1,17},{... | collective-permute-start | bytes 3145736 | tf_op jit(solution)/shard_map/ppermute | solution.py:25
  426.7 60.6 %collective-permute-start.5 = (bf16[256,2048]{1,0:T(8,128)(2,1)S(1)}, bf16[256,2048]{1,0:T(8,128)(2,1)S(1)}, u32[]{:S(2)}, u32[]{:S(2)}) collective-permute-start(bf16[256,2048]{1,0:T(8,128)(2,1)S(1)} %get-tuple-element.350), channel_id=1, source_target_pairs={{0,8},{4,12},{8,0},{12,4},{16,24},{20,28},{24,16},{28,20},{1,9},{5... | collective-permute-start | bytes 3145736 | tf_op jit(solution)/shard_map/ppermute | solution.py:25
  435.5 30.8 %collective-permute-start.31 = (bf16[128,2048]{1,0:T(8,128)(2,1)S(1)}, bf16[128,2048]{1,0:T(8,128)(2,1)S(1)}, u32[]{:S(2)}, u32[]{:S(2)}) collective-permute-start(bf16[128,2048]{1,0:T(8,128)(2,1)S(1)} %slice.652), channel_id=1, source_target_pairs={{0,8},{4,12},{8,0},{12,4},{16,24},{20,28},{24,16},{28,20},{1,9},{5... | collective-permute-start | bytes 1572872 | tf_op jit(solution)/shard_map/ppermute | solution.py:25
  447.0 40.8 %collective-permute-start.6 = (bf16[256,2048]{1,0:T(8,128)(2,1)S(1)}, bf16[256,2048]{1,0:T(8,128)(2,1)S(1)}, u32[]{:S(2)}, u32[]{:S(2)}) collective-permute-start(bf16[256,2048]{1,0:T(8,128)(2,1)S(1)} %get-tuple-element.350), channel_id=1, source_target_pairs={{0,16},{4,20},{8,24},{12,28},{16,0},{20,4},{24,8},{28,12},{1,17},{... | collective-permute-start | bytes 3145736 | tf_op jit(solution)/shard_map/ppermute | solution.py:25
  470.6 46.6 %collective-permute-start.32 = (bf16[1024,2048]{1,0:T(8,128)(2,1)}, bf16[1024,2048]{1,0:T(8,128)(2,1)}, u32[]{:S(2)}, u32[]{:S(2)}) collective-permute-start(bf16[1024,2048]{1,0:T(8,128)(2,1)} %get-tuple-element.270), channel_id=1, source_target_pairs={{0,4},{4,0},{8,12},{12,8},{16,20},{20,16},{24,28},{28,24},{1,5},{5... | collective-permute-start | bytes 12582920 | tf_op jit(solution)/shard_map/ppermute | solution.py:25
  504.1 34.3 %collective-permute-start.9 = (bf16[1024,2048]{1,0:T(8,128)(2,1)}, bf16[1024,2048]{1,0:T(8,128)(2,1)}, u32[]{:S(2)}, u32[]{:S(2)}) collective-permute-start(bf16[1024,2048]{1,0:T(8,128)(2,1)} %get-tuple-element.274), channel_id=1, source_target_pairs={{0,4},{4,0},{8,12},{12,8},{16,20},{20,16},{24,28},{28,24},{1,5},{5... | collective-permute-start | bytes 12582920 | tf_op jit(solution)/shard_map/ppermute | solution.py:25
  685.5 453.3 %reduce-scatter.17.cloned.1.call-start = ((), (), s32[]{:S(2)}) async-start(), calls=%async_computation.24 | async-start | bytes 5242880 | tf_op jit(solution)/shard_map/reduce_scatter | solution.py:597
  696.3 44.2 %collective-permute-start.41 = (bf16[1024,2048]{1,0:T(8,128)(2,1)}, bf16[1024,2048]{1,0:T(8,128)(2,1)}, u32[]{:S(2)}, u32[]{:S(2)}) collective-permute-start(bf16[1024,2048]{1,0:T(8,128)(2,1)} %convolution_convert_fusion.4), channel_id=1, source_target_pairs={{0,4},{4,0},{8,12},{12,8},{16,20},{20,16},{24,28},{28,24},{1,5},{5... | collective-permute-start | bytes 12582920 | tf_op jit(solution)/shard_map/ppermute | solution.py:25
  702.7 53.5 %collective-permute-start.56 = (bf16[1024,2048]{1,0:T(8,128)(2,1)}, bf16[1024,2048]{1,0:T(8,128)(2,1)}, u32[]{:S(2)}, u32[]{:S(2)}) collective-permute-start(bf16[1024,2048]{1,0:T(8,128)(2,1)} %convolution_convert_fusion.2), channel_id=1, source_target_pairs={{0,4},{4,0},{8,12},{12,8},{16,20},{20,16},{24,28},{28,24},{1,5},{5... | collective-permute-start | bytes 12582920 | tf_op jit(solution)/shard_map/ppermute | solution.py:25
  727.0 41.5 %collective-permute-start.18 = (bf16[1024,2048]{1,0:T(8,128)(2,1)}, bf16[1024,2048]{1,0:T(8,128)(2,1)}, u32[]{:S(2)}, u32[]{:S(2)}) collective-permute-start(bf16[1024,2048]{1,0:T(8,128)(2,1)} %convolution_convert_fusion.5), channel_id=1, source_target_pairs={{0,4},{4,0},{8,12},{12,8},{16,20},{20,16},{24,28},{28,24},{1,5},{5... | collective-permute-start | bytes 12582920 | tf_op jit(solution)/shard_map/ppermute | solution.py:25
  727.0 55.4 %collective-permute-start.46 = (bf16[1024,2048]{1,0:T(8,128)(2,1)}, bf16[1024,2048]{1,0:T(8,128)(2,1)}, u32[]{:S(2)}, u32[]{:S(2)}) collective-permute-start(bf16[1024,2048]{1,0:T(8,128)(2,1)} %convolution_convert_fusion.3), channel_id=1, source_target_pairs={{0,4},{4,0},{8,12},{12,8},{16,20},{20,16},{24,28},{28,24},{1,5},{5... | collective-permute-start | bytes 12582920 | tf_op jit(solution)/shard_map/ppermute | solution.py:25
  740.4 495.3 %reduce-scatter.11.cloned.1.call-start = ((), (), s32[]{:S(2)}) async-start(), calls=%async_computation.21 | async-start | bytes 9437184 | tf_op jit(solution)/shard_map/reduce_scatter | solution.py:604
  754.1 70.2 %collective-permute-start.42 = (bf16[128,2048]{1,0:T(8,128)(2,1)}, bf16[128,2048]{1,0:T(8,128)(2,1)}, u32[]{:S(2)}, u32[]{:S(2)}) collective-permute-start(bf16[128,2048]{1,0:T(8,128)(2,1)} %get-tuple-element.224), channel_id=1, source_target_pairs={{0,16},{4,20},{8,24},{12,28},{16,0},{20,4},{24,8},{28,12},{1,17},{... | collective-permute-start | bytes 1572872 | tf_op jit(solution)/shard_map/ppermute | solution.py:25
  754.7 70.4 %collective-permute-start.44 = (bf16[128,2048]{1,0:T(8,128)(2,1)}, bf16[128,2048]{1,0:T(8,128)(2,1)}, u32[]{:S(2)}, u32[]{:S(2)}) collective-permute-start(bf16[128,2048]{1,0:T(8,128)(2,1)} %get-tuple-element.225), channel_id=1, source_target_pairs={{0,8},{4,12},{8,0},{12,4},{16,24},{20,28},{24,16},{28,20},{1,9},{5... | collective-permute-start | bytes 1572872 | tf_op jit(solution)/shard_map/ppermute | solution.py:25
  767.8 24.3 %collective-permute-start.57 = (bf16[128,2048]{1,0:T(8,128)(2,1)S(1)}, bf16[128,2048]{1,0:T(8,128)(2,1)S(1)}, u32[]{:S(2)}, u32[]{:S(2)}) collective-permute-start(bf16[128,2048]{1,0:T(8,128)(2,1)S(1)} %get-tuple-element.216), channel_id=1, source_target_pairs={{0,16},{4,20},{8,24},{12,28},{16,0},{20,4},{24,8},{28,12},{1,17},{... | collective-permute-start | bytes 1572872 | tf_op jit(solution)/shard_map/ppermute | solution.py:25
  768.5 24.7 %collective-permute-start.59 = (bf16[128,2048]{1,0:T(8,128)(2,1)S(1)}, bf16[128,2048]{1,0:T(8,128)(2,1)S(1)}, u32[]{:S(2)}, u32[]{:S(2)}) collective-permute-start(bf16[128,2048]{1,0:T(8,128)(2,1)S(1)} %get-tuple-element.217), channel_id=1, source_target_pairs={{0,8},{4,12},{8,0},{12,4},{16,24},{20,28},{24,16},{28,20},{1,9},{5... | collective-permute-start | bytes 1572872 | tf_op jit(solution)/shard_map/ppermute | solution.py:25
  807.0 33.7 %collective-permute-start.58 = (bf16[256,2048]{1,0:T(8,128)(2,1)S(1)}, bf16[256,2048]{1,0:T(8,128)(2,1)S(1)}, u32[]{:S(2)}, u32[]{:S(2)}) collective-permute-start(bf16[256,2048]{1,0:T(8,128)(2,1)S(1)} %pad_maximum_fusion.11), channel_id=1, source_target_pairs={{0,8},{4,12},{8,0},{12,4},{16,24},{20,28},{24,16},{28,20},{1,9},{5... | collective-permute-start | bytes 3145736 | tf_op jit(solution)/shard_map/ppermute | solution.py:25
  812.2 53.8 %collective-permute-start.60 = (bf16[256,2048]{1,0:T(8,128)(2,1)}, bf16[256,2048]{1,0:T(8,128)(2,1)}, u32[]{:S(2)}, u32[]{:S(2)}) collective-permute-start(bf16[256,2048]{1,0:T(8,128)(2,1)} %pad_maximum_fusion.12), channel_id=1, source_target_pairs={{0,16},{4,20},{8,24},{12,28},{16,0},{20,4},{24,8},{28,12},{1,17},{... | collective-permute-start | bytes 3145736 | tf_op jit(solution)/shard_map/ppermute | solution.py:25
  818.2 48.5 %collective-permute-start.20 = (bf16[256,2048]{1,0:T(8,128)(2,1)}, bf16[256,2048]{1,0:T(8,128)(2,1)}, u32[]{:S(2)}, u32[]{:S(2)}) collective-permute-start(bf16[256,2048]{1,0:T(8,128)(2,1)} %pad_maximum_fusion.3), channel_id=1, source_target_pairs={{0,8},{4,12},{8,0},{12,4},{16,24},{20,28},{24,16},{28,20},{1,9},{5... | collective-permute-start | bytes 3145736 | tf_op jit(solution)/shard_map/ppermute | solution.py:25
  824.3 43.6 %collective-permute-start.22 = (bf16[256,2048]{1,0:T(8,128)(2,1)}, bf16[256,2048]{1,0:T(8,128)(2,1)}, u32[]{:S(2)}, u32[]{:S(2)}) collective-permute-start(bf16[256,2048]{1,0:T(8,128)(2,1)} %pad_maximum_fusion.4), channel_id=1, source_target_pairs={{0,16},{4,20},{8,24},{12,28},{16,0},{20,4},{24,8},{28,12},{1,17},{... | collective-permute-start | bytes 3145736 | tf_op jit(solution)/shard_map/ppermute | solution.py:25
  825.1 60.6 %collective-permute-start.48 = (bf16[256,2048]{1,0:T(8,128)(2,1)}, bf16[256,2048]{1,0:T(8,128)(2,1)}, u32[]{:S(2)}, u32[]{:S(2)}) collective-permute-start(bf16[256,2048]{1,0:T(8,128)(2,1)} %pad_maximum_fusion.7), channel_id=1, source_target_pairs={{0,8},{4,12},{8,0},{12,4},{16,24},{20,28},{24,16},{28,20},{1,9},{5... | collective-permute-start | bytes 3145736 | tf_op jit(solution)/shard_map/ppermute | solution.py:25
  841.7 44.0 %collective-permute-start.50 = (bf16[256,2048]{1,0:T(8,128)(2,1)}, bf16[256,2048]{1,0:T(8,128)(2,1)}, u32[]{:S(2)}, u32[]{:S(2)}) collective-permute-start(bf16[256,2048]{1,0:T(8,128)(2,1)} %pad_maximum_fusion.8), channel_id=1, source_target_pairs={{0,16},{4,20},{8,24},{12,28},{16,0},{20,4},{24,8},{28,12},{1,17},{... | collective-permute-start | bytes 3145736 | tf_op jit(solution)/shard_map/ppermute | solution.py:25
  865.9 40.6 %collective-permute-start.43 = (bf16[256,2048]{1,0:T(8,128)(2,1)S(1)}, bf16[256,2048]{1,0:T(8,128)(2,1)S(1)}, u32[]{:S(2)}, u32[]{:S(2)}) collective-permute-start(bf16[256,2048]{1,0:T(8,128)(2,1)S(1)} %pad_maximum_fusion.5), channel_id=1, source_target_pairs={{0,8},{4,12},{8,0},{12,4},{16,24},{20,28},{24,16},{28,20},{1,9},{5... | collective-permute-start | bytes 3145736 | tf_op jit(solution)/shard_map/ppermute | solution.py:25
  866.7 39.8 %collective-permute-start.45 = (bf16[256,2048]{1,0:T(8,128)(2,1)S(1)}, bf16[256,2048]{1,0:T(8,128)(2,1)S(1)}, u32[]{:S(2)}, u32[]{:S(2)}) collective-permute-start(bf16[256,2048]{1,0:T(8,128)(2,1)S(1)} %pad_maximum_fusion.6), channel_id=1, source_target_pairs={{0,16},{4,20},{8,24},{12,28},{16,0},{20,4},{24,8},{28,12},{1,17},{... | collective-permute-start | bytes 3145736 | tf_op jit(solution)/shard_map/ppermute | solution.py:25
  997.5 53.8 %all-to-all-start.5 = ((bf16[8,256,256]{2,1,0:T(8,128)(2,1)}), bf16[8,256,256]{2,1,0:T(8,128)(2,1)}, u32[]{:S(2)}, u32[]{:S(2)}) async-start(bf16[8,256,256]{2,1,0:T(8,128)(2,1)} %bitcast.383), calls=%async_computation.5 | async-start | bytes 2097152 | tf_op jit(solution)/shard_map/all_to_all | solution.py:556
  1051.1 97.6 %collective-permute-start.61 = (bf16[1024,2048]{1,0:T(8,128)(2,1)}, bf16[1024,2048]{1,0:T(8,128)(2,1)}, u32[]{:S(2)}, u32[]{:S(2)}) collective-permute-start(bf16[1024,2048]{1,0:T(8,128)(2,1)} %convolution_convert_fusion), channel_id=1, source_target_pairs={{0,4},{4,0},{8,12},{12,8},{16,20},{20,16},{24,28},{28,24},{1,5},{5... | collective-permute-start | bytes 12582920 | tf_op jit(solution)/shard_map/ppermute | solution.py:25
  1096.9 62.9 %collective-permute-start.51 = (bf16[1024,2048]{1,0:T(8,128)(2,1)}, bf16[1024,2048]{1,0:T(8,128)(2,1)}, u32[]{:S(2)}, u32[]{:S(2)}) collective-permute-start(bf16[1024,2048]{1,0:T(8,128)(2,1)} %convolution_convert_fusion.1), channel_id=1, source_target_pairs={{0,4},{4,0},{8,12},{12,8},{16,20},{20,16},{24,28},{28,24},{1,5},{5... | collective-permute-start | bytes 12582920 | tf_op jit(solution)/shard_map/ppermute | solution.py:25
  1113.6 27.4 %all-to-all-start.8 = ((bf16[8,256,256]{2,1,0:T(8,128)(2,1)}), bf16[8,256,256]{2,1,0:T(8,128)(2,1)}, u32[]{:S(2)}, u32[]{:S(2)}) async-start(bf16[8,256,256]{2,1,0:T(8,128)(2,1)} %bitcast.94), calls=%async_computation.12 | async-start | bytes 2097152 | tf_op jit(solution)/shard_map/all_to_all | solution.py:601
  1117.9 124.1 %reduce-scatter.9.cloned.1.call-start = ((), (), s32[]{:S(2)}) async-start(), calls=%async_computation.20 | async-start | bytes 3932160 | tf_op jit(solution)/shard_map/reduce_scatter | solution.py:611
  1141.0 55.1 %all-to-all-start.9 = ((bf16[8,256,256]{2,1,0:T(8,128)(2,1)}), bf16[8,256,256]{2,1,0:T(8,128)(2,1)}, u32[]{:S(2)}, u32[]{:S(2)}) async-start(bf16[8,256,256]{2,1,0:T(8,128)(2,1)} %bitcast.327), calls=%async_computation.14 | async-start | bytes 2097152 | tf_op jit(solution)/shard_map/all_to_all | solution.py:598
  1145.4 152.1 %reduce-scatter.19.cloned.1.call-start = ((), (), s32[]{:S(2)}) async-start(), calls=%async_computation.26 | async-start | bytes 1179648
  1176.1 31.1 %collective-permute-start.63 = (bf16[256,2048]{1,0:T(8,128)(2,1)}, bf16[256,2048]{1,0:T(8,128)(2,1)}, u32[]{:S(2)}, u32[]{:S(2)}) collective-permute-start(bf16[256,2048]{1,0:T(8,128)(2,1)} %pad_maximum_fusion.13), channel_id=1, source_target_pairs={{0,8},{4,12},{8,0},{12,4},{16,24},{20,28},{24,16},{28,20},{1,9},{5... | collective-permute-start | bytes 3145736 | tf_op jit(solution)/shard_map/ppermute | solution.py:25
  1178.6 28.6 %collective-permute-start.65 = (bf16[256,2048]{1,0:T(8,128)(2,1)}, bf16[256,2048]{1,0:T(8,128)(2,1)}, u32[]{:S(2)}, u32[]{:S(2)}) collective-permute-start(bf16[256,2048]{1,0:T(8,128)(2,1)} %pad_maximum_fusion.14), channel_id=1, source_target_pairs={{0,16},{4,20},{8,24},{12,28},{16,0},{20,4},{24,8},{28,12},{1,17},{... | collective-permute-start | bytes 3145736 | tf_op jit(solution)/shard_map/ppermute | solution.py:25
  1185.9 42.6 %collective-permute-start.53 = (bf16[256,2048]{1,0:T(8,128)(2,1)}, bf16[256,2048]{1,0:T(8,128)(2,1)}, u32[]{:S(2)}, u32[]{:S(2)}) collective-permute-start(bf16[256,2048]{1,0:T(8,128)(2,1)} %pad_maximum_fusion.9), channel_id=1, source_target_pairs={{0,8},{4,12},{8,0},{12,4},{16,24},{20,28},{24,16},{28,20},{1,9},{5... | collective-permute-start | bytes 3145736 | tf_op jit(solution)/shard_map/ppermute | solution.py:25
  1188.4 40.1 %collective-permute-start.55 = (bf16[256,2048]{1,0:T(8,128)(2,1)}, bf16[256,2048]{1,0:T(8,128)(2,1)}, u32[]{:S(2)}, u32[]{:S(2)}) collective-permute-start(bf16[256,2048]{1,0:T(8,128)(2,1)} %pad_maximum_fusion.10), channel_id=1, source_target_pairs={{0,16},{4,20},{8,24},{12,28},{16,0},{20,4},{24,8},{28,12},{1,17},{... | collective-permute-start | bytes 3145736 | tf_op jit(solution)/shard_map/ppermute | solution.py:25
  1235.7 91.4 %reduce-scatter.13.cloned.1.call-start = ((), (), s32[]{:S(2)}) async-start(), calls=%async_computation.22 | async-start | bytes 1310720 | tf_op jit(solution)/shard_map/reduce_scatter | solution.py:605
  1244.6 69.0 %all-to-all-start.7 = ((bf16[8,3,64,256]{3,2,1,0:T(8,128)(2,1)}), bf16[8,3,64,256]{3,2,1,0:T(8,128)(2,1)S(1)}, u32[]{:S(2)}, u32[]{:S(2)}) async-start(bf16[8,3,64,256]{3,2,1,0:T(8,128)(2,1)} %copy.391), calls=%async_computation.8 | async-start | bytes 1572864 | tf_op jit(solution)/shard_map/all_to_all | solution.py:613
  (129 other events, 2201.6 us)
Sparse Core Ops, SparseCore 0:
  9.6 30.6 all-gather.7
  41.8 62.9 all-gather.15
  106.8 97.9 all-gather.9
  206.1 79.3 all-gather.11
  286.9 79.0 all-gather.13
  685.6 82.7 reduce-scatter.14
  770.7 77.2 reduce-scatter.16
  958.8 96.0 reduce-scatter.10
  1138.8 85.5 reduce-scatter.8
  1235.8 61.6 reduce-scatter.18
  1299.9 27.2 reduce-scatter.12

commit v2 on v1

v2 whole, which is shorter than its diff:
```python
from functools import partial

import jax
import jax.numpy as jnp
import numpy as np
from jax import lax
from jax.experimental import pallas as pl
from jax.experimental.pallas import tpu as pltpu
from jax.sharding import PartitionSpec as P

HEAD_DIM = 64
HALF = HEAD_DIM // 2
SEQ_LEN = 2048
SCALE_BASE = 512
EPSILON = 1e-05
MASKED_SCORE = -1e30
FACTOR = HEAD_DIM ** (-0.5)
BF = jnp.bfloat16
F32 = jnp.float32
HASTE = 3
VMEM_LIMIT = 56 * 1024 * 1024


def swap(block, bit):
    size = lax.axis_size("seq")
    return lax.ppermute(block, "seq", [(i, i ^ bit) for i in range(size)])


def after(array, *others):
    return lax.optimization_barrier((array,) + others)[0]


class Line:
    def __init__(self):
        self.last, self.noted = (), ()

    def put(self, array):
        return after(array, *self.last) if self.last else array

    def note(self, *arrays):
        self.noted += arrays

    def enter(self, array):
        return after(array, *self.last, *self.noted) if self.last + self.noted else array

    def mark(self, *arrays):
        self.last, self.noted = arrays, ()


def join_kernel(*refs):
    parts, out_ref, held, came, left = refs[:-4], refs[-4], refs[-3], refs[-2], refs[-1]
    spots, at = [], 0
    for part in parts:
        spots.append(pl.ds(at, part.shape[0]))
        at += part.shape[0]
    ins = [
        pltpu.make_async_copy(part, held.at[spot], came.at[k])
        for k, (part, spot) in enumerate(zip(parts, spots))
    ]
    outs = [
        pltpu.make_async_copy(held.at[spot], out_ref.at[spot], left.at[k])
        for k, spot in enumerate(spots)
    ]
    for copy in ins:
        copy.start()
    for k, copy in enumerate(ins):
        copy.wait()
        outs[k].start()
    for copy in outs:
        copy.wait()


def join(parts):
    rows, width = sum(part.shape[0] for part in parts), parts[0].shape[1]
    if any(part.shape[0] % 16 for part in parts) or width % 128:
        return jnp.concatenate(parts)
    return pl.pallas_call(
        join_kernel,
        in_specs=[pl.BlockSpec(memory_space=pl.ANY)] * len(parts),
        out_specs=pl.BlockSpec(memory_space=pl.ANY),
        out_shape=jax.ShapeDtypeStruct((rows, width), parts[0].dtype),
        scratch_shapes=[
            pltpu.VMEM((rows, width), parts[0].dtype),
            pltpu.SemaphoreType.DMA((len(parts),)),
            pltpu.SemaphoreType.DMA((len(parts),)),
        ],
        compiler_params=params(),
        cost_estimate=cost(0, 4 * rows * width),
        name="join",
    )(*parts)


class Gather:
    def __init__(self, line, rows):
        self.line = line
        self.size = lax.axis_size("seq")
        self.rows = line.put(rows)
        self.pieces = [self.rows]
        if self.size == 8:
            self.pieces += [swap(self.rows, 2), swap(self.rows, 4)]
        line.note(self.rows)

    def corner(self):
        if self.size == 8:
            half = self.rows.shape[0] // 2
            across = self.line.put(self.pieces[1])[:half]
            along = self.line.put(self.pieces[2])[half:]
            self.pieces += [swap(across, 4), swap(along, 2)]
            self.line.note(across, along)
        return self

    def core(self):
        even = self.line.put(self.pieces[0])
        if self.size == 8:
            even = join([even] + self.pieces[1:])
        else:
            bit = 2
            while bit < self.size:
                even = jnp.concatenate([even, swap(even, bit)])
                bit *= 2
        self.halves = (even, swap(even, 1))
        self.line.note(even)
        return self


class Scatter:
    def __init__(self, line, odd, count):
        self.line, self.count = line, count
        self.size = lax.axis_size("seq")
        self.other = swap(odd, 1)

    def block(self, k, start, stop):
        here = slice(k * self.count + start, k * self.count + stop)
        return self.even[here].astype(F32) + self.other[here].astype(F32)

    def corner(self, even):
        self.even = self.line.put(even)
        if self.size == 8:
            half = self.count // 2
            low = self.block(3, 0, half).astype(BF)
            high = self.block(3, half, self.count).astype(BF)
            self.low, self.high = swap(low, 4), swap(high, 2)
            self.line.note(low, high)
        return self

    def near(self):
        if self.size == 8:
            half = self.count // 2
            low, high = self.line.put(self.low), self.line.put(self.high)
            across = [self.block(1, 0, half) + low.astype(F32), self.block(1, half, self.count)]
            along = [self.block(2, 0, half), self.block(2, half, self.count) + high.astype(F32)]
            across = jnp.concatenate(across).astype(BF)
            along = jnp.concatenate(along).astype(BF)
            self.parts = [swap(across, 2), swap(along, 4)]
            self.line.note(across, along)
        return self

    def total(self):
        if self.size == 8:
            return self.block(0, 0, self.count) + sum(part.astype(F32) for part in self.parts)
        total, bit = self.even.astype(F32) + self.other.astype(F32), self.size // 2
        while bit > 1:
            middle = total.shape[0] // 2
            total = total[:middle] + swap(total[middle:].astype(BF), bit).astype(F32)
            bit //= 2
        return total


class BlockSum:
    def __init__(self, line, stats):
        self.line, self.stats, self.bit = line, line.put(stats), 1
        self.size = stats.shape[0]
        self.send()

    def send(self):
        self.other = swap(self.stats, self.bit)
        self.line.note(self.stats)

    def add(self):
        shift = (self.bit & 1) * (self.size // 2) + (self.bit >> 1)
        other = self.line.put(self.other)
        self.stats = self.stats + jnp.stack([other[i ^ shift] for i in range(self.size)])
        self.bit *= 2

    def more(self):
        self.add()
        if self.bit < self.size:
            self.send()

    def total(self):
        while self.bit < self.size:
            self.add()
            if self.bit < self.size:
                self.send()
        return self.stats


def row_norm(features):
    mean = jnp.mean(features, axis=-1, keepdims=True)
    second = jnp.mean(features * features, axis=-1, keepdims=True)
    inverse = lax.rsqrt(second - mean * mean + EPSILON)
    return (features - mean) * inverse, inverse


def row_norm_back(scaled, normed, inverse):
    return inverse * (
        scaled
        - jnp.mean(scaled, axis=-1, keepdims=True)
        - normed * jnp.mean(scaled * normed, axis=-1, keepdims=True)
    )


def dot(a, b, dims):
    return lax.dot_general(a, b, (dims, ((), ())), preferred_element_type=F32)


NN = ((1,), (0,))
NT = ((1,), (1,))
TN = ((0,), (0,))


def params():
    return pltpu.CompilerParams(vmem_limit_bytes=VMEM_LIMIT)


def cost(flops, moved, special=0):
    return pl.CostEstimate(
        flops=int(flops) // HASTE, bytes_accessed=int(moved) // HASTE, transcendentals=int(special) // HASTE
    )


def qkv_kernel(
    place, x_ref, w_ref, cq_ref, sq_ref, ck_ref, sk_ref, qa, ka, va, q_ref, k_ref, v_ref
):
    cols = q_ref.shape[1]
    half = cols // 2
    full = dot(x_ref[...], w_ref[...], NN)
    q1, q2 = full[:, :half], full[:, half:cols]
    k1, k2 = full[:, cols : cols + half], full[:, cols + half : 2 * cols]
    cq, sq, ck, sk = cq_ref[...], sq_ref[...], ck_ref[...], sk_ref[...]
    q_ref[:, :half] = (q1 * cq - q2 * sq).astype(BF)
    q_ref[:, half:] = (q2 * cq + q1 * sq).astype(BF)
    k_ref[:, :half] = (k1 * ck - k2 * sk).astype(BF)
    k_ref[:, half:] = (k2 * ck + k1 * sk).astype(BF)
    v_ref[...] = full[:, 2 * cols :].astype(BF)


def project(place, rows, weights, tables, count, before):
    here, width = rows.shape
    cols = weights.shape[1] // 3
    length = tables[0].shape[0]
    table = pl.BlockSpec((count, cols // 2), lambda i, place: (place[i], 0))
    out = pl.BlockSpec((count, cols), lambda i, place: (place[i], 0))
    held = pl.BlockSpec(memory_space=pl.ANY)
    return pl.pallas_call(
        qkv_kernel,
        grid_spec=pltpu.PrefetchScalarGridSpec(
            num_scalar_prefetch=1,
            grid=(here // count,),
            in_specs=[
                pl.BlockSpec((count, width), lambda i, place: (i, 0)),
                pl.BlockSpec((width, 3 * cols), lambda i, place: (0, 0)),
                table,
                table,
                table,
                table,
                held,
                held,
                held,
            ],
            out_specs=[out, out, out],
        ),
        out_shape=[jax.ShapeDtypeStruct((length, cols), BF)] * 3,
        input_output_aliases={7: 0, 8: 1, 9: 2},
        compiler_params=params(),
        cost_estimate=cost(
            2 * here * width * 3 * cols, 2 * (here * width + 3 * cols * width + 3 * here * cols)
        ),
        name="project",
    )(place, rows, weights, *tables, *before)


def turned_row(kind, head, heads):
    first = kind * heads * HEAD_DIM
    if kind == 2:
        return first + head * HEAD_DIM, first + head * HEAD_DIM + HALF
    return first + head * HALF, first + (heads + head) * HALF


def arrange_kernel(raw_ref, turned_ref, plain_ref):
    parts, size, _, split, count = raw_ref.shape
    each = split // HEAD_DIM
    for kind in range(3):
        for t in range(parts):
            for j in range(each):
                starts = turned_row(kind, t * each + j, parts * each)
                for b in range(size):
                    for h in range(2):
                        here = slice(j * HEAD_DIM + h * HALF, j * HEAD_DIM + (h + 1) * HALF)
                        turned_ref[starts[h] : starts[h] + HALF, b * count : (b + 1) * count] = (
                            raw_ref[t, b, kind, here, :]
                        )
    plain_ref[...] = turned_ref[...].T


def arrange(raw):
    parts, size, _, split, count = raw.shape
    cols, width = parts * split, size * count
    if count % 128:
        proj = raw.transpose(2, 0, 3, 1, 4).reshape(3, cols, width)
        heads = proj[:2].reshape(2, cols // HEAD_DIM, 2, HALF, width).transpose(0, 2, 1, 3, 4)
        turned = jnp.concatenate([heads.reshape(2 * cols, width), proj[2]])
        return turned, turned.T
    return pl.pallas_call(
        arrange_kernel,
        out_shape=[
            jax.ShapeDtypeStruct((3 * cols, width), BF),
            jax.ShapeDtypeStruct((width, 3 * cols), BF),
        ],
        compiler_params=params(),
        cost_estimate=cost(0, 18 * cols * width),
        name="arrange",
    )(raw)


def out_grad_kernel(*refs):
    out_ref = refs[-1]
    parts = (len(refs) - 1) // 2
    total = dot(refs[0][...], refs[parts][...], TN)
    for k in range(1, parts):
        total = total + dot(refs[k][...], refs[parts + k][...], TN)
    low = total.astype(BF)
    count = out_ref.shape[-1]
    for b in range(out_ref.shape[0]):
        out_ref[b] = low[:, b * count : (b + 1) * count].reshape(out_ref.shape[1:])


def out_grad(inners, grads, split):
    size, count, cols = inners[0].shape
    width = size * cols
    count_out = width // size
    if split:
        shape = (size, cols // split, size, split, count_out)
        spec = pl.BlockSpec(
            (size, cols // split, pl.squeezed, split, count_out), lambda i: (0, 0, i, 0, 0)
        )
    else:
        shape = (size, size, cols, count_out)
        spec = pl.BlockSpec((size, pl.squeezed, cols, count_out), lambda i: (0, i, 0, 0))
    parts = len(inners)
    return pl.pallas_call(
        out_grad_kernel,
        grid=(size,),
        in_specs=[pl.BlockSpec((pl.squeezed, count, cols), lambda i: (i, 0, 0))] * parts
        + [pl.BlockSpec((count, width), lambda i: (0, 0))] * parts,
        out_specs=spec,
        out_shape=jax.ShapeDtypeStruct(shape, BF),
        compiler_params=params(),
        cost_estimate=cost(
            2 * parts * count * width * width, 4 * parts * count * width + 2 * width * width
        ),
        name="out_grad",
    )(*inners, *grads).reshape(size, width, count_out)


def head_rows(weight, b, split):
    return weight[:, b].reshape(-1, weight.shape[-1]) if split else weight[b]


def out_kernel(
    split, place, came_ref, even_ref, odd_ref, x_ref, gi_ref, gf_ref, inner_ref, res_ref, mid_ref, acc
):
    i = pl.program_id(0)
    size, rows, cols = came_ref.shape
    width = size * cols
    count = width // size

    @pl.when(i == 0)
    def _():
        first = jnp.zeros((rows, 1), F32)
        second = jnp.zeros((rows, 1), F32)
        for b in range(size):
            part = came_ref[b].astype(F32)
            first += jnp.sum(part, axis=1, keepdims=True)
            second += jnp.sum(part * part, axis=1, keepdims=True)
        mean = first / width
        inverse = lax.rsqrt(second / width - mean * mean + EPSILON)
        for b in range(size):
            inner_ref[b] = ((came_ref[b].astype(F32) - mean) * inverse * gi_ref[b]).astype(BF)

    def piece(ref):
        total = jnp.zeros((rows, count), F32)
        for b in range(size):
            total += dot(inner_ref[b], head_rows(ref, b, split), NN)
        acc[place[i]] = total

    pl.when(i < size // 2)(lambda: piece(even_ref))
    pl.when(i >= size // 2)(lambda: piece(odd_ref))

    @pl.when(i == size - 1)
    def _():
        first = jnp.zeros((rows, 1), F32)
        second = jnp.zeros((rows, 1), F32)
        for b in range(size):
            here = slice(b * count, (b + 1) * count)
            part = acc[b] + x_ref[:, here].astype(F32)
            res_ref[:, here] = part
            first += jnp.sum(part, axis=1, keepdims=True)
            second += jnp.sum(part * part, axis=1, keepdims=True)
        mean = first / width
        inverse = lax.rsqrt(second / width - mean * mean + EPSILON)
        mid_ref[...] = ((res_ref[...] - mean) * inverse * gf_ref[...]).astype(BF)


def weight_views(pieces, size, cols, split):
    half, count = size // 2, pieces[0].shape[1]
    if split:
        shape = (cols // split, size, split, count)
    else:
        shape = (size, cols, count)
    zeros = (0,) * len(shape)
    views = [piece.reshape((half,) + shape) for piece in pieces]
    specs = [
        pl.BlockSpec((pl.squeezed,) + shape, lambda i, *_: (jnp.minimum(i, half - 1),) + zeros),
        pl.BlockSpec((pl.squeezed,) + shape, lambda i, *_: (jnp.maximum(i - half, 0),) + zeros),
    ]
    return views, specs


def out_project(place, came, pieces, rows, gain_inner, gain_ffn, split):
    size, count, cols = came.shape
    width = size * cols
    views, specs = weight_views(pieces, size, cols, split)
    blocks = pl.BlockSpec((size, count, cols), lambda i, *_: (0, 0, 0))
    flat = pl.BlockSpec((count, width), lambda i, *_: (0, 0))
    return pl.pallas_call(
        partial(out_kernel, split),
        grid_spec=pltpu.PrefetchScalarGridSpec(
            num_scalar_prefetch=1,
            grid=(size,),
            in_specs=[blocks]
            + specs
            + [
                flat,
                pl.BlockSpec((size, 1, cols), lambda i, *_: (0, 0, 0)),
                pl.BlockSpec((1, width), lambda i, *_: (0, 0)),
            ],
            out_specs=[blocks, flat, flat],
            scratch_shapes=[pltpu.VMEM((size, count, width // size), F32)],
        ),
        out_shape=[
            jax.ShapeDtypeStruct((size, count, cols), BF),
            jax.ShapeDtypeStruct((count, width), F32),
            jax.ShapeDtypeStruct((count, width), BF),
        ],
        compiler_params=params(),
        cost_estimate=cost(2 * count * width * width, 2 * width * width + 12 * count * width),
        name="out_project",
    )(place, came, *views, rows, gain_inner, gain_ffn)


def out_back_kernel(
    split, place, grad_ref, res_ref, cot_ref, came_ref, even_ref, odd_ref, gi_ref, gf_ref,
    rg_ref, ag_ref, back_ref, fg_ref, ig_ref, held, sent,
):
    i = pl.program_id(0)
    size, rows, cols = came_ref.shape
    width = size * cols
    count = width // size

    @pl.when(i == 0)
    def _():
        residual, grad = res_ref[...], grad_ref[...]
        mean = jnp.mean(residual, axis=1, keepdims=True)
        second = jnp.mean(residual * residual, axis=1, keepdims=True)
        inverse = lax.rsqrt(second - mean * mean + EPSILON)
        normal = (residual - mean) * inverse
        fg_ref[...] = jnp.sum(grad * normal, axis=0, keepdims=True)
        scaled = grad * gf_ref[...]
        back = inverse * (
            scaled
            - jnp.mean(scaled, axis=1, keepdims=True)
            - normal * jnp.mean(scaled * normal, axis=1, keepdims=True)
        )
        total = cot_ref[...].astype(F32) + back
        rg_ref[...] = total
        low = total.astype(BF)
        ag_ref[...] = low
        for b in range(size):
            sent[b] = low[:, b * count : (b + 1) * count]
        held[...] = jnp.zeros_like(held)

    def piece(ref):
        grad = sent[place[i]]
        for b in range(size):
            held[b] += dot(grad, head_rows(ref, b, split), NT)

    pl.when(i < size // 2)(lambda: piece(even_ref))
    pl.when(i >= size // 2)(lambda: piece(odd_ref))

    @pl.when(i == size - 1)
    def _():
        zero = jnp.zeros((rows, 1), F32)
        first, second = zero, zero
        for b in range(size):
            part = came_ref[b].astype(F32)
            first += jnp.sum(part, axis=1, keepdims=True)
            second += jnp.sum(part * part, axis=1, keepdims=True)
        mean = first / width
        inverse = lax.rsqrt(second / width - mean * mean + EPSILON)
        plain, cross = zero, zero
        for b in range(size):
            normal = (came_ref[b].astype(F32) - mean) * inverse
            grad = held[b]
            ig_ref[b] = jnp.sum(grad * normal, axis=0, keepdims=True)
            scaled = grad * gi_ref[b]
            plain += jnp.sum(scaled, axis=1, keepdims=True)
            cross += jnp.sum(scaled * normal, axis=1, keepdims=True)
        plain, cross = plain / width, cross / width
        for b in range(size):
            normal = (came_ref[b].astype(F32) - mean) * inverse
            back_ref[b] = (inverse * (held[b] * gi_ref[b] - plain - normal * cross)).astype(BF)


def out_back(place, grad, residual, cotangent, came, pieces, gain_inner, gain_ffn, split):
    size, count, cols = came.shape
    width = size * cols
    views, specs = weight_views(pieces, size, cols, split)
    blocks = pl.BlockSpec((size, count, cols), lambda i, *_: (0, 0, 0))
    flat = pl.BlockSpec((count, width), lambda i, *_: (0, 0))
    line = pl.BlockSpec((1, width), lambda i, *_: (0, 0))
    lines = pl.BlockSpec((size, 1, cols), lambda i, *_: (0, 0, 0))
    return pl.pallas_call(
        partial(out_back_kernel, split),
        grid_spec=pltpu.PrefetchScalarGridSpec(
            num_scalar_prefetch=1,
            grid=(size,),
            in_specs=[flat, flat, flat, blocks] + specs + [lines, line],
            out_specs=[flat, flat, blocks, line, lines],
            scratch_shapes=[
                pltpu.VMEM((size, count, cols), F32),
                pltpu.VMEM((size, count, width // size), BF),
            ],
        ),
        out_shape=[
            jax.ShapeDtypeStruct((count, width), F32),
            jax.ShapeDtypeStruct((count, width), BF),
            jax.ShapeDtypeStruct((size, count, cols), BF),
            jax.ShapeDtypeStruct((1, width), F32),
            jax.ShapeDtypeStruct((size, 1, cols), F32),
        ],
        compiler_params=params(),
        cost_estimate=cost(2 * count * width * width, 2 * width * width + 20 * count * width),
        name="out_back",
    )(place, grad, residual, cotangent, came, *views, gain_inner, gain_ffn)


def ffn_grad_kernel(c_ref, down_ref, g_ref, t_ref):
    t_ref[...] = (dot(c_ref[...], down_ref[...], NT) * g_ref[...]).astype(BF)


def ffn_grad(grads, down, gain):
    here, width = grads.shape
    cols = down.shape[0]
    tile = 256
    return pl.pallas_call(
        ffn_grad_kernel,
        grid=(here // tile,),
        in_specs=[
            pl.BlockSpec((tile, width), lambda i: (i, 0)),
            pl.BlockSpec((cols, width), lambda i: (0, 0)),
            pl.BlockSpec((1, cols), lambda i: (0, 0)),
        ],
        out_specs=pl.BlockSpec((tile, cols), lambda i: (i, 0)),
        out_shape=jax.ShapeDtypeStruct((here, cols), BF),
        compiler_params=params(),
        cost_estimate=cost(2 * here * width * cols, 2 * here * (width + cols) + 2 * width * cols),
        name="ffn_grad",
    )(grads, down, gain)


def ffn_in_kernel(given, *refs):
    if given:
        x_ref, t_in_ref, up_ref, a_ref, p_ref, s_ref = refs
    else:
        x_ref, c_ref, up_ref, down_ref, g_ref, a_ref, p_ref, s_ref, t_ref = refs
    parts, _, units = up_ref.shape
    sums = [0.0] * 4
    for k in range(parts):
        here = slice(k * units, (k + 1) * units)
        hidden = dot(x_ref[...], up_ref[k], NN)
        if given:
            scaled = t_in_ref[:, here].astype(F32)
        else:
            low = (dot(c_ref[...], down_ref[here, :], NT) * g_ref[:, here]).astype(BF)
            t_ref[:, here] = low
            scaled = low.astype(F32)
        share = 0.5 * (1.0 + lax.erf(hidden * (2.0**-0.5)))
        activated = hidden * share
        slope = share + hidden * jnp.exp(-0.5 * hidden * hidden) * ((2.0 * np.pi) ** -0.5)
        a_ref[:, here] = activated
        p_ref[:, here] = slope.astype(BF)
        for j, terms in enumerate((activated, activated * activated, scaled, scaled * activated)):
            sums[j] = sums[j] + jnp.sum(terms, axis=1, keepdims=True)
    for j in range(4):
        s_ref[:, j : j + 1] = sums[j]


def ffn_in(rows, up_parts, scaled=None, grads=None, down=None, gain=None):
    given = scaled is not None
    here, width = rows.shape
    parts, _, units = up_parts.shape
    cols = parts * units
    tile = 256
    wide = pl.BlockSpec((tile, width), lambda i: (i, 0))
    out = pl.BlockSpec((tile, cols), lambda i: (i, 0))
    up_spec = pl.BlockSpec(up_parts.shape, lambda i: (0, 0, 0))
    if given:
        arrays, specs = (rows, scaled, up_parts), [wide, out, up_spec]
    else:
        arrays = (rows, grads, up_parts, down, gain)
        specs = [
            wide,
            wide,
            up_spec,
            pl.BlockSpec((cols, width), lambda i: (0, 0)),
            pl.BlockSpec((1, cols), lambda i: (0, 0)),
        ]
    low = jax.ShapeDtypeStruct((here, cols), BF)
    outs = [jax.ShapeDtypeStruct((here, cols), F32), low, jax.ShapeDtypeStruct((here, 4), F32)]
    out_specs = [out, out, pl.BlockSpec((tile, 4), lambda i: (i, 0))]
    result = pl.pallas_call(
        partial(ffn_in_kernel, given),
        grid=(here // tile,),
        in_specs=specs,
        out_specs=out_specs if given else out_specs + [out],
        out_shape=outs if given else outs + [low],
        compiler_params=params(),
        cost_estimate=cost(
            (2 if given else 4) * here * width * cols,
            4 * here * width + 4 * width * cols + 8 * here * cols,
            2 * here * cols,
        ),
        name="ffn_in",
    )(*arrays)
    return result[0], result[1], scaled if given else result[3], result[2]


def ffn_out_kernel(
    a_ref, p_ref, t_ref, s_ref, g_ref, up_ref, down_ref, sq_ref, hg_ref, m_ref, o_ref, n_ref
):
    parts, _, units = up_ref.shape
    stats = s_ref[...]
    mean, inverse, plain, cross = (stats[:, k : k + 1] for k in range(4))
    normal = (a_ref[...] - mean) * inverse
    scaled = t_ref[...].astype(F32)
    squeezed = (normal * g_ref[...]).astype(BF)
    sq_ref[...] = squeezed
    grad = (p_ref[...].astype(F32) * (inverse * (scaled - plain - normal * cross))).astype(BF)
    hg_ref[...] = grad
    total = dot(grad[:, :units], up_ref[0], NT)
    for k in range(1, parts):
        total = total + dot(grad[:, k * units : (k + 1) * units], up_ref[k], NT)
    m_ref[...] = total.astype(BF)
    o_ref[...] = dot(squeezed, down_ref[...], NN).astype(BF)
    part = jnp.sum(scaled * normal, axis=0, keepdims=True)

    @pl.when(pl.program_id(0) == 0)
    def _():
        n_ref[...] = part

    @pl.when(pl.program_id(0) > 0)
    def _():
        n_ref[...] += part


def ffn_out(held, stats, gain, up_parts, down, offset):
    activated, slope, scaled = held
    here, cols = activated.shape
    width = down.shape[1]
    tile = 256
    shift = offset // tile
    out = pl.BlockSpec((tile, cols), lambda i: (i, 0))
    wide = pl.BlockSpec((tile, width), lambda i: (i, 0))
    return pl.pallas_call(
        ffn_out_kernel,
        grid=(here // tile,),
        in_specs=[
            out,
            out,
            out,
            pl.BlockSpec((tile, 4), lambda i: (i + shift, 0)),
            pl.BlockSpec((1, cols), lambda i: (0, 0)),
            pl.BlockSpec(up_parts.shape, lambda i: (0, 0, 0)),
            pl.BlockSpec((cols, width), lambda i: (0, 0)),
        ],
        out_specs=[out, out, wide, wide, pl.BlockSpec((1, cols), lambda i: (0, 0))],
        out_shape=[
            jax.ShapeDtypeStruct((here, cols), BF),
            jax.ShapeDtypeStruct((here, cols), BF),
            jax.ShapeDtypeStruct((here, width), BF),
            jax.ShapeDtypeStruct((here, width), BF),
            jax.ShapeDtypeStruct((1, cols), F32),
        ],
        compiler_params=params(),
        cost_estimate=cost(
            4 * here * width * cols, 12 * here * cols + 4 * width * cols + 4 * here * width
        ),
        name="ffn_out",
    )(activated, slope, scaled, stats, gain, up_parts, down)


def multiply_kernel(x_ref, w_ref, o_ref):
    o_ref[...] = dot(x_ref[...], w_ref[...], NN).astype(BF)


def multiply(rows, weights, offset, here):
    depth, width = weights.shape
    tile = 256
    shift = offset // tile
    return pl.pallas_call(
        multiply_kernel,
        grid=(here // tile,),
        in_specs=[
            pl.BlockSpec((tile, depth), lambda i: (i + shift, 0)),
            pl.BlockSpec((depth, width), lambda i: (0, 0)),
        ],
        out_specs=pl.BlockSpec((tile, width), lambda i: (i, 0)),
        out_shape=jax.ShapeDtypeStruct((here, width), BF),
        compiler_params=params(),
        cost_estimate=cost(2 * here * width * depth, 2 * (here * width + here * depth + depth * width)),
        name="multiply",
    )(rows, weights)


def grads_kernel(weighted, *refs):
    outs = 2 if weighted else 1
    ins = refs[:-outs]
    parts = len(ins) // 2
    total = dot(ins[0][...], ins[parts][...], TN)
    for k in range(1, parts):
        total = total + dot(ins[k][...], ins[parts + k][...], TN)
    refs[-outs][...] = total.astype(BF)
    if weighted:
        refs[-1][...] = jnp.sum(total * ins[-1][...].astype(F32), axis=0, keepdims=True)


def weight_grad(lefts, rights, offsets, weights=None):
    cols, width, here = lefts[0].shape[1], rights[0].shape[1], rights[0].shape[0]
    tile = 512
    count = len(lefts)

    def left_spec(offset):
        return pl.BlockSpec((here, cols), lambda i: (offset // here, 0))

    out_specs = [pl.BlockSpec((cols, tile), lambda i: (0, i))]
    out_shape = [jax.ShapeDtypeStruct((cols, width), BF)]
    extra, extra_specs = (), []
    if weights is not None:
        out_specs.append(pl.BlockSpec((1, tile), lambda i: (0, i)))
        out_shape.append(jax.ShapeDtypeStruct((1, width), F32))
        extra, extra_specs = (weights,), [pl.BlockSpec((cols, tile), lambda i: (0, i))]
    return pl.pallas_call(
        partial(grads_kernel, weights is not None),
        grid=(width // tile,),
        in_specs=[left_spec(offset) for offset in offsets]
        + [pl.BlockSpec((here, tile), lambda i: (0, i))] * count
        + extra_specs,
        out_specs=out_specs,
        out_shape=out_shape,
        compiler_params=params(),
        cost_estimate=cost(
            2 * count * here * width * cols, 2 * (count * here * (width + cols) + cols * width)
        ),
        name="weight_grad",
    )(*lefts, *rights, *extra)


def head_mask(shape, head, heads, turned):
    lane = lax.broadcasted_iota(jnp.int32, shape, 1)
    if turned:
        return (lane // HALF) % heads == head
    return lane // HEAD_DIM == head


def attend_kernel(first, q_ref, k_ref, v_ref, start_ref, o_ref, low_ref, lse_ref, scores, vcat):
    i = pl.program_id(0)
    rows, cols = q_ref.shape
    heads = cols // HEAD_DIM
    blocks = k_ref.shape[0] // rows

    @pl.when(i == 0)
    def _():
        for b in range(blocks):
            value = v_ref[b * rows : (b + 1) * rows, :]
            for h in range(heads):
                vcat[b, h * rows : (h + 1) * rows, :] = jnp.where(
                    head_mask((rows, cols), h, heads, False), value, jnp.zeros_like(value)
                )

    query = q_ref[...]
    parts = [
        jnp.where(head_mask((rows, cols), h, heads, True), query, jnp.zeros_like(query))
        for h in range(heads)
    ]
    start = start_ref[...]
    low = first[i]
    place = i * rows + lax.broadcasted_iota(jnp.int32, (rows, rows), 0)
    lane = lax.broadcasted_iota(jnp.int32, (rows, rows), 1)

    def score_block(j, tops):
        column = j * rows + lane
        keep = (column <= place) & (column >= start)
        key = k_ref[pl.ds(pl.multiple_of(j * rows, rows), rows), :]
        new = []
        for h in range(heads):
            score = jnp.where(keep, dot(parts[h], key, NT), MASKED_SCORE)
            scores[j, h] = score
            new.append(jnp.maximum(tops[h], jnp.max(score, axis=1, keepdims=True)))
        return tuple(new)

    tops = lax.fori_loop(
        low, i + 1, score_block, tuple(jnp.full((rows, 1), MASKED_SCORE, F32) for _ in range(heads))
    )

    def value_block(j, carry):
        sums, total = carry
        chances, new = [], []
        for h in range(heads):
            chance = jnp.exp(scores[j, h] - tops[h])
            new.append(sums[h] + jnp.sum(chance, axis=1, keepdims=True))
            chances.append(chance.astype(BF))
        total = total + dot(jnp.concatenate(chances, axis=1), vcat[j], NN)
        return tuple(new), total

    sums, total = lax.fori_loop(
        low,
        i + 1,
        value_block,
        (tuple(jnp.zeros((rows, 1), F32) for _ in range(heads)), jnp.zeros((rows, cols), F32)),
    )
    scale = jnp.zeros((rows, cols), F32)
    for h in range(heads):
        scale = jnp.where(head_mask((rows, cols), h, heads, False), 1.0 / sums[h], scale)
        lse_ref[:, h : h + 1] = tops[h] + jnp.log(sums[h])
    result = total * scale
    o_ref[...] = result
    low_ref[...] = result.astype(BF)


def attend(first, query, key, value, start_column, count):
    length, cols = query.shape
    heads = cols // HEAD_DIM
    size = length // count
    whole = pl.BlockSpec((length, cols), lambda i, first: (0, 0))
    return pl.pallas_call(
        attend_kernel,
        grid_spec=pltpu.PrefetchScalarGridSpec(
            num_scalar_prefetch=1,
            grid=(size,),
            in_specs=[
                pl.BlockSpec((count, cols), lambda i, first: (i, 0)),
                whole,
                whole,
                pl.BlockSpec((count, 1), lambda i, first: (i, 0)),
            ],
            out_specs=[
                pl.BlockSpec((count, cols), lambda i, first: (i, 0)),
                pl.BlockSpec((count, cols), lambda i, first: (i, 0)),
                pl.BlockSpec((count, heads), lambda i, first: (i, 0)),
            ],
            scratch_shapes=[
                pltpu.VMEM((size, heads, count, count), F32),
                pltpu.VMEM((size, heads * count, cols), BF),
            ],
        ),
        out_shape=[
            jax.ShapeDtypeStruct((length, cols), F32),
            jax.ShapeDtypeStruct((length, cols), BF),
            jax.ShapeDtypeStruct((length, heads), F32),
        ],
        compiler_params=params(),
        cost_estimate=cost(18 * length * length * cols, 10 * length * cols),
        name="attend",
    )(first, query, key, value, start_column)


def attend_back_kernel(
    first, spot, q_ref, k_ref, v_ref, do_ref, lse_ref, delta_ref, start_ref,
    cq_ref, sq_ref, ck_ref, sk_ref, out_ref, kcat, dk_ref, dv_ref,
):
    i = pl.program_id(0)
    rows, cols = q_ref.shape
    half = cols // 2
    heads = cols // HEAD_DIM
    blocks = k_ref.shape[0] // rows

    @pl.when(i == 0)
    def _():
        dk_ref[...] = jnp.zeros_like(dk_ref)
        dv_ref[...] = jnp.zeros_like(dv_ref)
        for b in range(blocks):
            key = k_ref[b * rows : (b + 1) * rows, :]
            for h in range(heads):
                kcat[b, h * rows : (h + 1) * rows, :] = jnp.where(
                    head_mask((rows, cols), h, heads, True), key, jnp.zeros_like(key)
                )

    query, grad = q_ref[...], do_ref[...]
    parts = [
        jnp.where(head_mask((rows, cols), h, heads, True), query, jnp.zeros_like(query))
        for h in range(heads)
    ]
    grads = [
        jnp.where(head_mask((rows, cols), h, heads, False), grad, jnp.zeros_like(grad))
        for h in range(heads)
    ]
    query_stack = jnp.concatenate(parts, axis=0)
    grad_stack = jnp.concatenate(grads, axis=0)
    start = start_ref[...]
    place = i * rows + lax.broadcasted_iota(jnp.int32, (rows, rows), 1)
    line = lax.broadcasted_iota(jnp.int32, (rows, rows), 0)

    def block(j, total):
        where = pl.ds(pl.multiple_of(j * rows, rows), rows)
        column = j * rows + line
        keep = (column <= place) & (column >= start)
        key, value = k_ref[where, :], v_ref[where, :]
        chances, slopes = [], []
        for h in range(heads):
            score = jnp.where(keep, dot(key, parts[h], NT), MASKED_SCORE)
            chance = jnp.exp(score - lse_ref[h : h + 1, :])
            product = dot(value, grads[h], NT)
            slopes.append((chance * (product - delta_ref[h : h + 1, :])).astype(BF))
            chances.append(chance.astype(BF))
        slope = jnp.concatenate(slopes, axis=1)
        dk_ref[where, :] += dot(slope, query_stack, NN)
        dv_ref[where, :] += dot(jnp.concatenate(chances, axis=1), grad_stack, NN)
        return total + dot(jnp.concatenate(slopes, axis=0), kcat[j], TN)

    total = lax.fori_loop(first[i], i + 1, block, jnp.zeros((rows, cols), F32))
    here = pl.ds(pl.multiple_of(i * rows, rows), rows)
    target = pl.ds(pl.multiple_of(spot[i] * rows, rows), rows)
    cq, sq = cq_ref[here, :], sq_ref[here, :]
    d1, d2 = total[:, :half], total[:, half:]
    out_ref[target, :half] = (d1 * cq + d2 * sq).astype(BF)
    out_ref[target, half:cols] = (d2 * cq - d1 * sq).astype(BF)

    @pl.when(i == pl.num_programs(0) - 1)
    def _():
        def finish(j, carry):
            where = pl.ds(pl.multiple_of(j * rows, rows), rows)
            goal = pl.ds(pl.multiple_of(spot[j] * rows, rows), rows)
            ck, sk = ck_ref[where, :], sk_ref[where, :]
            k1, k2 = dk_ref[where, :half], dk_ref[where, half:]
            out_ref[goal, cols : cols + half] = (k1 * ck + k2 * sk).astype(BF)
            out_ref[goal, cols + half : 2 * cols] = (k2 * ck - k1 * sk).astype(BF)
            out_ref[goal, 2 * cols :] = dv_ref[where, :].astype(BF)
            return carry

        lax.fori_loop(0, blocks, finish, 0)


def attend_back(first, spot, query, key, value, grad, lse, delta, start_row, tables, count):
    length, cols = query.shape
    heads = cols // HEAD_DIM
    size = length // count
    whole = pl.BlockSpec((length, cols), lambda i, *_: (0, 0))
    table = pl.BlockSpec((length, cols // 2), lambda i, *_: (0, 0))
    rows = pl.BlockSpec((count, cols), lambda i, *_: (i, 0))
    line = pl.BlockSpec((pl.squeezed, heads, count), lambda i, *_: (i, 0, 0))
    return pl.pallas_call(
        attend_back_kernel,
        grid_spec=pltpu.PrefetchScalarGridSpec(
            num_scalar_prefetch=2,
            grid=(size,),
            in_specs=[
                rows,
                whole,
                whole,
                rows,
                line,
                line,
                pl.BlockSpec((pl.squeezed, 1, count), lambda i, *_: (i, 0, 0)),
                table,
                table,
                table,
                table,
            ],
            out_specs=pl.BlockSpec((length, 3 * cols), lambda i, *_: (0, 0)),
            scratch_shapes=[
                pltpu.VMEM((size, heads * count, cols), BF),
                pltpu.VMEM((length, cols), F32),
                pltpu.VMEM((length, cols), F32),
            ],
        ),
        out_shape=jax.ShapeDtypeStruct((length, 3 * cols), BF),
        compiler_params=params(),
        cost_estimate=cost(24 * length * length * cols, 20 * length * cols),
        name="attend_back",
    )(first, spot, query, key, value, grad, lse, delta, start_row, *tables)


def xpos_tables(heads, scale, positions):
    pair_index = (jnp.arange(HALF * heads) % HALF).astype(F32)
    frequency = 10000.0 ** (-pair_index / HALF)
    angles = positions[:, None] * frequency[None, :]
    zeta_base = (pair_index / HALF + 0.4) / 1.4
    growth = zeta_base[None, :] ** ((positions[:, None] - SEQ_LEN // 2) / SCALE_BASE)
    cosine, sine = jnp.cos(angles), jnp.sin(angles)
    return cosine * growth * scale, sine * growth * scale, cosine / growth, sine / growth


def on_device(
    layer_input,
    segment_ids,
    cotangent,
    projections,
    output_weight,
    up_weight,
    down_weight,
    norm_gains,
    hidden_gain,
    decays,
    average_projections,
    average_output,
    average_up,
    average_down,
    average_gains,
    average_hidden,
):
    size = lax.axis_size("seq")
    groups = lax.axis_size("tensor")
    me = lax.axis_index("seq")
    group = lax.axis_index("tensor")
    chunks, count, width = layer_input.shape
    length = segment_ids.shape[1]
    block_cols = projections.shape[2]
    heads = width // HEAD_DIM
    per_block = block_cols // HEAD_DIM
    mine = heads // size
    cols = mine * HEAD_DIM
    even_split = per_block % size == 0
    units = up_weight.shape[1] // size
    hidden_cols = units * groups
    hidden_total = hidden_cols * size

    each = per_block // size if even_split else 0
    split = each * HEAD_DIM

    def to_order(rows):
        if not even_split:
            return rows
        shaped = rows.reshape((groups, size, split) + rows.shape[1:])
        return jnp.swapaxes(shaped, 0, 1).reshape(rows.shape)

    def from_order(rows):
        if not even_split:
            return rows
        shaped = rows.reshape((size, groups, split) + rows.shape[1:])
        return jnp.swapaxes(shaped, 0, 1).reshape(rows.shape)

    line = Line()
    masks = np.concatenate([np.arange(0, size, 2), np.arange(1, size, 2)]).astype(np.int32)
    place = (jnp.asarray(masks) ^ me).astype(jnp.int32)
    middle = length // 2
    halves = (0, 1)

    gains_all = lax.all_gather(norm_gains, "seq", axis=1, tiled=True).astype(F32)
    gain_attn, gain_ffn = gains_all[0], gains_all[2][None]
    gain_inner = to_order(gains_all[1]).reshape(size, 1, cols)
    inputs = [layer_input[c].astype(F32) for c in range(chunks)]
    normed = [row_norm(rows) for rows in inputs]
    sent_in = [(normed[c][0] * gain_attn).astype(BF) for c in range(chunks)]

    turned = projections.transpose(1, 2, 0)
    if even_split:
        sent = turned.reshape(3, size, split, count).transpose(1, 0, 2, 3)
        came = lax.all_to_all(sent, "seq", 0, 0, tiled=True)
        raw = lax.all_gather(came, "tensor", axis=0, tiled=False)
    else:
        wide = lax.all_gather(turned, "tensor", axis=1, tiled=True)
        sent = wide.reshape(3, size, cols, count).transpose(1, 0, 2, 3)
        came = lax.all_to_all(sent, "seq", 0, 0, tiled=True)
        raw = came[None]
    proj, proj_plain = arrange(raw)
    tall = lax.all_gather(after(output_weight, came), "tensor", axis=0, tiled=True)

    def swapped(kind):
        if kind == "up":
            sent = line.put(up_weight).reshape(count, size, units).transpose(1, 0, 2)
            return lax.all_to_all(sent, "seq", 0, 0, tiled=True).reshape(width, units)
        sent = line.put(down_weight).reshape(size, units, count)
        came = lax.all_to_all(sent, "seq", 0, 0, tiled=True)
        return came.transpose(1, 0, 2).reshape(units, width)

    gain_hidden = jnp.zeros((groups, units), BF)
    for k in range(groups):
        part = hidden_gain
        if k:
            part = lax.ppermute(part, "tensor", [(i, (i - k) % groups) for i in range(groups)])
        gain_hidden = lax.dynamic_update_slice(
            gain_hidden, part.reshape(1, units), ((group + k) % groups, 0)
        )
    gain_hidden = gain_hidden.astype(F32).reshape(1, hidden_cols)

    blocks = jnp.arange(size, dtype=jnp.int32) ^ me
    spot = (blocks & 1) * (size // 2) + (blocks >> 1)
    segments = lax.dynamic_slice_in_dim(segment_ids, group * chunks, chunks, 0)
    starts = jnp.sum((segments[:, None, :] < segments[:, :, None]).astype(jnp.int32), axis=2)
    firsts = starts.reshape(chunks, size, count)[:, :, 0] // count

    rows_of = {}

    def projected(c, h):
        before = rows_of.get(c) or [jnp.zeros((length, cols), BF) for _ in range(3)]
        rows_of[c] = project(
            line.enter(place[h * (size // 2) : (h + 1) * (size // 2)]),
            ins[c].halves[h],
            proj_plain,
            tables_turn,
            count,
            before,
        )
        line.mark(rows_of[c][0])

    def attention(c):
        attended, low, lse = attend(
            line.enter(firsts[c]), *rows_of[c], starts[c][:, None], count
        )
        line.mark(lse)
        came = lax.all_to_all(low.reshape(size, count, cols), "seq", 0, 0, tiled=True)
        return rows_of[c], attended, lse, came

    def mixed(c):
        result = out_project(
            line.enter(place),
            kept[c][3],
            pieces.halves,
            layer_input[c],
            gain_inner,
            gain_ffn,
            split,
        )
        line.mark(result[1])
        return result

    ins = [Gather(line, sent_in[0])]
    line.mark(ins[0].pieces[-1])
    ins[0].corner()
    ins.append(Gather(line, sent_in[1]))
    came_up = swapped("up")
    line.note(gain_hidden)
    turn = line.enter(jnp.arange(SEQ_LEN, dtype=F32))
    tables_turn = xpos_tables(mine, FACTOR, turn)
    line.mark(tables_turn[0])
    ins[0].core()
    line.note(came_up)
    came_down = swapped("down")
    up_parts = lax.all_gather(after(came_up, tall), "tensor", axis=0, tiled=False)
    proj, proj_plain = arrange(line.enter(raw))
    line.mark(proj)
    ins[1].corner()
    line.note(came_down)
    projected(0, 0)
    pieces = Gather(line, tall)
    projected(0, 1)
    ins[1].core()
    down = lax.all_gather(line.put(came_down), "tensor", axis=0, tiled=True)
    kept = [attention(0)]
    pieces.corner()
    cots = [Gather(line, cotangent[0])]
    projected(1, 0)
    projected(1, 1)
    pieces.core()
    kept.append(attention(1))
    cots[0].corner()
    line.note(kept[0][3])
    outs = [mixed(0)]
    cots[0].core()
    mids = [Gather(line, outs[0][2])]
    line.note(kept[1][3])
    outs.append(mixed(1))
    cots.append(Gather(line, cotangent[1]))

    def graded(c, h):
        scaled = ffn_grad(cots[c].halves[h], down, line.enter(gain_hidden))
        line.mark(scaled)
        return scaled

    def entered(c, h, scaled=None):
        if scaled is None:
            result = ffn_in(
                mids[c].halves[h], up_parts, None, cots[c].halves[h], down, line.enter(gain_hidden)
            )
        else:
            result = ffn_in(mids[c].halves[h], up_parts, line.enter(scaled))
        line.mark(result[3])
        return result

    def summed(held):
        stats = jnp.concatenate([held[h][3] for h in halves]).reshape(size, count, 4)
        return BlockSum(line, stats.transpose(0, 2, 1))

    def row_stats(sums):
        stats = sums.total() / hidden_total
        mean, second, plain, cross = (stats[:, k] for k in range(4))
        inverse = lax.rsqrt(second - mean * mean + EPSILON)
        cross = inverse * (cross - mean * plain)
        return jnp.stack([mean, inverse, plain, cross], axis=-1).reshape(length, 4)

    def left(c, h):
        result = ffn_out(
            held[c][h][:3], stats[c], line.enter(gain_hidden), up_parts, down, h * middle
        )
        line.mark(result[4])
        return result

    scaled0 = [graded(0, 0)]
    mids[0].corner()
    mids.append(Gather(line, outs[1][2]))
    scaled0.append(graded(0, 1))
    mids[0].core()
    cots[1].corner()
    held = [[entered(0, 0, scaled0[0])]]
    cots[1].core()
    mids[1].corner()
    held[0].append(entered(0, 1, scaled0[1]))
    mids[1].core()
    sums = [summed(held[0])]
    held.append([entered(1, 0)])
    sums[0].more()
    held[1].append(entered(1, 1))
    sums[0].more()
    sums.append(summed(held[1]))
    stats = [row_stats(sums[0])]
    done = [[None, None] for _ in range(chunks)]
    done[0][1] = left(0, 1)
    sums[1].more()
    mid_sums = [Scatter(line, done[0][1][2], count)]
    done[0][0] = left(0, 0)
    mid_sums[0].corner(done[0][0][2])
    sums[1].more()
    stats.append(row_stats(sums[1]))
    done[1][1] = left(1, 1)
    mid_sums[0].near()
    mid_sums.append(Scatter(line, done[1][1][2], count))
    done[1][0] = left(1, 0)
    mid_sums[1].corner(done[1][0][2])
    out_sums = [Scatter(line, done[0][1][3], count)]
    hidden_gain_grad = sum(done[c][h][4] for c in range(chunks) for h in halves)
    hidden_gain_grad = (hidden_gain_grad / gain_hidden).reshape(groups, units)
    down_grad = weight_grad(
        [line.enter(done[c][h][0]) for c in range(chunks) for h in halves],
        [cots[c].halves[h] for c in range(chunks) for h in halves],
        [0] * 4,
    )[0]
    line.mark(down_grad)
    scatter = partial(lax.psum_scatter, axis_name="tensor", scatter_dimension=0, tiled=True)
    down_own = scatter(down_grad)

    def back_out(c):
        residual_grad, attn_grad, sent, ffn_gain, inner_gain = out_back(
            line.enter(place),
            mid_sums[c].total(),
            outs[c][1],
            cotangent[c],
            kept[c][3],
            pieces.halves,
            gain_inner,
            gain_ffn,
            split,
        )
        line.mark(sent)
        grad = lax.all_to_all(sent, "seq", 0, 0, tiled=True).reshape(length, cols)
        return residual_grad, attn_grad, grad, ffn_gain[0], inner_gain.reshape(width)

    def back_attention(c):
        turned_rows, attended, lse, came = kept[c]
        grad = backs[c][2]
        delta = jnp.sum((grad.astype(F32) * attended).reshape(length, mine, HEAD_DIM), axis=2)
        slope = attend_back(
            line.enter(firsts[c]),
            spot,
            *turned_rows,
            grad,
            lse.reshape(size, count, mine).transpose(0, 2, 1),
            delta.reshape(size, count, mine).transpose(0, 2, 1),
            starts[c].reshape(size, 1, count),
            tables_turn,
            count,
        )
        line.mark(slope)
        return slope

    def times(rows, weights, offset):
        result = multiply(line.enter(rows), weights, offset, middle)
        line.mark(result)
        return result

    mid_sums[1].near()
    backs = [back_out(0)]
    out_sums[0].corner(done[0][0][3])
    out_sums.append(Scatter(line, done[1][1][3], count))
    up_grad = weight_grad(
        [line.enter(done[c][h][1]) for c in range(chunks) for h in halves],
        [mids[c].halves[h] for c in range(chunks) for h in halves],
        [0] * 4,
    )[0]
    line.mark(up_grad)
    up_own = scatter(up_grad)
    out_sums[0].near()
    backs.append(back_out(1))
    line.note(backs[0][2])
    output_grad = out_grad(
        [line.enter(outs[c][0]) for c in range(chunks)], [back[1] for back in backs], split
    )
    line.mark(output_grad)
    output_own = scatter(
        lax.psum_scatter(output_grad, "seq", scatter_dimension=0, tiled=True).reshape(width, count)
    )
    out_sums[1].corner(done[1][0][3])
    slopes = [back_attention(0)]
    out_sums[1].near()
    line.note(down_own, backs[1][2])
    odd = times(slopes[0], proj, middle)
    in_sums = [Scatter(line, odd, count)]
    even = times(slopes[0], proj, 0)
    in_sums[0].corner(even)
    slopes.append(back_attention(1))
    in_sums[0].near()
    line.note(up_own)
    odd = times(slopes[1], proj, middle)
    in_sums.append(Scatter(line, odd, count))
    even = times(slopes[1], proj, 0)
    in_sums[1].corner(even)
    proj_grad, attn_gain = weight_grad(
        [line.enter(slopes[c]) for c in range(chunks) for h in halves],
        [ins[c].halves[h] for c in range(chunks) for h in halves],
        [h * middle for c in range(chunks) for h in halves],
        proj,
    )
    line.mark(proj_grad)
    in_sums[1].near()

    outputs = [outs[c][1] + out_sums[c].total() for c in range(chunks)]
    input_grads = [
        backs[c][0] + row_norm_back(in_sums[c].total() * gain_attn, *normed[c])
        for c in range(chunks)
    ]
    gain_terms = jnp.stack(
        [
            attn_gain[0] / gain_attn,
            from_order(sum(back[4] for back in backs)),
            sum(back[3] for back in backs),
        ]
    )
    gains_grad = lax.psum(
        lax.psum_scatter(gain_terms, "seq", scatter_dimension=1, tiled=True), "tensor"
    )

    part = down_own.reshape(units, size, count).transpose(1, 0, 2)
    down_final = lax.all_to_all(part, "seq", 0, 0, tiled=True).reshape(size * units, count)
    part = up_own.reshape(units, size, count).transpose(1, 0, 2)
    part = lax.all_to_all(part, "seq", 0, 0, tiled=True)
    up_final = part.transpose(2, 0, 1).reshape(count, size * units)
    output_final = output_own
    part = proj_grad
    turned_heads = part[: 2 * cols].reshape(2, 2, mine, HALF, width).transpose(0, 2, 1, 3, 4)
    part = jnp.concatenate([turned_heads.reshape(2, cols, width), part[None, 2 * cols :]])
    if even_split:
        part = part.reshape(3, groups, split, width).transpose(1, 0, 2, 3)
        part = scatter(part.reshape(3 * cols, width))
        part = part.reshape(3, split, size, count).transpose(2, 0, 1, 3)
        part = lax.all_to_all(part, "seq", 0, 0, tiled=True)
        proj_final = part.transpose(3, 1, 0, 2).reshape(count, 3, block_cols)
    else:
        part = lax.psum(part, "tensor").reshape(3, cols, size, count).transpose(2, 0, 1, 3)
        part = lax.all_to_all(part, "seq", 0, 0, tiled=True)
        part = part.transpose(3, 1, 0, 2).reshape(count, 3, width)
        proj_final = lax.dynamic_slice_in_dim(part, group * block_cols, block_cols, 2)
    hidden_final = lax.psum_scatter(
        hidden_gain_grad, "tensor", scatter_dimension=0, tiled=True
    )

    grads = (
        proj_final.astype(F32),
        output_final.astype(F32),
        up_final.astype(F32),
        down_final.astype(F32),
        gains_grad.astype(F32),
        hidden_final.astype(F32),
    )
    averages = (
        average_projections,
        average_output,
        average_up,
        average_down,
        average_gains,
        average_hidden,
    )
    updated = tuple(
        decays[i] * averages[i] + (1.0 - decays[i]) * grads[i] for i in range(6)
    )
    return (jnp.stack(outputs).astype(BF), jnp.stack(input_grads)) + grads + updated


def solution(mesh):
    weights = (P("seq", None, "tensor"), P("tensor", "seq"), P("seq", "tensor"), P("tensor", "seq"))
    gains = (P(None, "seq"), P("tensor", "seq"))
    rows = P("tensor", "seq", None)
    return jax.shard_map(
        on_device,
        mesh=mesh,
        in_specs=(rows, P(), rows) + weights + gains + (P(),) + weights + gains,
        out_specs=(rows, rows) + weights + gains + weights + gains,
        check_vma=False,
    )
```

time: 1350 us -> 1100 us (0.81)
  Pallas kernels: 128 us -> 484 us
  matrix products: 312 us -> 0 us
  local copies, waits for them, and re-layouts: 255 us -> 90.6 us
  waiting for transfers between devices: 332 us -> 232 us
  blocking collectives: 65.1 us -> 36.3 us
  other arithmetic: 132 us -> 111 us
  starting transfers between devices: 92.1 us -> 113 us
    pallas_call x0 -> x30, Pallas kernels: none -> 340 us  [the longest x4 71.1 us: ffn_out(): pl.pallas_call(ffn_out_kernel, grid=(here // tile,), in_specs=[out, out,...]
    dot_general x28 -> x0, matrix products: 312 us -> none  [dot(): return lax.dot_general(a, b, (dims, ((), ())), preferred_element_type=F32)]
    ppermute x66 -> x71, waiting for transfers between devices: 246 us -> 161 us  [swap(): return lax.ppermute(block, 'seq', [(i, i ^ bit) for i in range(size)])]
    unnamed x258 -> x187, local copies, waits for them, and re-layouts: 81 us -> 31.3 us
    unnamed x12 -> x11, waiting for transfers between devices: 46.7 us -> 0.17 us
    concatenate x12 -> x0, local copies, waits for them, and re-layouts: 40 us -> none  [the longest x2 12.7 us: on_device(): jnp.concatenate(gather_rows((normed_mid[c][0] * gain_ffn).astype(BF)))]
    reduce_sum x7 -> x3, other arithmetic: 45.6 us -> 10.2 us  [the longest x1 5.42 us: row_norm_back(): jnp.mean(scaled, axis=-1, keepdims=True)]
    slice x37 -> x24, local copies, waits for them, and re-layouts: 42.8 us -> 15 us  [the longest x7 7.3 us: corner(): across = self.line.put(self.pieces[1])[:half]]
  transfers between devices with their start and end apart: 86 -> 94, of which waited for: 30 -> 41; matrix products, arithmetic and copies ran while one was open for 41% -> 15% of each run, Pallas kernels for 10% -> 39%
where the time goes in v2:
time: 1100 us; the launch traced here: 1090 us
  Pallas kernels  484 us (44%)
  waiting for transfers between devices  232 us (21%)
  starting transfers between devices  113 us (10%)
  other arithmetic  111 us (10%)
  local copies, waits for them, and re-layouts  90.6 us (8%)
  blocking collectives  36.3 us (3%)
  between operations  19.8 us (2%)
    ppermute x71, waiting for transfers between devices, swap(): return lax.ppermute(block, 'seq', [(i, i ^ bit) for i in range(size)])  161 us
    pallas_call x4, Pallas kernels, ffn_out(): pl.pallas_call(ffn_out_kernel, grid=(here // tile,), in_specs=[out, out,...  71.1 us
    pallas_call x3, Pallas kernels, weight_grad(): pl.pallas_call(partial(grads_kernel, weights is not None), grid=(width //...  68.4 us
    ppermute x71, starting transfers between devices, swap(): return lax.ppermute(block, 'seq', [(i, i ^ bit) for i in range(size)])  68.1 us
    pallas_call x2, Pallas kernels, attend_back(): pl.pallas_call(attend_back_kernel, grid_spec=pltpu.PrefetchScalarGridSpec...  59.9 us
    pallas_call x4, Pallas kernels, ffn_in(): pl.pallas_call(partial(ffn_in_kernel, given), grid=(here // tile,), in_sp...  55.7 us
    pallas_call x2, Pallas kernels, attend(): pl.pallas_call(attend_kernel, grid_spec=pltpu.PrefetchScalarGridSpec(num_...  49.7 us
    pallas_call x4, Pallas kernels, project(): pl.pallas_call(qkv_kernel, grid_spec=pltpu.PrefetchScalarGridSpec(num_sca...  34.5 us
  transfers between devices with their start and end apart: 94, of which 41 were waited for; matrix products, arithmetic and copies ran while one was open for 15% of the time, Pallas kernels for 39%

profile of v2, /device:TPU:0, one launch (start us, length us, event | category | flops | bytes accessed | tf_op | source)
XLA Modules:
  0.0 1087.4 jit_solution(13228433440702294139)
XLA Ops:
  9.7 5.3 all-to-all-start
  15.8 14.8 %all_gather.23 = bf16[3,2048]{1,0:T(4,128)(2,1)S(1)} all-gather(bf16[3,256]{1,0:T(4,128)(2,1)S(1)} %copy-done.77), channel_id=1, replica_groups=mesh['seq'=8,'tensor'=4] {'seq'}, dimensions={1}, use_global_device_ids=true | all-gather | bytes 13824 | tf_op jit(solution)/shard_map/all_gather | solution.py:1069
  45.7 13.8 %collective-permute-done.refs_2_ = bf16[256,2048]{1,0:T(8,128)(2,1)} collective-permute-done((bf16[256,2048]{1,0:T(8,128)(2,1)S(1)}, bf16[256,2048]{1,0:T(8,128)(2,1)}, u32[]{:S(2)}, u32[]{:S(2)}) %collective-permute-start) | collective-permute-done | bytes 1048608 | tf_op jit(solution)/shard_map/ppermute | solution.py:26
  64.0 8.3 power_multiply_fusion
  90.2 12.4 %all-to-all-done.1 = bf16[8,256,256]{2,1,0:T(8,128)(2,1)S(1)} async-done(((bf16[8,256,256]{2,1,0:T(8,128)(2,1)}), bf16[8,256,256]{2,1,0:T(8,128)(2,1)S(1)}, u32[]{:S(2)}, u32[]{:S(2)}) %all-to-all-start.1) | async-done | bytes 1048608 | tf_op jit(solution)/shard_map/all_to_all | solution.py:1092
  102.7 4.2 all-to-all-start.2
  107.0 5.4 arrange.1
  112.4 11.8 %collective-permute-done.8.refs_2_ = bf16[256,2048]{1,0:T(8,128)(2,1)} collective-permute-done((bf16[256,2048]{1,0:T(8,128)(2,1)}, bf16[256,2048]{1,0:T(8,128)(2,1)}, u32[]{:S(2)}, u32[]{:S(2)}) %collective-permute-start.8) | collective-permute-done | bytes 1048608 | tf_op jit(solution)/shard_map/ppermute | solution.py:26
  130.7 5.9 all-to-all-done.2
  142.1 8.8 project.4
  150.9 8.6 project.5
  164.5 3.9 convert_reduce_fusion
  172.3 26.3 %attend.2 = (f32[2048,256]{1,0:T(8,128)}, bf16[2048,256]{1,0:T(8,128)(2,1)}, f32[2048,4]{1,0:T(8,128)}) custom-call(s32[8]{0:T(128)} %get-tuple-element.328.first, bf16[2048,256]{1,0:T(8,128)(2,1)} %get-tuple-element.203.q_ref, bf16[2048,256]{1,0:T(8,128)(2,1)} %get-tuple-element.206.k_ref, bf16[2048,256]{1,0:T(8,128)(2,1)} %get-tuple-element.207.v_ref, ...), custom_call_target="tpu_custom_call" | custom-call | flops 6442450944 | bytes 1747626 | tf_op jit(solution)/shard_map/attend/pallas_call | solution.py:856
  208.0 8.6 project.6
  216.6 8.6 project.7
  233.5 3.7 all-to-all-start.3
  237.2 23.3 %attend.3 = (f32[2048,256]{1,0:T(8,128)}, bf16[2048,256]{1,0:T(8,128)(2,1)}, f32[2048,4]{1,0:T(8,128)}) custom-call(s32[8]{0:T(128)} %get-tuple-element.336.first, bf16[2048,256]{1,0:T(8,128)(2,1)} %get-tuple-element.217.q_ref, bf16[2048,256]{1,0:T(8,128)(2,1)} %get-tuple-element.220.k_ref, bf16[2048,256]{1,0:T(8,128)(2,1)} %get-tuple-element.221.v_ref, ...), custom_call_target="tpu_custom_call" | custom-call | flops 6442450944 | bytes 1747626 | tf_op jit(solution)/shard_map/attend/pallas_call | solution.py:856
  270.2 13.0 %out_project.2 = (bf16[8,256,256]{2,1,0:T(8,128)(2,1)}, f32[256,2048]{1,0:T(8,128)}, bf16[256,2048]{1,0:T(8,128)(2,1)}) custom-call(s32[8]{0:T(128)} %copy-done.56, bf16[8,256,256]{2,1,0:T(8,128)(2,1)} %copy-done.6, bf16[4,4,8,64,256]{4,3,2,1,0:T(8,128)(2,1)} %bitcast.213, bf16[4,4,8,64,256]{4,3,2,1,0:T(8,128)(2,1)} %bitcast.21.odd_ref, ...), custom_call_target="tpu_custom_call" | custom-call | flops 715827904 | bytes 4893354 | tf_op jit(solution)/shard_map/out_project/pallas_call | solution.py:436
  293.5 12.4 %all-to-all-done.4.came_ref = bf16[8,256,256]{2,1,0:T(8,128)(2,1)S(1)} async-done(((bf16[8,256,256]{2,1,0:T(8,128)(2,1)}), bf16[8,256,256]{2,1,0:T(8,128)(2,1)S(1)}, u32[]{:S(2)}, u32[]{:S(2)}) %all-to-all-start.4) | async-done | bytes 1048608 | tf_op jit(solution)/shard_map/all_to_all | solution.py:1132
  306.9 13.1 %out_project.3 = (bf16[8,256,256]{2,1,0:T(8,128)(2,1)}, f32[256,2048]{1,0:T(8,128)}, bf16[256,2048]{1,0:T(8,128)(2,1)}) custom-call(s32[8]{0:T(128)} %copy-done.56, bf16[8,256,256]{2,1,0:T(8,128)(2,1)} %copy-done.5, bf16[4,4,8,64,256]{4,3,2,1,0:T(8,128)(2,1)} %bitcast.214, bf16[4,4,8,64,256]{4,3,2,1,0:T(8,128)(2,1)} %bitcast.21.odd_ref, ...), custom_call_target="tpu_custom_call" | custom-call | flops 715827904 | bytes 4893354 | tf_op jit(solution)/shard_map/out_project/pallas_call | solution.py:436
  320.0 8.7 ffn_grad.2.refs_1_.t_ref
  329.9 8.7 ffn_grad.3.refs_1_.t_ref
  350.9 21.9 %collective-permute-done.28.refs_2_ = bf16[256,2048]{1,0:T(8,128)(2,1)S(1)} collective-permute-done((bf16[256,2048]{1,0:T(8,128)(2,1)S(1)}, bf16[256,2048]{1,0:T(8,128)(2,1)S(1)}, u32[]{:S(2)}, u32[]{:S(2)}) %collective-permute-start.28) | collective-permute-done | bytes 1048608 | tf_op jit(solution)/shard_map/ppermute | solution.py:26
  377.7 11.1 %ffn_in.4 = (f32[1024,1024]{1,0:T(8,128)}, bf16[1024,1024]{1,0:T(8,128)(2,1)}, f32[1024,4]{1,0:T(8,128)}) custom-call(bf16[1024,2048]{1,0:T(8,128)(2,1)} %join.11.refs_0_.refs_4_, bf16[1024,1024]{1,0:T(8,128)(2,1)} %ffn_grad.2.refs_1_.t_ref, bf16[4,2048,256]{2,1,0:T(8,128)(2,1)} %bitcast.205), custom_call_target="tpu_custom_call" | custom-call | flops 1431655808 | bytes 8388608 | tf_op jit(solution)/shard_map/ffn_in/pallas_call | solution.py:632
  388.8 6.5 collective-permute-done.33.refs_2_
  398.5 8.4 collective-permute-done.31.refs_4_
  411.2 11.1 %ffn_in.5 = (f32[1024,1024]{1,0:T(8,128)}, bf16[1024,1024]{1,0:T(8,128)(2,1)}, f32[1024,4]{1,0:T(8,128)}) custom-call(bf16[1024,2048]{1,0:T(8,128)(2,1)} %collective-permute-done.29.refs_0_.refs_5_, bf16[1024,1024]{1,0:T(8,128)(2,1)} %ffn_grad.3.refs_1_.t_ref, bf16[4,2048,256]{2,1,0:T(8,128)(2,1)} %bitcast.206), custom_call_target="tpu_custom_call" | custom-call | flops 1431655808 | bytes 8388608 | tf_op jit(solution)/shard_map/ffn_in/pallas_call | solution.py:632
  428.3 16.8 %ffn_in.6 = (f32[1024,1024]{1,0:T(8,128)}, bf16[1024,1024]{1,0:T(8,128)(2,1)}, f32[1024,4]{1,0:T(8,128)}, bf16[1024,1024]{1,0:T(8,128)(2,1)}) custom-call(bf16[1024,2048]{1,0:T(8,128)(2,1)} %join.13.refs_0_.refs_6_, bf16[1024,2048]{1,0:T(8,128)(2,1)} %join.12.refs_1_.refs_6_, bf16[4,2048,256]{2,1,0:T(8,128)(2,1)} %bitcast.207, ...), custom_call_target="tpu_custom_call" | custom-call | flops 2863311616 | bytes 8388608 | tf_op jit(solution)/shard_map/ffn_in/pallas_call | solution.py:632
  447.5 16.7 %ffn_in.7 = (f32[1024,1024]{1,0:T(8,128)}, bf16[1024,1024]{1,0:T(8,128)(2,1)}, f32[1024,4]{1,0:T(8,128)}, bf16[1024,1024]{1,0:T(8,128)(2,1)}) custom-call(bf16[1024,2048]{1,0:T(8,128)(2,1)} %collective-permute-done.38.refs_0_.refs_7_, bf16[1024,2048]{1,0:T(8,128)(2,1)} %collective-permute-done.39.refs_1_.refs_7_, bf16[4,2048,256]{2,1,0:T(8,128)(2,1)} %bitcast.208, ...), custom_call_target="tpu_custom_call" | custom-call | flops 2863311616 | bytes 8388608 | tf_op jit(solution)/shard_map/ffn_in/pallas_call | solution.py:632
  471.0 17.6 %ffn_out.4 = (bf16[1024,1024]{1,0:T(8,128)(2,1)}, bf16[1024,1024]{1,0:T(8,128)(2,1)}, bf16[1024,2048]{1,0:T(8,128)(2,1)}, bf16[1024,2048]{1,0:T(8,128)(2,1)}, f32[1,1024]{1,0:T(1,128)}) custom-call(f32[1024,1024]{1,0:T(8,128)} %get-tuple-element.264.a_ref, bf16[1024,1024]{1,0:T(8,128)(2,1)} %get-tuple-element.265.p_ref, ...), custom_call_target="tpu_custom_call" | custom-call | flops 2863311616 | bytes 9786709 | tf_op jit(solution)/shard_map/ffn_out/pallas_call | solution.py:685
  489.2 5.4 collective-permute-done.41
  495.8 18.0 %ffn_out.5 = (bf16[1024,1024]{1,0:T(8,128)(2,1)}, bf16[1024,1024]{1,0:T(8,128)(2,1)}, bf16[1024,2048]{1,0:T(8,128)(2,1)}, bf16[1024,2048]{1,0:T(8,128)(2,1)}, f32[1,1024]{1,0:T(1,128)}) custom-call(f32[1024,1024]{1,0:T(8,128)} %get-tuple-element.247.a_ref, bf16[1024,1024]{1,0:T(8,128)(2,1)} %get-tuple-element.248.p_ref, ...), custom_call_target="tpu_custom_call" | custom-call | flops 2863311616 | bytes 9786709 | tf_op jit(solution)/shard_map/ffn_out/pallas_call | solution.py:685
  521.4 17.6 %ffn_out.6 = (bf16[1024,1024]{1,0:T(8,128)(2,1)}, bf16[1024,1024]{1,0:T(8,128)(2,1)}, bf16[1024,2048]{1,0:T(8,128)(2,1)}, bf16[1024,2048]{1,0:T(8,128)(2,1)}, f32[1,1024]{1,0:T(1,128)}) custom-call(f32[1024,1024]{1,0:T(8,128)} %get-tuple-element.279.a_ref, bf16[1024,1024]{1,0:T(8,128)(2,1)} %get-tuple-element.280.p_ref, ...), custom_call_target="tpu_custom_call" | custom-call | flops 2863311616 | bytes 9786709 | tf_op jit(solution)/shard_map/ffn_out/pallas_call | solution.py:685
  541.8 11.6 %collective-permute-done.46 = bf16[128,2048]{1,0:T(8,128)(2,1)S(1)} collective-permute-done((bf16[128,2048]{1,0:T(8,128)(2,1)S(1)}, bf16[128,2048]{1,0:T(8,128)(2,1)S(1)}, u32[]{:S(2)}, u32[]{:S(2)}) %collective-permute-start.46) | collective-permute-done | bytes 524320 | tf_op jit(solution)/shard_map/ppermute | solution.py:26
  557.5 17.8 %ffn_out.7 = (bf16[1024,1024]{1,0:T(8,128)(2,1)}, bf16[1024,1024]{1,0:T(8,128)(2,1)}, bf16[1024,2048]{1,0:T(8,128)(2,1)}, bf16[1024,2048]{1,0:T(8,128)(2,1)}, f32[1,1024]{1,0:T(1,128)}) custom-call(f32[1024,1024]{1,0:T(8,128)} %get-tuple-element.273.a_ref, bf16[1024,1024]{1,0:T(8,128)(2,1)} %get-tuple-element.274.p_ref, ...), custom_call_target="tpu_custom_call" | custom-call | flops 2863311616 | bytes 9786709 | tf_op jit(solution)/shard_map/ffn_out/pallas_call | solution.py:685
  578.8 24.3 %weight_grad.3 = bf16[1024,2048]{1,0:T(8,128)(2,1)} custom-call(bf16[1024,1024]{1,0:T(8,128)(2,1)} %get-tuple-element.294.refs_0_, bf16[1024,1024]{1,0:T(8,128)(2,1)} %get-tuple-element.296.refs_1_, bf16[1024,1024]{1,0:T(8,128)(2,1)} %get-tuple-element.298.refs_2_, bf16[1024,1024]{1,0:T(8,128)(2,1)} %get-tuple-element.300.refs_3_, ...), custom_call_target="tpu_custom_call" | custom-call | flops 5726623232 | bytes 9786709 | tf_op jit(solution)/shard_map/weight_grad/pallas_call | solution.py:763
  607.8 21.9 %collective-permute-done.50 = bf16[256,2048]{1,0:T(8,128)(2,1)S(1)} collective-permute-done((bf16[256,2048]{1,0:T(8,128)(2,1)S(1)}, bf16[256,2048]{1,0:T(8,128)(2,1)S(1)}, u32[]{:S(2)}, u32[]{:S(2)}) %collective-permute-start.50) | collective-permute-done | bytes 1048608 | tf_op jit(solution)/shard_map/ppermute | solution.py:26
  634.3 6.2 collective-permute-done.49
  646.0 16.2 %out_back.2 = (f32[256,2048]{1,0:T(8,128)}, bf16[256,2048]{1,0:T(8,128)(2,1)}, bf16[8,256,256]{2,1,0:T(8,128)(2,1)}, f32[1,2048]{1,0:T(1,128)}, f32[8,1,256]{2,1,0:T(1,128)}) custom-call(s32[8]{0:T(128)} %copy-done.56, f32[256,2048]{1,0:T(8,128)} %add_add_fusion.1.grad_ref, f32[256,2048]{1,0:T(8,128)} %get-tuple-element.227.res_ref, ...), custom_call_target="tpu_custom_call" | custom-call | flops 715827904 | bytes 6291456 | tf_op jit(solution)/shard_map/out_back/pallas_call | solution.py:533
  666.7 24.3 %weight_grad.4 = bf16[1024,2048]{1,0:T(8,128)(2,1)} custom-call(bf16[1024,1024]{1,0:T(8,128)(2,1)} %get-tuple-element.308.refs_0_, bf16[1024,1024]{1,0:T(8,128)(2,1)} %get-tuple-element.310.refs_1_, bf16[1024,1024]{1,0:T(8,128)(2,1)} %get-tuple-element.312.refs_2_, bf16[1024,1024]{1,0:T(8,128)(2,1)} %get-tuple-element.314.refs_3_, ...), custom_call_target="tpu_custom_call" | custom-call | flops 5726623232 | bytes 9786709 | tf_op jit(solution)/shard_map/weight_grad/pallas_call | solution.py:763
  695.3 3.7 all-to-all-start.5
  712.6 5.8 all-to-all-done.5
  724.8 14.7 %collective-permute-done.57 = bf16[256,2048]{1,0:T(8,128)(2,1)} collective-permute-done((bf16[256,2048]{1,0:T(8,128)(2,1)}, bf16[256,2048]{1,0:T(8,128)(2,1)}, u32[]{:S(2)}, u32[]{:S(2)}) %collective-permute-start.57) | collective-permute-done | bytes 1048608 | tf_op jit(solution)/shard_map/ppermute | solution.py:26
  740.2 4.2 add_add_fusion.grad_ref
  744.4 16.2 %out_back.3 = (f32[256,2048]{1,0:T(8,128)}, bf16[256,2048]{1,0:T(8,128)(2,1)}, bf16[8,256,256]{2,1,0:T(8,128)(2,1)}, f32[1,2048]{1,0:T(1,128)}, f32[8,1,256]{2,1,0:T(1,128)}) custom-call(s32[8]{0:T(128)} %copy-done.56, f32[256,2048]{1,0:T(8,128)} %add_add_fusion.grad_ref, f32[256,2048]{1,0:T(8,128)} %get-tuple-element.234.res_ref, ...), custom_call_target="tpu_custom_call" | custom-call | flops 715827904 | bytes 6291456 | tf_op jit(solution)/shard_map/out_back/pallas_call | solution.py:533
  764.3 10.6 out_grad.1
  780.5 32.3 %attend_back.2.x_ref.refs_0_.refs_1_ = bf16[2048,768]{1,0:T(8,128)(2,1)} custom-call(s32[8]{0:T(128)} %get-tuple-element.328.first, s32[8]{0:T(128)} %shift-right-arithmetic_add_fusion.spot, bf16[2048,256]{1,0:T(8,128)(2,1)} %get-tuple-element.203.q_ref, bf16[2048,256]{1,0:T(8,128)(2,1)} %get-tuple-element.206.k_ref, ...), custom_call_target="tpu_custom_call" | custom-call | flops 8589934592 | bytes 3495253 | tf_op jit(solution)/shard_map/attend_back/pallas_call | solution.py:972
  817.8 7.8 multiply.81
  832.6 7.3 multiply.82
  842.2 27.6 %attend_back.3.x_ref.refs_2_.refs_3_ = bf16[2048,768]{1,0:T(8,128)(2,1)} custom-call(s32[8]{0:T(128)} %get-tuple-element.336.first, s32[8]{0:T(128)} %shift-right-arithmetic_add_fusion.spot, bf16[2048,256]{1,0:T(8,128)(2,1)} %get-tuple-element.217.q_ref, bf16[2048,256]{1,0:T(8,128)(2,1)} %get-tuple-element.220.k_ref, ...), custom_call_target="tpu_custom_call" | custom-call | flops 8589934592 | bytes 3495253 | tf_op jit(solution)/shard_map/attend_back/pallas_call | solution.py:972
  874.7 7.5 multiply.83
  894.7 4.0 all-to-all-start.9
  899.0 7.3 multiply.84
  909.2 19.9 %weight_grad.5 = (bf16[768,2048]{1,0:T(8,128)(2,1)}, f32[1,2048]{1,0:T(1,128)}) custom-call(bf16[2048,768]{1,0:T(8,128)(2,1)} %attend_back.2.x_ref.refs_0_.refs_1_, bf16[2048,768]{1,0:T(8,128)(2,1)} %attend_back.2.x_ref.refs_0_.refs_1_, bf16[2048,768]{1,0:T(8,128)(2,1)} %attend_back.3.x_ref.refs_2_.refs_3_, ...), custom_call_target="tpu_custom_call" | custom-call | flops 4294967296 | bytes 8738133 | tf_op jit(solution)/shard_map/weight_grad/pallas_call | solution.py:763
  943.8 4.0 fusion.24
  965.7 4.6 all-to-all-done.8
  973.5 10.0 collective-permute-done.70
  997.8 21.5 %all-reduce.1 = (f32[3,256]{1,0:T(4,128)S(1)}, f32[4,256]{1,0:T(4,128)S(1)}) all-reduce(f32[3,256]{1,0:T(4,128)S(1)} %copy.279, f32[4,256]{1,0:T(4,128)S(1)} %reshape.402), channel_id=1, replica_groups=mesh['seq'=8,'tensor'=4] {'tensor'}, use_global_device_ids=true, to_apply=%region_17.18 | all-reduce | flops 1792 | bytes 14336 | tf_op jit(solution)/shard_map/psum | solution.py:1358
  1022.3 7.1 collective-permute-done.73
  1029.5 5.4 fusion.31
  1035.0 17.8 %reduce-scatter.13.cloned.1.call-done = bf16[192,2048]{1,0:T(8,128)(2,1)} async-done(((bf16[768,2048]{1,0:T(8,128)(2,1)}), bf16[192,2048]{1,0:T(8,128)(2,1)}) %reduce-scatter.13.cloned.1.call-update) | async-done | bytes 786448 | tf_op jit(solution)/shard_map/reduce_scatter | solution.py:1373
  1055.3 4.2 all-to-all-start.7
  1059.5 4.2 fusion.9
  1065.9 6.1 all-to-all-done.7
  (514 shorter events, 310.5 us)
Async XLA Ops:
  15.0 92.0 %all-gather.11.cloned.1.call-start = ((), (), s32[]{:S(2)}) async-start(), calls=%async_computation.23 | async-start | bytes 3932160 | tf_op jit(solution)/shard_map/all_gather | solution.py:1080
  33.9 25.6 %collective-permute-start = (bf16[256,2048]{1,0:T(8,128)(2,1)S(1)}, bf16[256,2048]{1,0:T(8,128)(2,1)}, u32[]{:S(2)}, u32[]{:S(2)}) collective-permute-start(bf16[256,2048]{1,0:T(8,128)(2,1)S(1)} %get-tuple-element.188.refs_0_), channel_id=1, source_target_pairs={{0,16},{4,20},{8,24},{12,28},{16,0},{20,4},{24,8},{28,12},{1,17},{... | collective-permute-start | bytes 3145736 | tf_op jit(solution)/shard_map/ppermute | solution.py:26
  34.5 25.2 %collective-permute-start.1 = (bf16[256,2048]{1,0:T(8,128)(2,1)S(1)}, bf16[256,2048]{1,0:T(8,128)(2,1)}, u32[]{:S(2)}, u32[]{:S(2)}) collective-permute-start(bf16[256,2048]{1,0:T(8,128)(2,1)S(1)} %get-tuple-element.188.refs_0_), channel_id=1, source_target_pairs={{0,8},{4,12},{8,0},{12,4},{16,24},{20,28},{24,16},{28,20},{1,9},{5... | collective-permute-start | bytes 3145736 | tf_op jit(solution)/shard_map/ppermute | solution.py:26
  80.3 70.5 %collective-permute-start.9 = (bf16[1024,2048]{1,0:T(8,128)(2,1)}, bf16[1024,2048]{1,0:T(8,128)(2,1)}, u32[]{:S(2)}, u32[]{:S(2)}) collective-permute-start(bf16[1024,2048]{1,0:T(8,128)(2,1)} %join.7.x_ref.refs_4_), channel_id=1, source_target_pairs={{0,4},{4,0},{8,12},{12,8},{16,20},{20,16},{24,28},{28,24},{1,5},{5... | collective-permute-start | bytes 12582920 | tf_op jit(solution)/shard_map/ppermute | solution.py:26
  86.8 64.1 %all-gather.7.cloned.1.call-start = ((), (), s32[]{:S(2)}) async-start(), calls=%async_computation.16 | async-start | bytes 1310720 | tf_op jit(solution)/shard_map/all_gather | solution.py:1087
  86.8 37.4 %collective-permute-start.8 = (bf16[256,2048]{1,0:T(8,128)(2,1)}, bf16[256,2048]{1,0:T(8,128)(2,1)}, u32[]{:S(2)}, u32[]{:S(2)}) collective-permute-start(bf16[256,2048]{1,0:T(8,128)(2,1)} %get-tuple-element.204.refs_0_), channel_id=1, source_target_pairs={{0,16},{4,20},{8,24},{12,28},{16,0},{20,4},{24,8},{28,12},{1,17},{... | collective-permute-start | bytes 3145736 | tf_op jit(solution)/shard_map/ppermute | solution.py:26
  88.7 35.6 %collective-permute-start.7 = (bf16[256,2048]{1,0:T(8,128)(2,1)}, bf16[256,2048]{1,0:T(8,128)(2,1)}, u32[]{:S(2)}, u32[]{:S(2)}) collective-permute-start(bf16[256,2048]{1,0:T(8,128)(2,1)} %get-tuple-element.204.refs_0_), channel_id=1, source_target_pairs={{0,8},{4,12},{8,0},{12,4},{16,24},{20,28},{24,16},{28,20},{1,9},{5... | collective-permute-start | bytes 3145736 | tf_op jit(solution)/shard_map/ppermute | solution.py:26
  102.7 33.9 %all-to-all-start.2 = ((bf16[8,256,256]{2,1,0:T(8,128)(2,1)}), bf16[8,256,256]{2,1,0:T(8,128)(2,1)}, u32[]{:S(2)}, u32[]{:S(2)}) async-start(bf16[8,256,256]{2,1,0:T(8,128)(2,1)} %bitcast.234), calls=%async_computation.2 | async-start | bytes 2097152 | tf_op jit(solution)/shard_map/all_to_all | solution.py:1094
  106.9 213.0 %all-gather.9.cloned.1.call-start = ((), (), s32[]{:S(2)}) async-start(), calls=%async_computation.17 | async-start | bytes 5242880 | tf_op jit(solution)/shard_map/all_gather | solution.py:1169
  128.1 31.4 %collective-permute-start.11 = (bf16[128,2048]{1,0:T(8,128)(2,1)}, bf16[128,2048]{1,0:T(8,128)(2,1)S(1)}, u32[]{:S(2)}, u32[]{:S(2)}) collective-permute-start(bf16[128,2048]{1,0:T(8,128)(2,1)} %slice.527), channel_id=1, source_target_pairs={{0,8},{4,12},{8,0},{12,4},{16,24},{20,28},{24,16},{28,20},{1,9},{5... | collective-permute-start | bytes 1572872 | tf_op jit(solution)/shard_map/ppermute | solution.py:26
  129.5 30.0 %collective-permute-start.10 = (bf16[128,2048]{1,0:T(8,128)(2,1)}, bf16[128,2048]{1,0:T(8,128)(2,1)S(1)}, u32[]{:S(2)}, u32[]{:S(2)}) collective-permute-start(bf16[128,2048]{1,0:T(8,128)(2,1)} %slice.526), channel_id=1, source_target_pairs={{0,16},{4,20},{8,24},{12,28},{16,0},{20,4},{24,8},{28,12},{1,17},{... | collective-permute-start | bytes 1572872 | tf_op jit(solution)/shard_map/ppermute | solution.py:26
  164.3 52.2 %collective-permute-start.14 = (bf16[1024,2048]{1,0:T(8,128)(2,1)}, bf16[1024,2048]{1,0:T(8,128)(2,1)}, u32[]{:S(2)}, u32[]{:S(2)}) collective-permute-start(bf16[1024,2048]{1,0:T(8,128)(2,1)} %join.8.x_ref.refs_6_), channel_id=1, source_target_pairs={{0,4},{4,0},{8,12},{12,8},{16,20},{20,16},{24,28},{28,24},{1,5},{5... | collective-permute-start | bytes 12582920 | tf_op jit(solution)/shard_map/ppermute | solution.py:26
  170.5 28.1 %collective-permute-start.13 = (bf16[2048,256]{1,0:T(8,128)(2,1)}, bf16[2048,256]{1,0:T(8,128)(2,1)S(1)}, u32[]{:S(2)}, u32[]{:S(2)}) collective-permute-start(bf16[2048,256]{1,0:T(8,128)(2,1)} %all-gather.7.cloned.1.call-done.refs_0_), channel_id=1, source_target_pairs={{0,16},{4,20},{8,24},{12,28},{16,0},{20,4},{24,8},{28,12},{1,17},{... | collective-permute-start | bytes 3145736 | tf_op jit(solution)/shard_map/ppermute | solution.py:26
  171.1 27.6 %collective-permute-start.12 = (bf16[2048,256]{1,0:T(8,128)(2,1)}, bf16[2048,256]{1,0:T(8,128)(2,1)}, u32[]{:S(2)}, u32[]{:S(2)}) collective-permute-start(bf16[2048,256]{1,0:T(8,128)(2,1)} %all-gather.7.cloned.1.call-done.refs_0_), channel_id=1, source_target_pairs={{0,8},{4,12},{8,0},{12,4},{16,24},{20,28},{24,16},{28,20},{1,9},{5... | collective-permute-start | bytes 3145736 | tf_op jit(solution)/shard_map/ppermute | solution.py:26
  200.2 24.9 %collective-permute-start.16 = (bf16[1024,256]{1,0:T(8,128)(2,1)S(1)}, bf16[1024,256]{1,0:T(8,128)(2,1)S(1)}, u32[]{:S(2)}, u32[]{:S(2)}) collective-permute-start(bf16[1024,256]{1,0:T(8,128)(2,1)S(1)} %slice.530), channel_id=1, source_target_pairs={{0,8},{4,12},{8,0},{12,4},{16,24},{20,28},{24,16},{28,20},{1,9},{5... | collective-permute-start | bytes 1572872 | tf_op jit(solution)/shard_map/ppermute | solution.py:26
  230.1 39.1 %collective-permute-start.19 = (bf16[8192,256]{1,0:T(8,128)(2,1)}, bf16[8192,256]{1,0:T(8,128)(2,1)}, u32[]{:S(2)}, u32[]{:S(2)}) collective-permute-start(bf16[8192,256]{1,0:T(8,128)(2,1)} %join.9), channel_id=1, source_target_pairs={{0,4},{4,0},{8,12},{12,8},{16,20},{20,16},{24,28},{28,24},{1,5},{5... | collective-permute-start | bytes 12582920 | tf_op jit(solution)/shard_map/ppermute | solution.py:26
  230.2 30.4 %collective-permute-start.18 = (bf16[256,2048]{1,0:T(8,128)(2,1)}, bf16[256,2048]{1,0:T(8,128)(2,1)}, u32[]{:S(2)}, u32[]{:S(2)}) collective-permute-start(bf16[256,2048]{1,0:T(8,128)(2,1)} %get-tuple-element.230.refs_0_.cot_ref), channel_id=1, source_target_pairs={{0,16},{4,20},{8,24},{12,28},{16,0},{20,4},{24,8},{28,12},{1,17},{... | collective-permute-start | bytes 3145736 | tf_op jit(solution)/shard_map/ppermute | solution.py:26
  230.7 29.8 %collective-permute-start.17 = (bf16[256,2048]{1,0:T(8,128)(2,1)}, bf16[256,2048]{1,0:T(8,128)(2,1)}, u32[]{:S(2)}, u32[]{:S(2)}) collective-permute-start(bf16[256,2048]{1,0:T(8,128)(2,1)} %get-tuple-element.230.refs_0_.cot_ref), channel_id=1, source_target_pairs={{0,8},{4,12},{8,0},{12,4},{16,24},{20,28},{24,16},{28,20},{1,9},{5... | collective-permute-start | bytes 3145736 | tf_op jit(solution)/shard_map/ppermute | solution.py:26
  233.5 35.7 %all-to-all-start.3 = ((bf16[8,256,256]{2,1,0:T(8,128)(2,1)}), bf16[8,256,256]{2,1,0:T(8,128)(2,1)S(1)}, u32[]{:S(2)}, u32[]{:S(2)}) async-start(bf16[8,256,256]{2,1,0:T(8,128)(2,1)} %bitcast.240), calls=%async_computation.3 | async-start | bytes 2097152 | tf_op jit(solution)/shard_map/all_to_all | solution.py:1132
  237.1 140.5 %all-gather.13.cloned.1.call-start = ((), (), s32[]{:S(2)}) async-start(), calls=%async_computation.24 | async-start | bytes 5242880 | tf_op jit(solution)/shard_map/all_gather | solution.py:1160
  286.4 43.5 %collective-permute-start.22 = (bf16[1024,2048]{1,0:T(8,128)(2,1)}, bf16[1024,2048]{1,0:T(8,128)(2,1)}, u32[]{:S(2)}, u32[]{:S(2)}) collective-permute-start(bf16[1024,2048]{1,0:T(8,128)(2,1)} %join.10.c_ref.refs_4_), channel_id=1, source_target_pairs={{0,4},{4,0},{8,12},{12,8},{16,20},{20,16},{24,28},{28,24},{1,5},{5... | collective-permute-start | bytes 12582920 | tf_op jit(solution)/shard_map/ppermute | solution.py:26
  290.1 527.7 %reduce-scatter.9.cloned.1.call-start = ((), (), s32[]{:S(2)}) async-start(), calls=%async_computation.18 | async-start | bytes 5242880 | tf_op jit(solution)/shard_map/reduce_scatter | solution.py:1260
  290.1 38.6 %collective-permute-start.24 = (bf16[256,2048]{1,0:T(8,128)(2,1)}, bf16[256,2048]{1,0:T(8,128)(2,1)S(1)}, u32[]{:S(2)}, u32[]{:S(2)}) collective-permute-start(bf16[256,2048]{1,0:T(8,128)(2,1)} %get-tuple-element.242.refs_0_), channel_id=1, source_target_pairs={{0,16},{4,20},{8,24},{12,28},{16,0},{20,4},{24,8},{28,12},{1,17},{... | collective-permute-start | bytes 3145736 | tf_op jit(solution)/shard_map/ppermute | solution.py:26
  292.0 36.7 %collective-permute-start.23 = (bf16[256,2048]{1,0:T(8,128)(2,1)}, bf16[256,2048]{1,0:T(8,128)(2,1)S(1)}, u32[]{:S(2)}, u32[]{:S(2)}) collective-permute-start(bf16[256,2048]{1,0:T(8,128)(2,1)} %get-tuple-element.242.refs_0_), channel_id=1, source_target_pairs={{0,8},{4,12},{8,0},{12,4},{16,24},{20,28},{24,16},{28,20},{1,9},{5... | collective-permute-start | bytes 3145736 | tf_op jit(solution)/shard_map/ppermute | solution.py:26
  346.7 64.5 %collective-permute-start.29 = (bf16[1024,2048]{1,0:T(8,128)(2,1)}, bf16[1024,2048]{1,0:T(8,128)(2,1)}, u32[]{:S(2)}, u32[]{:S(2)}) collective-permute-start(bf16[1024,2048]{1,0:T(8,128)(2,1)} %join.11.refs_0_.refs_4_), channel_id=1, source_target_pairs={{0,4},{4,0},{8,12},{12,8},{16,20},{20,16},{24,28},{28,24},{1,5},{5... | collective-permute-start | bytes 12582920 | tf_op jit(solution)/shard_map/ppermute | solution.py:26
  346.8 26.0 %collective-permute-start.28 = (bf16[256,2048]{1,0:T(8,128)(2,1)S(1)}, bf16[256,2048]{1,0:T(8,128)(2,1)S(1)}, u32[]{:S(2)}, u32[]{:S(2)}) collective-permute-start(bf16[256,2048]{1,0:T(8,128)(2,1)S(1)} %copy-done.7), channel_id=1, source_target_pairs={{0,16},{4,20},{8,24},{12,28},{16,0},{20,4},{24,8},{28,12},{1,17},{... | collective-permute-start | bytes 3145736 | tf_op jit(solution)/shard_map/ppermute | solution.py:26
  347.3 26.0 %collective-permute-start.27 = (bf16[256,2048]{1,0:T(8,128)(2,1)S(1)}, bf16[256,2048]{1,0:T(8,128)(2,1)S(1)}, u32[]{:S(2)}, u32[]{:S(2)}) collective-permute-start(bf16[256,2048]{1,0:T(8,128)(2,1)S(1)} %copy-done.7), channel_id=1, source_target_pairs={{0,8},{4,12},{8,0},{12,4},{16,24},{20,28},{24,16},{28,20},{1,9},{5... | collective-permute-start | bytes 3145736 | tf_op jit(solution)/shard_map/ppermute | solution.py:26
  348.2 47.0 %collective-permute-start.33 = (bf16[256,2048]{1,0:T(8,128)(2,1)}, bf16[256,2048]{1,0:T(8,128)(2,1)S(1)}, u32[]{:S(2)}, u32[]{:S(2)}) collective-permute-start(bf16[256,2048]{1,0:T(8,128)(2,1)} %get-tuple-element.256.refs_0_), channel_id=1, source_target_pairs={{0,16},{4,20},{8,24},{12,28},{16,0},{20,4},{24,8},{28,12},{1,17},{... | collective-permute-start | bytes 3145736 | tf_op jit(solution)/shard_map/ppermute | solution.py:26
  349.9 45.8 %collective-permute-start.32 = (bf16[256,2048]{1,0:T(8,128)(2,1)}, bf16[256,2048]{1,0:T(8,128)(2,1)S(1)}, u32[]{:S(2)}, u32[]{:S(2)}) collective-permute-start(bf16[256,2048]{1,0:T(8,128)(2,1)} %get-tuple-element.256.refs_0_), channel_id=1, source_target_pairs={{0,8},{4,12},{8,0},{12,4},{16,24},{20,28},{24,16},{28,20},{1,9},{5... | collective-permute-start | bytes 3145736 | tf_op jit(solution)/shard_map/ppermute | solution.py:26
  375.0 32.0 %collective-permute-start.31 = (bf16[128,2048]{1,0:T(8,128)(2,1)}, bf16[128,2048]{1,0:T(8,128)(2,1)S(1)}, u32[]{:S(2)}, u32[]{:S(2)}) collective-permute-start(bf16[128,2048]{1,0:T(8,128)(2,1)} %slice.541), channel_id=1, source_target_pairs={{0,8},{4,12},{8,0},{12,4},{16,24},{20,28},{24,16},{28,20},{1,9},{5... | collective-permute-start | bytes 1572872 | tf_op jit(solution)/shard_map/ppermute | solution.py:26
  375.9 31.0 %collective-permute-start.30 = (bf16[128,2048]{1,0:T(8,128)(2,1)}, bf16[128,2048]{1,0:T(8,128)(2,1)}, u32[]{:S(2)}, u32[]{:S(2)}) collective-permute-start(bf16[128,2048]{1,0:T(8,128)(2,1)} %slice.540), channel_id=1, source_target_pairs={{0,16},{4,20},{8,24},{12,28},{16,0},{20,4},{24,8},{28,12},{1,17},{... | collective-permute-start | bytes 1572872 | tf_op jit(solution)/shard_map/ppermute | solution.py:26
  395.8 26.5 %collective-permute-start.36 = (bf16[128,2048]{1,0:T(8,128)(2,1)S(1)}, bf16[128,2048]{1,0:T(8,128)(2,1)S(1)}, u32[]{:S(2)}, u32[]{:S(2)}) collective-permute-start(bf16[128,2048]{1,0:T(8,128)(2,1)S(1)} %slice.543), channel_id=1, source_target_pairs={{0,8},{4,12},{8,0},{12,4},{16,24},{20,28},{24,16},{28,20},{1,9},{5... | collective-permute-start | bytes 1572872 | tf_op jit(solution)/shard_map/ppermute | solution.py:26
  396.8 25.5 %collective-permute-start.35 = (bf16[128,2048]{1,0:T(8,128)(2,1)S(1)}, bf16[128,2048]{1,0:T(8,128)(2,1)S(1)}, u32[]{:S(2)}, u32[]{:S(2)}) collective-permute-start(bf16[128,2048]{1,0:T(8,128)(2,1)S(1)} %slice.542), channel_id=1, source_target_pairs={{0,16},{4,20},{8,24},{12,28},{16,0},{20,4},{24,8},{28,12},{1,17},{... | collective-permute-start | bytes 1572872 | tf_op jit(solution)/shard_map/ppermute | solution.py:26
  411.1 36.4 %collective-permute-start.39 = (bf16[1024,2048]{1,0:T(8,128)(2,1)}, bf16[1024,2048]{1,0:T(8,128)(2,1)}, u32[]{:S(2)}, u32[]{:S(2)}) collective-permute-start(bf16[1024,2048]{1,0:T(8,128)(2,1)} %join.12.refs_1_.refs_6_), channel_id=1, source_target_pairs={{0,4},{4,0},{8,12},{12,8},{16,20},{20,16},{24,28},{28,24},{1,5},{5... | collective-permute-start | bytes 12582920 | tf_op jit(solution)/shard_map/ppermute | solution.py:26
  488.6 30.8 %collective-permute-start.44 = (bf16[1024,2048]{1,0:T(8,128)(2,1)}, bf16[1024,2048]{1,0:T(8,128)(2,1)}, u32[]{:S(2)}, u32[]{:S(2)}) collective-permute-start(bf16[1024,2048]{1,0:T(8,128)(2,1)} %get-tuple-element.284), channel_id=1, source_target_pairs={{0,4},{4,0},{8,12},{12,8},{16,20},{20,16},{24,28},{28,24},{1,5},{5... | collective-permute-start | bytes 12582920 | tf_op jit(solution)/shard_map/ppermute | solution.py:26
  539.0 36.2 %collective-permute-start.47 = (bf16[1024,2048]{1,0:T(8,128)(2,1)}, bf16[1024,2048]{1,0:T(8,128)(2,1)S(1)}, u32[]{:S(2)}, u32[]{:S(2)}) collective-permute-start(bf16[1024,2048]{1,0:T(8,128)(2,1)} %get-tuple-element.293), channel_id=1, source_target_pairs={{0,4},{4,0},{8,12},{12,8},{16,20},{20,16},{24,28},{28,24},{1,5},{5... | collective-permute-start | bytes 12582920 | tf_op jit(solution)/shard_map/ppermute | solution.py:26
  603.1 271.5 %reduce-scatter.11.cloned.1.call-start = ((), (), s32[]{:S(2)}) async-start(), calls=%async_computation.19 | async-start | bytes 5242880 | tf_op jit(solution)/shard_map/reduce_scatter | solution.py:1311
  603.6 58.6 %collective-permute-start.52 = (bf16[1024,2048]{1,0:T(8,128)(2,1)}, bf16[1024,2048]{1,0:T(8,128)(2,1)S(1)}, u32[]{:S(2)}, u32[]{:S(2)}) collective-permute-start(bf16[1024,2048]{1,0:T(8,128)(2,1)} %get-tuple-element.306), channel_id=1, source_target_pairs={{0,4},{4,0},{8,12},{12,8},{16,20},{20,16},{24,28},{28,24},{1,5},{5... | collective-permute-start | bytes 12582920 | tf_op jit(solution)/shard_map/ppermute | solution.py:26
  603.7 26.0 %collective-permute-start.50 = (bf16[256,2048]{1,0:T(8,128)(2,1)S(1)}, bf16[256,2048]{1,0:T(8,128)(2,1)S(1)}, u32[]{:S(2)}, u32[]{:S(2)}) collective-permute-start(bf16[256,2048]{1,0:T(8,128)(2,1)S(1)} %pad_maximum_fusion.2), channel_id=1, source_target_pairs={{0,8},{4,12},{8,0},{12,4},{16,24},{20,28},{24,16},{28,20},{1,9},{5... | collective-permute-start | bytes 3145736 | tf_op jit(solution)/shard_map/ppermute | solution.py:26
  604.8 26.0 %collective-permute-start.51 = (bf16[256,2048]{1,0:T(8,128)(2,1)S(1)}, bf16[256,2048]{1,0:T(8,128)(2,1)S(1)}, u32[]{:S(2)}, u32[]{:S(2)}) collective-permute-start(bf16[256,2048]{1,0:T(8,128)(2,1)S(1)} %pad_maximum_fusion.3), channel_id=1, source_target_pairs={{0,16},{4,20},{8,24},{12,28},{16,0},{20,4},{24,8},{28,12},{1,17},{... | collective-permute-start | bytes 3145736 | tf_op jit(solution)/shard_map/ppermute | solution.py:26
  606.4 34.1 %collective-permute-start.49 = (bf16[128,2048]{1,0:T(8,128)(2,1)S(1)}, bf16[128,2048]{1,0:T(8,128)(2,1)S(1)}, u32[]{:S(2)}, u32[]{:S(2)}) collective-permute-start(bf16[128,2048]{1,0:T(8,128)(2,1)S(1)} %get-tuple-element.484), channel_id=1, source_target_pairs={{0,8},{4,12},{8,0},{12,4},{16,24},{20,28},{24,16},{28,20},{1,9},{5... | collective-permute-start | bytes 1572872 | tf_op jit(solution)/shard_map/ppermute | solution.py:26
  607.5 33.8 %collective-permute-start.48 = (bf16[128,2048]{1,0:T(8,128)(2,1)S(1)}, bf16[128,2048]{1,0:T(8,128)(2,1)S(1)}, u32[]{:S(2)}, u32[]{:S(2)}) collective-permute-start(bf16[128,2048]{1,0:T(8,128)(2,1)S(1)} %get-tuple-element.485), channel_id=1, source_target_pairs={{0,16},{4,20},{8,24},{12,28},{16,0},{20,4},{24,8},{28,12},{1,17},{... | collective-permute-start | bytes 1572872 | tf_op jit(solution)/shard_map/ppermute | solution.py:26
  691.0 84.2 %collective-permute-start.59 = (bf16[1024,2048]{1,0:T(8,128)(2,1)}, bf16[1024,2048]{1,0:T(8,128)(2,1)}, u32[]{:S(2)}, u32[]{:S(2)}) collective-permute-start(bf16[1024,2048]{1,0:T(8,128)(2,1)} %get-tuple-element.327), channel_id=1, source_target_pairs={{0,4},{4,0},{8,12},{12,8},{16,20},{20,16},{24,28},{28,24},{1,5},{5... | collective-permute-start | bytes 12582920 | tf_op jit(solution)/shard_map/ppermute | solution.py:26
  699.1 40.5 %collective-permute-start.57 = (bf16[256,2048]{1,0:T(8,128)(2,1)}, bf16[256,2048]{1,0:T(8,128)(2,1)}, u32[]{:S(2)}, u32[]{:S(2)}) collective-permute-start(bf16[256,2048]{1,0:T(8,128)(2,1)} %pad_maximum_fusion.4), channel_id=1, source_target_pairs={{0,8},{4,12},{8,0},{12,4},{16,24},{20,28},{24,16},{28,20},{1,9},{5... | collective-permute-start | bytes 3145736 | tf_op jit(solution)/shard_map/ppermute | solution.py:26
  701.1 39.2 %collective-permute-start.58 = (bf16[256,2048]{1,0:T(8,128)(2,1)}, bf16[256,2048]{1,0:T(8,128)(2,1)}, u32[]{:S(2)}, u32[]{:S(2)}) collective-permute-start(bf16[256,2048]{1,0:T(8,128)(2,1)} %pad_maximum_fusion.5), channel_id=1, source_target_pairs={{0,16},{4,20},{8,24},{12,28},{16,0},{20,4},{24,8},{28,12},{1,17},{... | collective-permute-start | bytes 3145736 | tf_op jit(solution)/shard_map/ppermute | solution.py:26
  760.7 57.2 %all-to-all-start.6 = ((bf16[8,256,256]{2,1,0:T(8,128)(2,1)}), bf16[8,256,256]{2,1,0:T(8,128)(2,1)S(1)}, u32[]{:S(2)}, u32[]{:S(2)}) async-start(bf16[8,256,256]{2,1,0:T(8,128)(2,1)} %get-tuple-element.320), calls=%async_computation.7 | async-start | bytes 2097152 | tf_op jit(solution)/shard_map/all_to_all | solution.py:1275
  764.2 118.5 %reduce-scatter.15.cloned.1.call-start = ((), (), s32[]{:S(2)}) async-start(), calls=%async_computation.21 | async-start | bytes 9437184 | tf_op jit(solution)/shard_map/reduce_scatter | solution.py:1320
  774.9 219.2 %reduce-scatter.17.cloned.1.call-start = ((), (), s32[]{:S(2)}) async-start(), calls=%async_computation.22 | async-start | bytes 1310720 | tf_op jit(solution)/shard_map/reduce_scatter | solution.py:1319
  777.1 35.7 %collective-permute-start.60 = (bf16[128,2048]{1,0:T(8,128)(2,1)S(1)}, bf16[128,2048]{1,0:T(8,128)(2,1)S(1)}, u32[]{:S(2)}, u32[]{:S(2)}) collective-permute-start(bf16[128,2048]{1,0:T(8,128)(2,1)S(1)} %get-tuple-element.472), channel_id=1, source_target_pairs={{0,16},{4,20},{8,24},{12,28},{16,0},{20,4},{24,8},{28,12},{1,17},{... | collective-permute-start | bytes 1572872 | tf_op jit(solution)/shard_map/ppermute | solution.py:26
  779.0 33.8 %collective-permute-start.62 = (bf16[128,2048]{1,0:T(8,128)(2,1)S(1)}, bf16[128,2048]{1,0:T(8,128)(2,1)}, u32[]{:S(2)}, u32[]{:S(2)}) collective-permute-start(bf16[128,2048]{1,0:T(8,128)(2,1)S(1)} %get-tuple-element.473), channel_id=1, source_target_pairs={{0,8},{4,12},{8,0},{12,4},{16,24},{20,28},{24,16},{28,20},{1,9},{5... | collective-permute-start | bytes 1572872 | tf_op jit(solution)/shard_map/ppermute | solution.py:26
  841.9 28.0 %collective-permute-start.65 = (bf16[128,2048]{1,0:T(8,128)(2,1)S(1)}, bf16[128,2048]{1,0:T(8,128)(2,1)S(1)}, u32[]{:S(2)}, u32[]{:S(2)}) collective-permute-start(bf16[128,2048]{1,0:T(8,128)(2,1)S(1)} %get-tuple-element.466), channel_id=1, source_target_pairs={{0,16},{4,20},{8,24},{12,28},{16,0},{20,4},{24,8},{28,12},{1,17},{... | collective-permute-start | bytes 1572872 | tf_op jit(solution)/shard_map/ppermute | solution.py:26
  842.1 27.7 %collective-permute-start.67 = (bf16[128,2048]{1,0:T(8,128)(2,1)S(1)}, bf16[128,2048]{1,0:T(8,128)(2,1)S(1)}, u32[]{:S(2)}, u32[]{:S(2)}) collective-permute-start(bf16[128,2048]{1,0:T(8,128)(2,1)S(1)} %get-tuple-element.467), channel_id=1, source_target_pairs={{0,8},{4,12},{8,0},{12,4},{16,24},{20,28},{24,16},{28,20},{1,9},{5... | collective-permute-start | bytes 1572872 | tf_op jit(solution)/shard_map/ppermute | solution.py:26
  889.3 53.6 %collective-permute-start.54 = (bf16[256,2048]{1,0:T(8,128)(2,1)}, bf16[256,2048]{1,0:T(8,128)(2,1)}, u32[]{:S(2)}, u32[]{:S(2)}) collective-permute-start(bf16[256,2048]{1,0:T(8,128)(2,1)} %pad_maximum_fusion.6), channel_id=1, source_target_pairs={{0,8},{4,12},{8,0},{12,4},{16,24},{20,28},{24,16},{28,20},{1,9},{5... | collective-permute-start | bytes 3145736 | tf_op jit(solution)/shard_map/ppermute | solution.py:26
  890.9 52.1 %collective-permute-start.56 = (bf16[256,2048]{1,0:T(8,128)(2,1)}, bf16[256,2048]{1,0:T(8,128)(2,1)}, u32[]{:S(2)}, u32[]{:S(2)}) collective-permute-start(bf16[256,2048]{1,0:T(8,128)(2,1)} %pad_maximum_fusion.7), channel_id=1, source_target_pairs={{0,16},{4,20},{8,24},{12,28},{16,0},{20,4},{24,8},{28,12},{1,17},{... | collective-permute-start | bytes 3145736 | tf_op jit(solution)/shard_map/ppermute | solution.py:26
  892.8 61.7 %collective-permute-start.63 = (bf16[256,2048]{1,0:T(8,128)(2,1)}, bf16[256,2048]{1,0:T(8,128)(2,1)}, u32[]{:S(2)}, u32[]{:S(2)}) collective-permute-start(bf16[256,2048]{1,0:T(8,128)(2,1)} %pad_maximum_fusion.9), channel_id=1, source_target_pairs={{0,16},{4,20},{8,24},{12,28},{16,0},{20,4},{24,8},{28,12},{1,17},{... | collective-permute-start | bytes 3145736 | tf_op jit(solution)/shard_map/ppermute | solution.py:26
  893.2 61.3 %collective-permute-start.61 = (bf16[256,2048]{1,0:T(8,128)(2,1)}, bf16[256,2048]{1,0:T(8,128)(2,1)}, u32[]{:S(2)}, u32[]{:S(2)}) collective-permute-start(bf16[256,2048]{1,0:T(8,128)(2,1)} %pad_maximum_fusion.8), channel_id=1, source_target_pairs={{0,8},{4,12},{8,0},{12,4},{16,24},{20,28},{24,16},{28,20},{1,9},{5... | collective-permute-start | bytes 3145736 | tf_op jit(solution)/shard_map/ppermute | solution.py:26
  894.7 55.2 %all-to-all-start.9 = ((bf16[8,256,256]{2,1,0:T(8,128)(2,1)}), bf16[8,256,256]{2,1,0:T(8,128)(2,1)S(1)}, u32[]{:S(2)}, u32[]{:S(2)}) async-start(bf16[8,256,256]{2,1,0:T(8,128)(2,1)} %bitcast.195), calls=%async_computation.14 | async-start | bytes 2097152 | tf_op jit(solution)/shard_map/all_to_all | solution.py:1363
  898.7 98.1 %reduce-scatter.19.cloned.1.call-start = ((), (), s32[]{:S(2)}) async-start(), calls=%async_computation.25 | async-start | bytes 1179648
  938.5 114.3 %reduce-scatter.13.cloned.1.call-start = ((), (), s32[]{:S(2)}) async-start(), calls=%async_computation.20 | async-start | bytes 3932160 | tf_op jit(solution)/shard_map/reduce_scatter | solution.py:1373
  959.3 24.2 %collective-permute-start.70 = (bf16[128,2048]{1,0:T(8,128)(2,1)}, bf16[128,2048]{1,0:T(8,128)(2,1)}, u32[]{:S(2)}, u32[]{:S(2)}) collective-permute-start(bf16[128,2048]{1,0:T(8,128)(2,1)} %get-tuple-element.460), channel_id=1, source_target_pairs={{0,16},{4,20},{8,24},{12,28},{16,0},{20,4},{24,8},{28,12},{1,17},{... | collective-permute-start | bytes 1572872 | tf_op jit(solution)/shard_map/ppermute | solution.py:26
  972.4 49.9 %collective-permute-start.68 = (bf16[256,2048]{1,0:T(8,128)(2,1)}, bf16[256,2048]{1,0:T(8,128)(2,1)S(1)}, u32[]{:S(2)}, u32[]{:S(2)}) collective-permute-start(bf16[256,2048]{1,0:T(8,128)(2,1)} %pad_maximum_fusion.11), channel_id=1, source_target_pairs={{0,16},{4,20},{8,24},{12,28},{16,0},{20,4},{24,8},{28,12},{1,17},{... | collective-permute-start | bytes 3145736 | tf_op jit(solution)/shard_map/ppermute | solution.py:26
  972.9 49.4 %collective-permute-start.66 = (bf16[256,2048]{1,0:T(8,128)(2,1)}, bf16[256,2048]{1,0:T(8,128)(2,1)}, u32[]{:S(2)}, u32[]{:S(2)}) collective-permute-start(bf16[256,2048]{1,0:T(8,128)(2,1)} %pad_maximum_fusion.10), channel_id=1, source_target_pairs={{0,8},{4,12},{8,0},{12,4},{16,24},{20,28},{24,16},{28,20},{1,9},{5... | collective-permute-start | bytes 3145736 | tf_op jit(solution)/shard_map/ppermute | solution.py:26
  988.3 41.1 %collective-permute-start.73 = (bf16[256,2048]{1,0:T(8,128)(2,1)}, bf16[256,2048]{1,0:T(8,128)(2,1)}, u32[]{:S(2)}, u32[]{:S(2)}) collective-permute-start(bf16[256,2048]{1,0:T(8,128)(2,1)} %pad_maximum_fusion.13), channel_id=1, source_target_pairs={{0,16},{4,20},{8,24},{12,28},{16,0},{20,4},{24,8},{28,12},{1,17},{... | collective-permute-start | bytes 3145736 | tf_op jit(solution)/shard_map/ppermute | solution.py:26
  990.9 38.6 %collective-permute-start.71 = (bf16[256,2048]{1,0:T(8,128)(2,1)}, bf16[256,2048]{1,0:T(8,128)(2,1)}, u32[]{:S(2)}, u32[]{:S(2)}) collective-permute-start(bf16[256,2048]{1,0:T(8,128)(2,1)} %pad_maximum_fusion.12), channel_id=1, source_target_pairs={{0,8},{4,12},{8,0},{12,4},{16,24},{20,28},{24,16},{28,20},{1,9},{5... | collective-permute-start | bytes 3145736 | tf_op jit(solution)/shard_map/ppermute | solution.py:26
  (112 other events, 1461.5 us)
Sparse Core Ops, SparseCore 0:
  32.4 63.7 all-gather.10
  97.8 26.5 all-gather.6
  172.4 81.9 all-gather.8
  286.6 82.0 all-gather.12
  603.3 79.3 reduce-scatter.8
  691.1 79.4 reduce-scatter.10
  775.0 77.1 reduce-scatter.14
  882.9 35.4 reduce-scatter.16
  938.6 50.6 reduce-scatter.18
  992.1 60.6 reduce-scatter.12

commit v3 on v2

--- a/solution.py
+++ b/solution.py
@@ -17,7 +17,7 @@
 FACTOR = HEAD_DIM ** (-0.5)
 BF = jnp.bfloat16
 F32 = jnp.float32
-HASTE = 3
+SCALE = 4
 VMEM_LIMIT = 56 * 1024 * 1024
 
 
@@ -225,7 +225,7 @@
 
 def cost(flops, moved, special=0):
     return pl.CostEstimate(
-        flops=int(flops) // HASTE, bytes_accessed=int(moved) // HASTE, transcendentals=int(special) // HASTE
+        flops=int(flops * SCALE), bytes_accessed=int(moved * SCALE), transcendentals=int(special * SCALE)
     )
 
 

time: 1100 us -> 1040 us (0.945)
  waiting for transfers between devices: 232 us -> 184 us
    ppermute x71, waiting for transfers between devices: 161 us -> 109 us  [swap(): return lax.ppermute(block, 'seq', [(i, i ^ bit) for i in range(size)])]
    all_to_all x1, waiting for transfers between devices: 12.4 us -> 24.4 us  [swapped(): return lax.all_to_all(sent, 'seq', 0, 0, tiled=True).reshape(width, units)]
    unnamed x187 -> x183, local copies, waits for them, and re-layouts: 31.3 us -> 29.2 us
  transfers between devices with their start and end apart: 94 -> 94, of which waited for: 41 -> 28; matrix products, arithmetic and copies ran while one was open for 15% -> 16% of each run, Pallas kernels for 39% -> 48%
where the time goes in v3:
time: 1040 us; the launch traced here: 1030 us
  Pallas kernels  494 us (48%)
  waiting for transfers between devices  184 us (18%)
  other arithmetic  112 us (11%)
  starting transfers between devices  111 us (11%)
  local copies, waits for them, and re-layouts  84.6 us (8%)
  blocking collectives  27.7 us (3%)
  between operations  20 us (2%)
    ppermute x71, waiting for transfers between devices, swap(): return lax.ppermute(block, 'seq', [(i, i ^ bit) for i in range(size)])  109 us
    pallas_call x4, Pallas kernels, ffn_out(): pl.pallas_call(ffn_out_kernel, grid=(here // tile,), in_specs=[out, out,...  71.1 us
    pallas_call x3, Pallas kernels, weight_grad(): pl.pallas_call(partial(grads_kernel, weights is not None), grid=(width //...  69.1 us
    ppermute x71, starting transfers between devices, swap(): return lax.ppermute(block, 'seq', [(i, i ^ bit) for i in range(size)])  66.5 us
    pallas_call x2, Pallas kernels, attend_back(): pl.pallas_call(attend_back_kernel, grid_spec=pltpu.PrefetchScalarGridSpec...  65.2 us
    pallas_call x4, Pallas kernels, ffn_in(): pl.pallas_call(partial(ffn_in_kernel, given), grid=(here // tile,), in_sp...  56 us
    pallas_call x2, Pallas kernels, attend(): pl.pallas_call(attend_kernel, grid_spec=pltpu.PrefetchScalarGridSpec(num_...  52.9 us
    pallas_call x4, Pallas kernels, project(): pl.pallas_call(qkv_kernel, grid_spec=pltpu.PrefetchScalarGridSpec(num_sca...  34.3 us
  transfers between devices with their start and end apart: 94, of which 28 were waited for; matrix products, arithmetic and copies ran while one was open for 16% of the time, Pallas kernels for 48%

profile of v3, /device:TPU:0, one launch (start us, length us, event | category | flops | bytes accessed | tf_op | source)
XLA Modules:
  0.0 1033.1 jit_solution(2302895444493374995)
XLA Ops:
  9.7 5.3 all-to-all-start
  15.8 14.8 %all_gather.23 = bf16[3,2048]{1,0:T(4,128)(2,1)S(1)} all-gather(bf16[3,256]{1,0:T(4,128)(2,1)S(1)} %copy-done.74), channel_id=1, replica_groups=mesh['seq'=8,'tensor'=4] {'seq'}, dimensions={1}, use_global_device_ids=true | all-gather | bytes 13824 | tf_op jit(solution)/shard_map/all_gather | solution.py:1069
  36.0 3.6 collective-permute-start.2
  45.7 13.8 %collective-permute-done.refs_2_ = bf16[256,2048]{1,0:T(8,128)(2,1)} collective-permute-done((bf16[256,2048]{1,0:T(8,128)(2,1)S(1)}, bf16[256,2048]{1,0:T(8,128)(2,1)}, u32[]{:S(2)}, u32[]{:S(2)}) %collective-permute-start) | collective-permute-done | bytes 1048608 | tf_op jit(solution)/shard_map/ppermute | solution.py:26
  64.0 8.3 power_multiply_fusion
  80.4 4.0 convert_reduce_fusion
  85.1 3.6 all-to-all-start.2
  99.1 5.4 all-to-all-done.2
  113.4 24.4 %all-to-all-done.1 = bf16[8,256,256]{2,1,0:T(8,128)(2,1)S(1)} async-done(((bf16[8,256,256]{2,1,0:T(8,128)(2,1)}), bf16[8,256,256]{2,1,0:T(8,128)(2,1)S(1)}, u32[]{:S(2)}, u32[]{:S(2)}) %all-to-all-start.1) | async-done | bytes 1048608 | tf_op jit(solution)/shard_map/all_to_all | solution.py:1092
  137.8 5.7 arrange.1
  150.1 8.6 project.4
  161.6 8.6 project.5
  175.2 26.6 %attend.2 = (f32[2048,256]{1,0:T(8,128)}, bf16[2048,256]{1,0:T(8,128)(2,1)}, f32[2048,4]{1,0:T(8,128)}) custom-call(s32[8]{0:T(128)} %get-tuple-element.328.first, bf16[2048,256]{1,0:T(8,128)(2,1)} %get-tuple-element.203.q_ref, bf16[2048,256]{1,0:T(8,128)(2,1)} %get-tuple-element.206.k_ref, bf16[2048,256]{1,0:T(8,128)(2,1)} %get-tuple-element.207.v_ref, ...), custom_call_target="tpu_custom_call" | custom-call | flops 77309411328 | bytes 20971520 | tf_op jit(solution)/shard_map/attend/pallas_call | solution.py:856
  202.7 4.2 all-to-all-start.3
  215.7 8.6 project.6
  224.3 8.6 project.7
  232.9 17.2 %collective-permute-done.16.refs_4_ = bf16[1024,256]{1,0:T(8,128)(2,1)S(1)} collective-permute-done((bf16[1024,256]{1,0:T(8,128)(2,1)S(1)}, bf16[1024,256]{1,0:T(8,128)(2,1)S(1)}, u32[]{:S(2)}, u32[]{:S(2)}) %collective-permute-start.16) | collective-permute-done | bytes 524320 | tf_op jit(solution)/shard_map/ppermute | solution.py:26
  255.0 26.3 %attend.3 = (f32[2048,256]{1,0:T(8,128)}, bf16[2048,256]{1,0:T(8,128)(2,1)}, f32[2048,4]{1,0:T(8,128)}) custom-call(s32[8]{0:T(128)} %get-tuple-element.336.first, bf16[2048,256]{1,0:T(8,128)(2,1)} %get-tuple-element.217.q_ref, bf16[2048,256]{1,0:T(8,128)(2,1)} %get-tuple-element.220.k_ref, bf16[2048,256]{1,0:T(8,128)(2,1)} %get-tuple-element.221.v_ref, ...), custom_call_target="tpu_custom_call" | custom-call | flops 77309411328 | bytes 20971520 | tf_op jit(solution)/shard_map/attend/pallas_call | solution.py:856
  285.0 13.0 %out_project.2 = (bf16[8,256,256]{2,1,0:T(8,128)(2,1)}, f32[256,2048]{1,0:T(8,128)}, bf16[256,2048]{1,0:T(8,128)(2,1)}) custom-call(s32[8]{0:T(128)} %copy-done.75, bf16[8,256,256]{2,1,0:T(8,128)(2,1)} %all-to-all-done.3.came_ref, bf16[4,4,8,64,256]{4,3,2,1,0:T(8,128)(2,1)} %bitcast.213, bf16[4,4,8,64,256]{4,3,2,1,0:T(8,128)(2,1)} %bitcast.21.odd_ref, ...), custom_call_target="tpu_custom_call" | custom-call | flops 8589934592 | bytes 58720256 | tf_op jit(solution)/shard_map/out_project/pallas_call | solution.py:436
  303.0 3.6 all-to-all-start.4
  310.8 11.6 %all-to-all-done.4.came_ref = bf16[8,256,256]{2,1,0:T(8,128)(2,1)S(1)} async-done(((bf16[8,256,256]{2,1,0:T(8,128)(2,1)}), bf16[8,256,256]{2,1,0:T(8,128)(2,1)S(1)}, u32[]{:S(2)}, u32[]{:S(2)}) %all-to-all-start.4) | async-done | bytes 1048608 | tf_op jit(solution)/shard_map/all_to_all | solution.py:1132
  323.4 13.0 %out_project.3 = (bf16[8,256,256]{2,1,0:T(8,128)(2,1)}, f32[256,2048]{1,0:T(8,128)}, bf16[256,2048]{1,0:T(8,128)(2,1)}) custom-call(s32[8]{0:T(128)} %copy-done.75, bf16[8,256,256]{2,1,0:T(8,128)(2,1)} %copy-done.31, bf16[4,4,8,64,256]{4,3,2,1,0:T(8,128)(2,1)} %bitcast.214, bf16[4,4,8,64,256]{4,3,2,1,0:T(8,128)(2,1)} %bitcast.21.odd_ref, ...), custom_call_target="tpu_custom_call" | custom-call | flops 8589934592 | bytes 58720256 | tf_op jit(solution)/shard_map/out_project/pallas_call | solution.py:436
  336.5 8.7 ffn_grad.2.refs_1_.t_ref
  346.4 8.7 ffn_grad.3.refs_1_.t_ref
  367.3 21.9 %collective-permute-done.28.refs_2_ = bf16[256,2048]{1,0:T(8,128)(2,1)S(1)} collective-permute-done((bf16[256,2048]{1,0:T(8,128)(2,1)S(1)}, bf16[256,2048]{1,0:T(8,128)(2,1)S(1)}, u32[]{:S(2)}, u32[]{:S(2)}) %collective-permute-start.28) | collective-permute-done | bytes 1048608 | tf_op jit(solution)/shard_map/ppermute | solution.py:26
  394.1 11.1 %ffn_in.4 = (f32[1024,1024]{1,0:T(8,128)}, bf16[1024,1024]{1,0:T(8,128)(2,1)}, f32[1024,4]{1,0:T(8,128)}) custom-call(bf16[1024,2048]{1,0:T(8,128)(2,1)} %join.11.refs_0_.refs_4_, bf16[1024,1024]{1,0:T(8,128)(2,1)} %ffn_grad.2.refs_1_.t_ref, bf16[4,2048,256]{2,1,0:T(8,128)(2,1)} %bitcast.274), custom_call_target="tpu_custom_call" | custom-call | flops 17179869184 | bytes 100663296 | tf_op jit(solution)/shard_map/ffn_in/pallas_call | solution.py:632
  405.2 6.5 collective-permute-done.33.refs_2_
  415.0 8.5 collective-permute-done.31.refs_4_
  427.8 11.2 %ffn_in.5 = (f32[1024,1024]{1,0:T(8,128)}, bf16[1024,1024]{1,0:T(8,128)(2,1)}, f32[1024,4]{1,0:T(8,128)}) custom-call(bf16[1024,2048]{1,0:T(8,128)(2,1)} %collective-permute-done.29.refs_0_.refs_5_, bf16[1024,1024]{1,0:T(8,128)(2,1)} %ffn_grad.3.refs_1_.t_ref, bf16[4,2048,256]{2,1,0:T(8,128)(2,1)} %bitcast.275), custom_call_target="tpu_custom_call" | custom-call | flops 17179869184 | bytes 100663296 | tf_op jit(solution)/shard_map/ffn_in/pallas_call | solution.py:632
  445.0 17.1 %ffn_in.6 = (f32[1024,1024]{1,0:T(8,128)}, bf16[1024,1024]{1,0:T(8,128)(2,1)}, f32[1024,4]{1,0:T(8,128)}, bf16[1024,1024]{1,0:T(8,128)(2,1)}) custom-call(bf16[1024,2048]{1,0:T(8,128)(2,1)} %join.13.refs_0_.refs_6_, bf16[1024,2048]{1,0:T(8,128)(2,1)} %join.12.refs_1_.refs_6_, bf16[4,2048,256]{2,1,0:T(8,128)(2,1)} %bitcast.276, ...), custom_call_target="tpu_custom_call" | custom-call | flops 34359738368 | bytes 100663296 | tf_op jit(solution)/shard_map/ffn_in/pallas_call | solution.py:632
  464.3 16.7 %ffn_in.7 = (f32[1024,1024]{1,0:T(8,128)}, bf16[1024,1024]{1,0:T(8,128)(2,1)}, f32[1024,4]{1,0:T(8,128)}, bf16[1024,1024]{1,0:T(8,128)(2,1)}) custom-call(bf16[1024,2048]{1,0:T(8,128)(2,1)} %collective-permute-done.38.refs_0_.refs_7_, bf16[1024,2048]{1,0:T(8,128)(2,1)} %collective-permute-done.39.refs_1_.refs_7_, bf16[4,2048,256]{2,1,0:T(8,128)(2,1)} %bitcast.277, ...), custom_call_target="tpu_custom_call" | custom-call | flops 34359738368 | bytes 100663296 | tf_op jit(solution)/shard_map/ffn_in/pallas_call | solution.py:632
  487.9 17.7 %ffn_out.4 = (bf16[1024,1024]{1,0:T(8,128)(2,1)}, bf16[1024,1024]{1,0:T(8,128)(2,1)}, bf16[1024,2048]{1,0:T(8,128)(2,1)}, bf16[1024,2048]{1,0:T(8,128)(2,1)}, f32[1,1024]{1,0:T(1,128)}) custom-call(f32[1024,1024]{1,0:T(8,128)} %get-tuple-element.264.a_ref, bf16[1024,1024]{1,0:T(8,128)(2,1)} %get-tuple-element.265.p_ref, ...), custom_call_target="tpu_custom_call" | custom-call | flops 34359738368 | bytes 117440512 | tf_op jit(solution)/shard_map/ffn_out/pallas_call | solution.py:685
  506.7 18.0 %ffn_out.5 = (bf16[1024,1024]{1,0:T(8,128)(2,1)}, bf16[1024,1024]{1,0:T(8,128)(2,1)}, bf16[1024,2048]{1,0:T(8,128)(2,1)}, bf16[1024,2048]{1,0:T(8,128)(2,1)}, f32[1,1024]{1,0:T(1,128)}) custom-call(f32[1024,1024]{1,0:T(8,128)} %get-tuple-element.247.a_ref, bf16[1024,1024]{1,0:T(8,128)(2,1)} %get-tuple-element.248.p_ref, ...), custom_call_target="tpu_custom_call" | custom-call | flops 34359738368 | bytes 117440512 | tf_op jit(solution)/shard_map/ffn_out/pallas_call | solution.py:685
  534.9 17.7 %ffn_out.6 = (bf16[1024,1024]{1,0:T(8,128)(2,1)}, bf16[1024,1024]{1,0:T(8,128)(2,1)}, bf16[1024,2048]{1,0:T(8,128)(2,1)}, bf16[1024,2048]{1,0:T(8,128)(2,1)}, f32[1,1024]{1,0:T(1,128)}) custom-call(f32[1024,1024]{1,0:T(8,128)} %get-tuple-element.279.a_ref, bf16[1024,1024]{1,0:T(8,128)(2,1)} %get-tuple-element.280.p_ref, ...), custom_call_target="tpu_custom_call" | custom-call | flops 34359738368 | bytes 117440512 | tf_op jit(solution)/shard_map/ffn_out/pallas_call | solution.py:685
  558.3 17.8 %ffn_out.7 = (bf16[1024,1024]{1,0:T(8,128)(2,1)}, bf16[1024,1024]{1,0:T(8,128)(2,1)}, bf16[1024,2048]{1,0:T(8,128)(2,1)}, bf16[1024,2048]{1,0:T(8,128)(2,1)}, f32[1,1024]{1,0:T(1,128)}) custom-call(f32[1024,1024]{1,0:T(8,128)} %get-tuple-element.273.a_ref, bf16[1024,1024]{1,0:T(8,128)(2,1)} %get-tuple-element.274.p_ref, ...), custom_call_target="tpu_custom_call" | custom-call | flops 34359738368 | bytes 117440512 | tf_op jit(solution)/shard_map/ffn_out/pallas_call | solution.py:685
  576.1 5.7 collective-permute-done.50
  582.7 3.9 add_add_fusion.1.grad_ref
  591.7 24.5 %weight_grad.3 = bf16[1024,2048]{1,0:T(8,128)(2,1)} custom-call(bf16[1024,1024]{1,0:T(8,128)(2,1)} %get-tuple-element.294.refs_0_, bf16[1024,1024]{1,0:T(8,128)(2,1)} %get-tuple-element.296.refs_1_, bf16[1024,1024]{1,0:T(8,128)(2,1)} %get-tuple-element.298.refs_2_, bf16[1024,1024]{1,0:T(8,128)(2,1)} %get-tuple-element.300.refs_3_, ...), custom_call_target="tpu_custom_call" | custom-call | flops 68719476736 | bytes 117440512 | tf_op jit(solution)/shard_map/weight_grad/pallas_call | solution.py:763
  624.2 16.2 %out_back.2 = (f32[256,2048]{1,0:T(8,128)}, bf16[256,2048]{1,0:T(8,128)(2,1)}, bf16[8,256,256]{2,1,0:T(8,128)(2,1)}, f32[1,2048]{1,0:T(1,128)}, f32[8,1,256]{2,1,0:T(1,128)}) custom-call(s32[8]{0:T(128)} %copy-done.75, f32[256,2048]{1,0:T(8,128)} %add_add_fusion.1.grad_ref, f32[256,2048]{1,0:T(8,128)} %get-tuple-element.227.res_ref, ...), custom_call_target="tpu_custom_call" | custom-call | flops 8589934592 | bytes 75497472 | tf_op jit(solution)/shard_map/out_back/pallas_call | solution.py:533
  649.4 24.8 %weight_grad.4 = bf16[1024,2048]{1,0:T(8,128)(2,1)} custom-call(bf16[1024,1024]{1,0:T(8,128)(2,1)} %get-tuple-element.308.refs_0_, bf16[1024,1024]{1,0:T(8,128)(2,1)} %get-tuple-element.310.refs_1_, bf16[1024,1024]{1,0:T(8,128)(2,1)} %get-tuple-element.312.refs_2_, bf16[1024,1024]{1,0:T(8,128)(2,1)} %get-tuple-element.314.refs_3_, ...), custom_call_target="tpu_custom_call" | custom-call | flops 68719476736 | bytes 117440512 | tf_op jit(solution)/shard_map/weight_grad/pallas_call | solution.py:763
  685.9 4.2 add_add_fusion.grad_ref
  690.1 16.2 %out_back.3 = (f32[256,2048]{1,0:T(8,128)}, bf16[256,2048]{1,0:T(8,128)(2,1)}, bf16[8,256,256]{2,1,0:T(8,128)(2,1)}, f32[1,2048]{1,0:T(1,128)}, f32[8,1,256]{2,1,0:T(1,128)}) custom-call(s32[8]{0:T(128)} %copy-done.75, f32[256,2048]{1,0:T(8,128)} %add_add_fusion.grad_ref, f32[256,2048]{1,0:T(8,128)} %get-tuple-element.234.res_ref, ...), custom_call_target="tpu_custom_call" | custom-call | flops 8589934592 | bytes 75497472 | tf_op jit(solution)/shard_map/out_back/pallas_call | solution.py:533
  709.9 10.7 %out_grad.1 = bf16[8,4,8,64,256]{4,3,2,1,0:T(8,128)(2,1)} custom-call(bf16[8,256,256]{2,1,0:T(8,128)(2,1)} %get-tuple-element.321.refs_0_, bf16[8,256,256]{2,1,0:T(8,128)(2,1)} %get-tuple-element.323.refs_1_, bf16[256,2048]{1,0:T(8,128)(2,1)} %get-tuple-element.324.refs_2_, bf16[256,2048]{1,0:T(8,128)(2,1)} %get-tuple-element.325.refs_3_), custom_call_target="tpu_custom_call" | custom-call | flops 17179869184 | bytes 50331648 | tf_op jit(solution)/shard_map/out_grad/pallas_call | solution.py:351
  726.0 31.6 %attend_back.2.x_ref.refs_0_.refs_1_ = bf16[2048,768]{1,0:T(8,128)(2,1)} custom-call(s32[8]{0:T(128)} %get-tuple-element.328.first, s32[8]{0:T(128)} %shift-right-arithmetic_add_fusion.spot, bf16[2048,256]{1,0:T(8,128)(2,1)} %get-tuple-element.203.q_ref, bf16[2048,256]{1,0:T(8,128)(2,1)} %get-tuple-element.206.k_ref, ...), custom_call_target="tpu_custom_call" | custom-call | flops 103079215104 | bytes 41943040 | tf_op jit(solution)/shard_map/attend_back/pallas_call | solution.py:972
  762.7 7.7 multiply.81
  777.3 7.3 multiply.82
  787.6 33.6 %attend_back.3.x_ref.refs_2_.refs_3_ = bf16[2048,768]{1,0:T(8,128)(2,1)} custom-call(s32[8]{0:T(128)} %get-tuple-element.336.first, s32[8]{0:T(128)} %shift-right-arithmetic_add_fusion.spot, bf16[2048,256]{1,0:T(8,128)(2,1)} %get-tuple-element.217.q_ref, bf16[2048,256]{1,0:T(8,128)(2,1)} %get-tuple-element.220.k_ref, ...), custom_call_target="tpu_custom_call" | custom-call | flops 103079215104 | bytes 41943040 | tf_op jit(solution)/shard_map/attend_back/pallas_call | solution.py:972
  826.0 7.5 multiply.83
  845.8 4.1 all-to-all-start.9
  850.0 7.4 multiply.84
  860.3 19.8 %weight_grad.5 = (bf16[768,2048]{1,0:T(8,128)(2,1)}, f32[1,2048]{1,0:T(1,128)}) custom-call(bf16[2048,768]{1,0:T(8,128)(2,1)} %attend_back.2.x_ref.refs_0_.refs_1_, bf16[2048,768]{1,0:T(8,128)(2,1)} %attend_back.2.x_ref.refs_0_.refs_1_, bf16[2048,768]{1,0:T(8,128)(2,1)} %attend_back.3.x_ref.refs_2_.refs_3_, ...), custom_call_target="tpu_custom_call" | custom-call | flops 51539607552 | bytes 104857600 | tf_op jit(solution)/shard_map/weight_grad/pallas_call | solution.py:763
  894.0 3.7 fusion.24
  898.7 6.7 all-to-all-done.9
  910.0 3.6 fusion.25
  921.6 7.0 all-to-all-done.8
  931.8 8.6 collective-permute-done.70
  940.4 3.6 add_convert_fusion.5
  954.7 12.9 %all-reduce.1 = (f32[3,256]{1,0:T(4,128)S(1)}, f32[4,256]{1,0:T(4,128)S(1)}) all-reduce(f32[3,256]{1,0:T(4,128)S(1)} %copy.279, f32[4,256]{1,0:T(4,128)S(1)} %reshape.402), channel_id=1, replica_groups=mesh['seq'=8,'tensor'=4] {'tensor'}, use_global_device_ids=true, to_apply=%region_17.18 | all-reduce | flops 1792 | bytes 14336 | tf_op jit(solution)/shard_map/psum | solution.py:1358
  970.6 14.2 %collective-permute-done.73 = bf16[256,2048]{1,0:T(8,128)(2,1)} collective-permute-done((bf16[256,2048]{1,0:T(8,128)(2,1)}, bf16[256,2048]{1,0:T(8,128)(2,1)}, u32[]{:S(2)}, u32[]{:S(2)}) %collective-permute-start.73) | collective-permute-done | bytes 1048608 | tf_op jit(solution)/shard_map/ppermute | solution.py:26
  985.0 5.5 fusion.31
  990.5 8.1 reduce-scatter.13.cloned.1.call-done
  1001.0 4.2 all-to-all-start.7
  1005.2 4.2 fusion.9
  1011.7 6.1 all-to-all-done.7
  (510 shorter events, 279.8 us)
Async XLA Ops:
  15.0 122.8 %all-gather.11.cloned.1.call-start = ((), (), s32[]{:S(2)}) async-start(), calls=%async_computation.23 | async-start | bytes 3932160 | tf_op jit(solution)/shard_map/all_gather | solution.py:1080
  33.9 25.6 %collective-permute-start = (bf16[256,2048]{1,0:T(8,128)(2,1)S(1)}, bf16[256,2048]{1,0:T(8,128)(2,1)}, u32[]{:S(2)}, u32[]{:S(2)}) collective-permute-start(bf16[256,2048]{1,0:T(8,128)(2,1)S(1)} %get-tuple-element.188.refs_0_), channel_id=1, source_target_pairs={{0,16},{4,20},{8,24},{12,28},{16,0},{20,4},{24,8},{28,12},{1,17},{... | collective-permute-start | bytes 3145736 | tf_op jit(solution)/shard_map/ppermute | solution.py:26
  34.5 25.2 %collective-permute-start.1 = (bf16[256,2048]{1,0:T(8,128)(2,1)S(1)}, bf16[256,2048]{1,0:T(8,128)(2,1)}, u32[]{:S(2)}, u32[]{:S(2)}) collective-permute-start(bf16[256,2048]{1,0:T(8,128)(2,1)S(1)} %get-tuple-element.188.refs_0_), channel_id=1, source_target_pairs={{0,8},{4,12},{8,0},{12,4},{16,24},{20,28},{24,16},{28,20},{1,9},{5... | collective-permute-start | bytes 3145736 | tf_op jit(solution)/shard_map/ppermute | solution.py:26
  80.4 81.2 %collective-permute-start.9 = (bf16[1024,2048]{1,0:T(8,128)(2,1)}, bf16[1024,2048]{1,0:T(8,128)(2,1)}, u32[]{:S(2)}, u32[]{:S(2)}) collective-permute-start(bf16[1024,2048]{1,0:T(8,128)(2,1)} %join.7.x_ref.refs_4_), channel_id=1, source_target_pairs={{0,4},{4,0},{8,12},{12,8},{16,20},{20,16},{24,28},{28,24},{1,5},{5... | collective-permute-start | bytes 12582920 | tf_op jit(solution)/shard_map/ppermute | solution.py:26
  90.3 53.1 %collective-permute-start.8 = (bf16[256,2048]{1,0:T(8,128)(2,1)}, bf16[256,2048]{1,0:T(8,128)(2,1)}, u32[]{:S(2)}, u32[]{:S(2)}) collective-permute-start(bf16[256,2048]{1,0:T(8,128)(2,1)} %get-tuple-element.204.refs_0_), channel_id=1, source_target_pairs={{0,16},{4,20},{8,24},{12,28},{16,0},{20,4},{24,8},{28,12},{1,17},{... | collective-permute-start | bytes 3145736 | tf_op jit(solution)/shard_map/ppermute | solution.py:26
  92.3 51.2 %collective-permute-start.7 = (bf16[256,2048]{1,0:T(8,128)(2,1)}, bf16[256,2048]{1,0:T(8,128)(2,1)}, u32[]{:S(2)}, u32[]{:S(2)}) collective-permute-start(bf16[256,2048]{1,0:T(8,128)(2,1)} %get-tuple-element.204.refs_0_), channel_id=1, source_target_pairs={{0,8},{4,12},{8,0},{12,4},{16,24},{20,28},{24,16},{28,20},{1,9},{5... | collective-permute-start | bytes 3145736 | tf_op jit(solution)/shard_map/ppermute | solution.py:26
  104.5 33.3 %all-to-all-start.1 = ((bf16[8,256,256]{2,1,0:T(8,128)(2,1)}), bf16[8,256,256]{2,1,0:T(8,128)(2,1)S(1)}, u32[]{:S(2)}, u32[]{:S(2)}) async-start(bf16[8,256,256]{2,1,0:T(8,128)(2,1)} %copy.245), calls=%async_computation.1 | async-start | bytes 2097152 | tf_op jit(solution)/shard_map/all_to_all | solution.py:1092
  108.1 50.6 %all-gather.7.cloned.1.call-start = ((), (), s32[]{:S(2)}) async-start(), calls=%async_computation.16 | async-start | bytes 1310720 | tf_op jit(solution)/shard_map/all_gather | solution.py:1087
  110.9 225.6 %all-gather.9.cloned.1.call-start = ((), (), s32[]{:S(2)}) async-start(), calls=%async_computation.17 | async-start | bytes 5242880 | tf_op jit(solution)/shard_map/all_gather | solution.py:1169
  158.6 48.3 %collective-permute-start.13 = (bf16[2048,256]{1,0:T(8,128)(2,1)}, bf16[2048,256]{1,0:T(8,128)(2,1)}, u32[]{:S(2)}, u32[]{:S(2)}) collective-permute-start(bf16[2048,256]{1,0:T(8,128)(2,1)} %all-gather.7.cloned.1.call-done.refs_0_), channel_id=1, source_target_pairs={{0,16},{4,20},{8,24},{12,28},{16,0},{20,4},{24,8},{28,12},{1,17},{... | collective-permute-start | bytes 3145736 | tf_op jit(solution)/shard_map/ppermute | solution.py:26
  160.0 47.0 %collective-permute-start.12 = (bf16[2048,256]{1,0:T(8,128)(2,1)}, bf16[2048,256]{1,0:T(8,128)(2,1)}, u32[]{:S(2)}, u32[]{:S(2)}) collective-permute-start(bf16[2048,256]{1,0:T(8,128)(2,1)} %all-gather.7.cloned.1.call-done.refs_0_), channel_id=1, source_target_pairs={{0,8},{4,12},{8,0},{12,4},{16,24},{20,28},{24,16},{28,20},{1,9},{5... | collective-permute-start | bytes 3145736 | tf_op jit(solution)/shard_map/ppermute | solution.py:26
  175.1 49.2 %collective-permute-start.14 = (bf16[1024,2048]{1,0:T(8,128)(2,1)}, bf16[1024,2048]{1,0:T(8,128)(2,1)}, u32[]{:S(2)}, u32[]{:S(2)}) collective-permute-start(bf16[1024,2048]{1,0:T(8,128)(2,1)} %join.8.x_ref.refs_6_), channel_id=1, source_target_pairs={{0,4},{4,0},{8,12},{12,8},{16,20},{20,16},{24,28},{28,24},{1,5},{5... | collective-permute-start | bytes 12582920 | tf_op jit(solution)/shard_map/ppermute | solution.py:26
  201.8 79.5 %collective-permute-start.18 = (bf16[256,2048]{1,0:T(8,128)(2,1)S(1)}, bf16[256,2048]{1,0:T(8,128)(2,1)S(1)}, u32[]{:S(2)}, u32[]{:S(2)}) collective-permute-start(bf16[256,2048]{1,0:T(8,128)(2,1)S(1)} %get-tuple-element.230.refs_0_.cot_ref), channel_id=1, source_target_pairs={{0,16},{4,20},{8,24},{12,28},{16,0},{20,4},{24,8},{28,12},{1,17},{... | collective-permute-start | bytes 3145736 | tf_op jit(solution)/shard_map/ppermute | solution.py:26
  202.1 79.2 %collective-permute-start.17 = (bf16[256,2048]{1,0:T(8,128)(2,1)S(1)}, bf16[256,2048]{1,0:T(8,128)(2,1)S(1)}, u32[]{:S(2)}, u32[]{:S(2)}) collective-permute-start(bf16[256,2048]{1,0:T(8,128)(2,1)S(1)} %get-tuple-element.230.refs_0_.cot_ref), channel_id=1, source_target_pairs={{0,8},{4,12},{8,0},{12,4},{16,24},{20,28},{24,16},{28,20},{1,9},{5... | collective-permute-start | bytes 3145736 | tf_op jit(solution)/shard_map/ppermute | solution.py:26
  202.7 82.3 %all-to-all-start.3 = ((bf16[8,256,256]{2,1,0:T(8,128)(2,1)}), bf16[8,256,256]{2,1,0:T(8,128)(2,1)}, u32[]{:S(2)}, u32[]{:S(2)}) async-start(bf16[8,256,256]{2,1,0:T(8,128)(2,1)} %bitcast.232), calls=%async_computation.3 | async-start | bytes 2097152 | tf_op jit(solution)/shard_map/all_to_all | solution.py:1132
  209.1 40.9 %collective-permute-start.16 = (bf16[1024,256]{1,0:T(8,128)(2,1)S(1)}, bf16[1024,256]{1,0:T(8,128)(2,1)S(1)}, u32[]{:S(2)}, u32[]{:S(2)}) collective-permute-start(bf16[1024,256]{1,0:T(8,128)(2,1)S(1)} %slice.530), channel_id=1, source_target_pairs={{0,8},{4,12},{8,0},{12,4},{16,24},{20,28},{24,16},{28,20},{1,9},{5... | collective-permute-start | bytes 1572872 | tf_op jit(solution)/shard_map/ppermute | solution.py:26
  211.1 39.0 %collective-permute-start.15 = (bf16[1024,256]{1,0:T(8,128)(2,1)S(1)}, bf16[1024,256]{1,0:T(8,128)(2,1)S(1)}, u32[]{:S(2)}, u32[]{:S(2)}) collective-permute-start(bf16[1024,256]{1,0:T(8,128)(2,1)S(1)} %slice.529), channel_id=1, source_target_pairs={{0,16},{4,20},{8,24},{12,28},{16,0},{20,4},{24,8},{28,12},{1,17},{... | collective-permute-start | bytes 1572872 | tf_op jit(solution)/shard_map/ppermute | solution.py:26
  254.9 30.1 %collective-permute-start.19 = (bf16[8192,256]{1,0:T(8,128)(2,1)}, bf16[8192,256]{1,0:T(8,128)(2,1)}, u32[]{:S(2)}, u32[]{:S(2)}) collective-permute-start(bf16[8192,256]{1,0:T(8,128)(2,1)} %join.9), channel_id=1, source_target_pairs={{0,4},{4,0},{8,12},{12,8},{16,20},{20,16},{24,28},{28,24},{1,5},{5... | collective-permute-start | bytes 12582920 | tf_op jit(solution)/shard_map/ppermute | solution.py:26
  302.9 43.5 %collective-permute-start.22 = (bf16[1024,2048]{1,0:T(8,128)(2,1)}, bf16[1024,2048]{1,0:T(8,128)(2,1)}, u32[]{:S(2)}, u32[]{:S(2)}) collective-permute-start(bf16[1024,2048]{1,0:T(8,128)(2,1)} %join.10.c_ref.refs_4_), channel_id=1, source_target_pairs={{0,4},{4,0},{8,12},{12,8},{16,20},{20,16},{24,28},{28,24},{1,5},{5... | collective-permute-start | bytes 12582920 | tf_op jit(solution)/shard_map/ppermute | solution.py:26
  306.5 87.5 %all-gather.13.cloned.1.call-start = ((), (), s32[]{:S(2)}) async-start(), calls=%async_computation.24 | async-start | bytes 5242880 | tf_op jit(solution)/shard_map/all_gather | solution.py:1160
  307.1 455.5 %reduce-scatter.9.cloned.1.call-start = ((), (), s32[]{:S(2)}) async-start(), calls=%async_computation.18 | async-start | bytes 5242880 | tf_op jit(solution)/shard_map/reduce_scatter | solution.py:1260
  307.4 37.8 %collective-permute-start.24 = (bf16[256,2048]{1,0:T(8,128)(2,1)}, bf16[256,2048]{1,0:T(8,128)(2,1)S(1)}, u32[]{:S(2)}, u32[]{:S(2)}) collective-permute-start(bf16[256,2048]{1,0:T(8,128)(2,1)} %get-tuple-element.242.refs_0_), channel_id=1, source_target_pairs={{0,16},{4,20},{8,24},{12,28},{16,0},{20,4},{24,8},{28,12},{1,17},{... | collective-permute-start | bytes 3145736 | tf_op jit(solution)/shard_map/ppermute | solution.py:26
  309.4 35.8 %collective-permute-start.23 = (bf16[256,2048]{1,0:T(8,128)(2,1)}, bf16[256,2048]{1,0:T(8,128)(2,1)S(1)}, u32[]{:S(2)}, u32[]{:S(2)}) collective-permute-start(bf16[256,2048]{1,0:T(8,128)(2,1)} %get-tuple-element.242.refs_0_), channel_id=1, source_target_pairs={{0,8},{4,12},{8,0},{12,4},{16,24},{20,28},{24,16},{28,20},{1,9},{5... | collective-permute-start | bytes 3145736 | tf_op jit(solution)/shard_map/ppermute | solution.py:26
  363.1 64.7 %collective-permute-start.29 = (bf16[1024,2048]{1,0:T(8,128)(2,1)}, bf16[1024,2048]{1,0:T(8,128)(2,1)}, u32[]{:S(2)}, u32[]{:S(2)}) collective-permute-start(bf16[1024,2048]{1,0:T(8,128)(2,1)} %join.11.refs_0_.refs_4_), channel_id=1, source_target_pairs={{0,4},{4,0},{8,12},{12,8},{16,20},{20,16},{24,28},{28,24},{1,5},{5... | collective-permute-start | bytes 12582920 | tf_op jit(solution)/shard_map/ppermute | solution.py:26
  363.2 26.0 %collective-permute-start.28 = (bf16[256,2048]{1,0:T(8,128)(2,1)S(1)}, bf16[256,2048]{1,0:T(8,128)(2,1)S(1)}, u32[]{:S(2)}, u32[]{:S(2)}) collective-permute-start(bf16[256,2048]{1,0:T(8,128)(2,1)S(1)} %copy-done.15), channel_id=1, source_target_pairs={{0,16},{4,20},{8,24},{12,28},{16,0},{20,4},{24,8},{28,12},{1,17},{... | collective-permute-start | bytes 3145736 | tf_op jit(solution)/shard_map/ppermute | solution.py:26
  363.8 26.0 %collective-permute-start.27 = (bf16[256,2048]{1,0:T(8,128)(2,1)S(1)}, bf16[256,2048]{1,0:T(8,128)(2,1)S(1)}, u32[]{:S(2)}, u32[]{:S(2)}) collective-permute-start(bf16[256,2048]{1,0:T(8,128)(2,1)S(1)} %copy-done.15), channel_id=1, source_target_pairs={{0,8},{4,12},{8,0},{12,4},{16,24},{20,28},{24,16},{28,20},{1,9},{5... | collective-permute-start | bytes 3145736 | tf_op jit(solution)/shard_map/ppermute | solution.py:26
  364.7 47.0 %collective-permute-start.33 = (bf16[256,2048]{1,0:T(8,128)(2,1)}, bf16[256,2048]{1,0:T(8,128)(2,1)S(1)}, u32[]{:S(2)}, u32[]{:S(2)}) collective-permute-start(bf16[256,2048]{1,0:T(8,128)(2,1)} %get-tuple-element.256.refs_0_), channel_id=1, source_target_pairs={{0,16},{4,20},{8,24},{12,28},{16,0},{20,4},{24,8},{28,12},{1,17},{... | collective-permute-start | bytes 3145736 | tf_op jit(solution)/shard_map/ppermute | solution.py:26
  366.3 45.9 %collective-permute-start.32 = (bf16[256,2048]{1,0:T(8,128)(2,1)}, bf16[256,2048]{1,0:T(8,128)(2,1)S(1)}, u32[]{:S(2)}, u32[]{:S(2)}) collective-permute-start(bf16[256,2048]{1,0:T(8,128)(2,1)} %get-tuple-element.256.refs_0_), channel_id=1, source_target_pairs={{0,8},{4,12},{8,0},{12,4},{16,24},{20,28},{24,16},{28,20},{1,9},{5... | collective-permute-start | bytes 3145736 | tf_op jit(solution)/shard_map/ppermute | solution.py:26
  391.5 32.0 %collective-permute-start.31 = (bf16[128,2048]{1,0:T(8,128)(2,1)}, bf16[128,2048]{1,0:T(8,128)(2,1)S(1)}, u32[]{:S(2)}, u32[]{:S(2)}) collective-permute-start(bf16[128,2048]{1,0:T(8,128)(2,1)} %slice.541), channel_id=1, source_target_pairs={{0,8},{4,12},{8,0},{12,4},{16,24},{20,28},{24,16},{28,20},{1,9},{5... | collective-permute-start | bytes 1572872 | tf_op jit(solution)/shard_map/ppermute | solution.py:26
  392.5 31.0 %collective-permute-start.30 = (bf16[128,2048]{1,0:T(8,128)(2,1)}, bf16[128,2048]{1,0:T(8,128)(2,1)}, u32[]{:S(2)}, u32[]{:S(2)}) collective-permute-start(bf16[128,2048]{1,0:T(8,128)(2,1)} %slice.540), channel_id=1, source_target_pairs={{0,16},{4,20},{8,24},{12,28},{16,0},{20,4},{24,8},{28,12},{1,17},{... | collective-permute-start | bytes 1572872 | tf_op jit(solution)/shard_map/ppermute | solution.py:26
  412.3 26.7 %collective-permute-start.36 = (bf16[128,2048]{1,0:T(8,128)(2,1)S(1)}, bf16[128,2048]{1,0:T(8,128)(2,1)S(1)}, u32[]{:S(2)}, u32[]{:S(2)}) collective-permute-start(bf16[128,2048]{1,0:T(8,128)(2,1)S(1)} %slice.543), channel_id=1, source_target_pairs={{0,8},{4,12},{8,0},{12,4},{16,24},{20,28},{24,16},{28,20},{1,9},{5... | collective-permute-start | bytes 1572872 | tf_op jit(solution)/shard_map/ppermute | solution.py:26
  413.3 25.7 %collective-permute-start.35 = (bf16[128,2048]{1,0:T(8,128)(2,1)S(1)}, bf16[128,2048]{1,0:T(8,128)(2,1)S(1)}, u32[]{:S(2)}, u32[]{:S(2)}) collective-permute-start(bf16[128,2048]{1,0:T(8,128)(2,1)S(1)} %slice.542), channel_id=1, source_target_pairs={{0,16},{4,20},{8,24},{12,28},{16,0},{20,4},{24,8},{28,12},{1,17},{... | collective-permute-start | bytes 1572872 | tf_op jit(solution)/shard_map/ppermute | solution.py:26
  427.7 36.6 %collective-permute-start.39 = (bf16[1024,2048]{1,0:T(8,128)(2,1)}, bf16[1024,2048]{1,0:T(8,128)(2,1)}, u32[]{:S(2)}, u32[]{:S(2)}) collective-permute-start(bf16[1024,2048]{1,0:T(8,128)(2,1)} %join.12.refs_1_.refs_6_), channel_id=1, source_target_pairs={{0,4},{4,0},{8,12},{12,8},{16,20},{20,16},{24,28},{28,24},{1,5},{5... | collective-permute-start | bytes 12582920 | tf_op jit(solution)/shard_map/ppermute | solution.py:26
  527.9 116.1 %collective-permute-start.52 = (bf16[1024,2048]{1,0:T(8,128)(2,1)}, bf16[1024,2048]{1,0:T(8,128)(2,1)}, u32[]{:S(2)}, u32[]{:S(2)}) collective-permute-start(bf16[1024,2048]{1,0:T(8,128)(2,1)} %get-tuple-element.306), channel_id=1, source_target_pairs={{0,4},{4,0},{8,12},{12,8},{16,20},{20,16},{24,28},{28,24},{1,5},{5... | collective-permute-start | bytes 12582920 | tf_op jit(solution)/shard_map/ppermute | solution.py:26
  552.6 34.0 %collective-permute-start.47 = (bf16[1024,2048]{1,0:T(8,128)(2,1)}, bf16[1024,2048]{1,0:T(8,128)(2,1)S(1)}, u32[]{:S(2)}, u32[]{:S(2)}) collective-permute-start(bf16[1024,2048]{1,0:T(8,128)(2,1)} %get-tuple-element.293), channel_id=1, source_target_pairs={{0,4},{4,0},{8,12},{12,8},{16,20},{20,16},{24,28},{28,24},{1,5},{5... | collective-permute-start | bytes 12582920 | tf_op jit(solution)/shard_map/ppermute | solution.py:26
  552.7 167.9 %collective-permute-start.59 = (bf16[1024,2048]{1,0:T(8,128)(2,1)}, bf16[1024,2048]{1,0:T(8,128)(2,1)}, u32[]{:S(2)}, u32[]{:S(2)}) collective-permute-start(bf16[1024,2048]{1,0:T(8,128)(2,1)} %get-tuple-element.327), channel_id=1, source_target_pairs={{0,4},{4,0},{8,12},{12,8},{16,20},{20,16},{24,28},{28,24},{1,5},{5... | collective-permute-start | bytes 12582920 | tf_op jit(solution)/shard_map/ppermute | solution.py:26
  556.6 25.2 %collective-permute-start.50 = (bf16[256,2048]{1,0:T(8,128)(2,1)S(1)}, bf16[256,2048]{1,0:T(8,128)(2,1)S(1)}, u32[]{:S(2)}, u32[]{:S(2)}) collective-permute-start(bf16[256,2048]{1,0:T(8,128)(2,1)S(1)} %pad_maximum_fusion.2), channel_id=1, source_target_pairs={{0,8},{4,12},{8,0},{12,4},{16,24},{20,28},{24,16},{28,20},{1,9},{5... | collective-permute-start | bytes 3145736 | tf_op jit(solution)/shard_map/ppermute | solution.py:26
  557.7 25.0 %collective-permute-start.51 = (bf16[256,2048]{1,0:T(8,128)(2,1)S(1)}, bf16[256,2048]{1,0:T(8,128)(2,1)}, u32[]{:S(2)}, u32[]{:S(2)}) collective-permute-start(bf16[256,2048]{1,0:T(8,128)(2,1)S(1)} %pad_maximum_fusion.3), channel_id=1, source_target_pairs={{0,16},{4,20},{8,24},{12,28},{16,0},{20,4},{24,8},{28,12},{1,17},{... | collective-permute-start | bytes 3145736 | tf_op jit(solution)/shard_map/ppermute | solution.py:26
  590.2 26.0 %collective-permute-start.49 = (bf16[128,2048]{1,0:T(8,128)(2,1)S(1)}, bf16[128,2048]{1,0:T(8,128)(2,1)S(1)}, u32[]{:S(2)}, u32[]{:S(2)}) collective-permute-start(bf16[128,2048]{1,0:T(8,128)(2,1)S(1)} %get-tuple-element.484), channel_id=1, source_target_pairs={{0,8},{4,12},{8,0},{12,4},{16,24},{20,28},{24,16},{28,20},{1,9},{5... | collective-permute-start | bytes 1572872 | tf_op jit(solution)/shard_map/ppermute | solution.py:26
  620.4 65.5 %collective-permute-start.57 = (bf16[256,2048]{1,0:T(8,128)(2,1)}, bf16[256,2048]{1,0:T(8,128)(2,1)}, u32[]{:S(2)}, u32[]{:S(2)}) collective-permute-start(bf16[256,2048]{1,0:T(8,128)(2,1)} %pad_maximum_fusion.4), channel_id=1, source_target_pairs={{0,8},{4,12},{8,0},{12,4},{16,24},{20,28},{24,16},{28,20},{1,9},{5... | collective-permute-start | bytes 3145736 | tf_op jit(solution)/shard_map/ppermute | solution.py:26
  622.7 63.3 %collective-permute-start.58 = (bf16[256,2048]{1,0:T(8,128)(2,1)}, bf16[256,2048]{1,0:T(8,128)(2,1)}, u32[]{:S(2)}, u32[]{:S(2)}) collective-permute-start(bf16[256,2048]{1,0:T(8,128)(2,1)} %pad_maximum_fusion.5), channel_id=1, source_target_pairs={{0,16},{4,20},{8,24},{12,28},{16,0},{20,4},{24,8},{28,12},{1,17},{... | collective-permute-start | bytes 3145736 | tf_op jit(solution)/shard_map/ppermute | solution.py:26
  640.4 39.1 %all-to-all-start.5 = ((bf16[8,256,256]{2,1,0:T(8,128)(2,1)}), bf16[8,256,256]{2,1,0:T(8,128)(2,1)S(1)}, u32[]{:S(2)}, u32[]{:S(2)}) async-start(bf16[8,256,256]{2,1,0:T(8,128)(2,1)} %get-tuple-element.304), calls=%async_computation.5 | async-start | bytes 2097152 | tf_op jit(solution)/shard_map/all_to_all | solution.py:1275
  643.9 182.1 %reduce-scatter.11.cloned.1.call-start = ((), (), s32[]{:S(2)}) async-start(), calls=%async_computation.19 | async-start | bytes 5242880 | tf_op jit(solution)/shard_map/reduce_scatter | solution.py:1311
  646.0 28.2 %collective-permute-start.55 = (bf16[128,2048]{1,0:T(8,128)(2,1)S(1)}, bf16[128,2048]{1,0:T(8,128)(2,1)S(1)}, u32[]{:S(2)}, u32[]{:S(2)}) collective-permute-start(bf16[128,2048]{1,0:T(8,128)(2,1)S(1)} %get-tuple-element.478), channel_id=1, source_target_pairs={{0,8},{4,12},{8,0},{12,4},{16,24},{20,28},{24,16},{28,20},{1,9},{5... | collective-permute-start | bytes 1572872 | tf_op jit(solution)/shard_map/ppermute | solution.py:26
  647.9 26.3 %collective-permute-start.53 = (bf16[128,2048]{1,0:T(8,128)(2,1)S(1)}, bf16[128,2048]{1,0:T(8,128)(2,1)S(1)}, u32[]{:S(2)}, u32[]{:S(2)}) collective-permute-start(bf16[128,2048]{1,0:T(8,128)(2,1)S(1)} %get-tuple-element.479), channel_id=1, source_target_pairs={{0,16},{4,20},{8,24},{12,28},{16,0},{20,4},{24,8},{28,12},{1,17},{... | collective-permute-start | bytes 1572872 | tf_op jit(solution)/shard_map/ppermute | solution.py:26
  706.3 56.3 %all-to-all-start.6 = ((bf16[8,256,256]{2,1,0:T(8,128)(2,1)}), bf16[8,256,256]{2,1,0:T(8,128)(2,1)S(1)}, u32[]{:S(2)}, u32[]{:S(2)}) async-start(bf16[8,256,256]{2,1,0:T(8,128)(2,1)} %get-tuple-element.320), calls=%async_computation.7 | async-start | bytes 2097152 | tf_op jit(solution)/shard_map/all_to_all | solution.py:1275
  709.9 147.5 %reduce-scatter.15.cloned.1.call-start = ((), (), s32[]{:S(2)}) async-start(), calls=%async_computation.21 | async-start | bytes 9437184 | tf_op jit(solution)/shard_map/reduce_scatter | solution.py:1320
  722.5 35.1 %collective-permute-start.60 = (bf16[128,2048]{1,0:T(8,128)(2,1)S(1)}, bf16[128,2048]{1,0:T(8,128)(2,1)S(1)}, u32[]{:S(2)}, u32[]{:S(2)}) collective-permute-start(bf16[128,2048]{1,0:T(8,128)(2,1)S(1)} %get-tuple-element.472), channel_id=1, source_target_pairs={{0,16},{4,20},{8,24},{12,28},{16,0},{20,4},{24,8},{28,12},{1,17},{... | collective-permute-start | bytes 1572872 | tf_op jit(solution)/shard_map/ppermute | solution.py:26
  724.5 33.1 %collective-permute-start.62 = (bf16[128,2048]{1,0:T(8,128)(2,1)S(1)}, bf16[128,2048]{1,0:T(8,128)(2,1)}, u32[]{:S(2)}, u32[]{:S(2)}) collective-permute-start(bf16[128,2048]{1,0:T(8,128)(2,1)S(1)} %get-tuple-element.473), channel_id=1, source_target_pairs={{0,8},{4,12},{8,0},{12,4},{16,24},{20,28},{24,16},{28,20},{1,9},{5... | collective-permute-start | bytes 1572872 | tf_op jit(solution)/shard_map/ppermute | solution.py:26
  786.6 34.6 %collective-permute-start.65 = (bf16[128,2048]{1,0:T(8,128)(2,1)S(1)}, bf16[128,2048]{1,0:T(8,128)(2,1)S(1)}, u32[]{:S(2)}, u32[]{:S(2)}) collective-permute-start(bf16[128,2048]{1,0:T(8,128)(2,1)S(1)} %get-tuple-element.466), channel_id=1, source_target_pairs={{0,16},{4,20},{8,24},{12,28},{16,0},{20,4},{24,8},{28,12},{1,17},{... | collective-permute-start | bytes 1572872 | tf_op jit(solution)/shard_map/ppermute | solution.py:26
  787.5 33.6 %collective-permute-start.67 = (bf16[128,2048]{1,0:T(8,128)(2,1)S(1)}, bf16[128,2048]{1,0:T(8,128)(2,1)S(1)}, u32[]{:S(2)}, u32[]{:S(2)}) collective-permute-start(bf16[128,2048]{1,0:T(8,128)(2,1)S(1)} %get-tuple-element.467), channel_id=1, source_target_pairs={{0,8},{4,12},{8,0},{12,4},{16,24},{20,28},{24,16},{28,20},{1,9},{5... | collective-permute-start | bytes 1572872 | tf_op jit(solution)/shard_map/ppermute | solution.py:26
  840.4 53.6 %collective-permute-start.54 = (bf16[256,2048]{1,0:T(8,128)(2,1)}, bf16[256,2048]{1,0:T(8,128)(2,1)}, u32[]{:S(2)}, u32[]{:S(2)}) collective-permute-start(bf16[256,2048]{1,0:T(8,128)(2,1)} %pad_maximum_fusion.6), channel_id=1, source_target_pairs={{0,8},{4,12},{8,0},{12,4},{16,24},{20,28},{24,16},{28,20},{1,9},{5... | collective-permute-start | bytes 3145736 | tf_op jit(solution)/shard_map/ppermute | solution.py:26
  842.2 51.8 %collective-permute-start.56 = (bf16[256,2048]{1,0:T(8,128)(2,1)}, bf16[256,2048]{1,0:T(8,128)(2,1)}, u32[]{:S(2)}, u32[]{:S(2)}) collective-permute-start(bf16[256,2048]{1,0:T(8,128)(2,1)} %pad_maximum_fusion.7), channel_id=1, source_target_pairs={{0,16},{4,20},{8,24},{12,28},{16,0},{20,4},{24,8},{28,12},{1,17},{... | collective-permute-start | bytes 3145736 | tf_op jit(solution)/shard_map/ppermute | solution.py:26
  843.8 66.2 %collective-permute-start.63 = (bf16[256,2048]{1,0:T(8,128)(2,1)}, bf16[256,2048]{1,0:T(8,128)(2,1)}, u32[]{:S(2)}, u32[]{:S(2)}) collective-permute-start(bf16[256,2048]{1,0:T(8,128)(2,1)} %pad_maximum_fusion.9), channel_id=1, source_target_pairs={{0,16},{4,20},{8,24},{12,28},{16,0},{20,4},{24,8},{28,12},{1,17},{... | collective-permute-start | bytes 3145736 | tf_op jit(solution)/shard_map/ppermute | solution.py:26
  844.6 65.5 %collective-permute-start.61 = (bf16[256,2048]{1,0:T(8,128)(2,1)}, bf16[256,2048]{1,0:T(8,128)(2,1)}, u32[]{:S(2)}, u32[]{:S(2)}) collective-permute-start(bf16[256,2048]{1,0:T(8,128)(2,1)} %pad_maximum_fusion.8), channel_id=1, source_target_pairs={{0,8},{4,12},{8,0},{12,4},{16,24},{20,28},{24,16},{28,20},{1,9},{5... | collective-permute-start | bytes 3145736 | tf_op jit(solution)/shard_map/ppermute | solution.py:26
  845.8 59.6 %all-to-all-start.9 = ((bf16[8,256,256]{2,1,0:T(8,128)(2,1)}), bf16[8,256,256]{2,1,0:T(8,128)(2,1)S(1)}, u32[]{:S(2)}, u32[]{:S(2)}) async-start(bf16[8,256,256]{2,1,0:T(8,128)(2,1)} %bitcast.195), calls=%async_computation.14 | async-start | bytes 2097152 | tf_op jit(solution)/shard_map/all_to_all | solution.py:1363
  849.9 101.1 %reduce-scatter.17.cloned.1.call-start = ((), (), s32[]{:S(2)}) async-start(), calls=%async_computation.22 | async-start | bytes 1310720 | tf_op jit(solution)/shard_map/reduce_scatter | solution.py:1319
  857.4 96.4 %reduce-scatter.19.cloned.1.call-start = ((), (), s32[]{:S(2)}) async-start(), calls=%async_computation.25 | async-start | bytes 1179648
  889.6 109.0 %reduce-scatter.13.cloned.1.call-start = ((), (), s32[]{:S(2)}) async-start(), calls=%async_computation.20 | async-start | bytes 3932160 | tf_op jit(solution)/shard_map/reduce_scatter | solution.py:1373
  915.2 25.2 %collective-permute-start.70 = (bf16[128,2048]{1,0:T(8,128)(2,1)}, bf16[128,2048]{1,0:T(8,128)(2,1)}, u32[]{:S(2)}, u32[]{:S(2)}) collective-permute-start(bf16[128,2048]{1,0:T(8,128)(2,1)} %get-tuple-element.460), channel_id=1, source_target_pairs={{0,16},{4,20},{8,24},{12,28},{16,0},{20,4},{24,8},{28,12},{1,17},{... | collective-permute-start | bytes 1572872 | tf_op jit(solution)/shard_map/ppermute | solution.py:26
  930.6 40.0 %collective-permute-start.68 = (bf16[256,2048]{1,0:T(8,128)(2,1)}, bf16[256,2048]{1,0:T(8,128)(2,1)S(1)}, u32[]{:S(2)}, u32[]{:S(2)}) collective-permute-start(bf16[256,2048]{1,0:T(8,128)(2,1)} %pad_maximum_fusion.11), channel_id=1, source_target_pairs={{0,16},{4,20},{8,24},{12,28},{16,0},{20,4},{24,8},{28,12},{1,17},{... | collective-permute-start | bytes 3145736 | tf_op jit(solution)/shard_map/ppermute | solution.py:26
  931.2 39.5 %collective-permute-start.66 = (bf16[256,2048]{1,0:T(8,128)(2,1)}, bf16[256,2048]{1,0:T(8,128)(2,1)}, u32[]{:S(2)}, u32[]{:S(2)}) collective-permute-start(bf16[256,2048]{1,0:T(8,128)(2,1)} %pad_maximum_fusion.10), channel_id=1, source_target_pairs={{0,8},{4,12},{8,0},{12,4},{16,24},{20,28},{24,16},{28,20},{1,9},{5... | collective-permute-start | bytes 3145736 | tf_op jit(solution)/shard_map/ppermute | solution.py:26
  945.1 39.8 %collective-permute-start.73 = (bf16[256,2048]{1,0:T(8,128)(2,1)}, bf16[256,2048]{1,0:T(8,128)(2,1)}, u32[]{:S(2)}, u32[]{:S(2)}) collective-permute-start(bf16[256,2048]{1,0:T(8,128)(2,1)} %pad_maximum_fusion.13), channel_id=1, source_target_pairs={{0,16},{4,20},{8,24},{12,28},{16,0},{20,4},{24,8},{28,12},{1,17},{... | collective-permute-start | bytes 3145736 | tf_op jit(solution)/shard_map/ppermute | solution.py:26
  947.8 37.1 %collective-permute-start.71 = (bf16[256,2048]{1,0:T(8,128)(2,1)}, bf16[256,2048]{1,0:T(8,128)(2,1)}, u32[]{:S(2)}, u32[]{:S(2)}) collective-permute-start(bf16[256,2048]{1,0:T(8,128)(2,1)} %pad_maximum_fusion.12), channel_id=1, source_target_pairs={{0,8},{4,12},{8,0},{12,4},{16,24},{20,28},{24,16},{28,20},{1,9},{5... | collective-permute-start | bytes 3145736 | tf_op jit(solution)/shard_map/ppermute | solution.py:26
  (110 other events, 1434.0 us)
Sparse Core Ops, SparseCore 0:
  32.4 63.7 all-gather.10
  111.0 29.5 all-gather.6
  170.3 80.1 all-gather.8
  308.6 83.3 all-gather.12
  616.3 78.6 reduce-scatter.8
  697.3 77.2 reduce-scatter.10
  778.0 76.3 reduce-scatter.14
  857.5 31.7 reduce-scatter.16
  892.5 42.5 reduce-scatter.18
  937.8 60.7 reduce-scatter.12

commit v4 on v3

--- a/solution.py
+++ b/solution.py
@@ -17,7 +17,7 @@
 FACTOR = HEAD_DIM ** (-0.5)
 BF = jnp.bfloat16
 F32 = jnp.float32
-SCALE = 4
+SCALE = 8
 VMEM_LIMIT = 56 * 1024 * 1024
 
 

time: 1040 us -> 1050 us (level)
  local copies, waits for them, and re-layouts: 84.6 us -> 98.9 us
    all_to_all x1, waiting for transfers between devices: 0.01 us -> 11.8 us  [on_device(): came = lax.all_to_all(sent, 'seq', 0, 0, tiled=True)]
    all_to_all x2, waiting for transfers between devices: 11.6 us -> 0.01 us  [attention(): lax.all_to_all(low.reshape(size, count, cols), 'seq', 0, 0, tiled=True)]
    unnamed x183 -> x165, local copies, waits for them, and re-layouts: 29.2 us -> 30.7 us
  transfers between devices with their start and end apart: 94 -> 94, of which waited for: 28 -> 27; matrix products, arithmetic and copies ran while one was open for 16% -> 18% of each run, Pallas kernels for 48% -> 46%
where the time goes in v4:
time: 1050 us; the launch traced here: 1040 us
  Pallas kernels  485 us (46%)
  waiting for transfers between devices  187 us (18%)
  other arithmetic  115 us (11%)
  starting transfers between devices  111 us (11%)
  local copies, waits for them, and re-layouts  98.9 us (9%)
  blocking collectives  20.5 us (2%)
  between operations  19.6 us (2%)
    ppermute x71, waiting for transfers between devices, swap(): return lax.ppermute(block, 'seq', [(i, i ^ bit) for i in range(size)])  109 us
    pallas_call x4, Pallas kernels, ffn_out(): pl.pallas_call(ffn_out_kernel, grid=(here // tile,), in_specs=[out, out,...  71.3 us
    pallas_call x3, Pallas kernels, weight_grad(): pl.pallas_call(partial(grads_kernel, weights is not None), grid=(width //...  68.8 us
    ppermute x71, starting transfers between devices, swap(): return lax.ppermute(block, 'seq', [(i, i ^ bit) for i in range(size)])  65.9 us
    pallas_call x2, Pallas kernels, attend_back(): pl.pallas_call(attend_back_kernel, grid_spec=pltpu.PrefetchScalarGridSpec...  60.2 us
    pallas_call x4, Pallas kernels, ffn_in(): pl.pallas_call(partial(ffn_in_kernel, given), grid=(here // tile,), in_sp...  55.7 us
    pallas_call x2, Pallas kernels, attend(): pl.pallas_call(attend_kernel, grid_spec=pltpu.PrefetchScalarGridSpec(num_...  49.3 us
    pallas_call x4, Pallas kernels, project(): pl.pallas_call(qkv_kernel, grid_spec=pltpu.PrefetchScalarGridSpec(num_sca...  34.4 us
  transfers between devices with their start and end apart: 94, of which 27 were waited for; matrix products, arithmetic and copies ran while one was open for 18% of the time, Pallas kernels for 46%

profile of v4, /device:TPU:0, one launch (start us, length us, event | category | flops | bytes accessed | tf_op | source)
XLA Modules:
  0.0 1036.0 jit_solution(13340286138728493533)
XLA Ops:
  9.7 5.3 all-to-all-start
  15.8 11.8 %all-to-all-done = bf16[8,3,64,256]{3,2,1,0:T(8,128)(2,1)S(1)} async-done(((bf16[8,3,64,256]{3,2,1,0:T(8,128)(2,1)}), bf16[8,3,64,256]{3,2,1,0:T(8,128)(2,1)S(1)}, u32[]{:S(2)}, u32[]{:S(2)}) %all-to-all-start) | async-done | bytes 786464 | tf_op jit(solution)/shard_map/all_to_all | solution.py:1079
  28.6 7.9 all_gather.23
  50.5 13.8 %collective-permute-done.refs_2_ = bf16[256,2048]{1,0:T(8,128)(2,1)} collective-permute-done((bf16[256,2048]{1,0:T(8,128)(2,1)S(1)}, bf16[256,2048]{1,0:T(8,128)(2,1)}, u32[]{:S(2)}, u32[]{:S(2)}) %collective-permute-start) | collective-permute-done | bytes 1048608 | tf_op jit(solution)/shard_map/ppermute | solution.py:26
  71.3 8.3 power_multiply_fusion
  94.8 4.3 all-to-all-done.2
  107.3 25.1 %all-to-all-done.1 = bf16[8,256,256]{2,1,0:T(8,128)(2,1)S(1)} async-done(((bf16[8,256,256]{2,1,0:T(8,128)(2,1)}), bf16[8,256,256]{2,1,0:T(8,128)(2,1)S(1)}, u32[]{:S(2)}, u32[]{:S(2)}) %all-to-all-start.1) | async-done | bytes 1048608 | tf_op jit(solution)/shard_map/all_to_all | solution.py:1092
  132.4 5.7 arrange.1
  145.0 8.5 project.4
  153.6 8.6 project.5
  162.7 4.0 convert_reduce_fusion
  178.8 9.2 collective-permute-done.11.refs_4_
  192.9 26.4 %attend.2 = (f32[2048,256]{1,0:T(8,128)}, bf16[2048,256]{1,0:T(8,128)(2,1)}, f32[2048,4]{1,0:T(8,128)}) custom-call(s32[8]{0:T(128)} %get-tuple-element.328.first, bf16[2048,256]{1,0:T(8,128)(2,1)} %get-tuple-element.203.q_ref, bf16[2048,256]{1,0:T(8,128)(2,1)} %get-tuple-element.206.k_ref, bf16[2048,256]{1,0:T(8,128)(2,1)} %get-tuple-element.207.v_ref, ...), custom_call_target="tpu_custom_call" | custom-call | flops 154618822656 | bytes 41943040 | tf_op jit(solution)/shard_map/attend/pallas_call | solution.py:856
  221.2 4.2 all-to-all-start.3
  234.3 8.5 project.6
  242.8 8.7 project.7
  251.5 16.5 %collective-permute-done.16.refs_4_ = bf16[1024,256]{1,0:T(8,128)(2,1)S(1)} collective-permute-done((bf16[1024,256]{1,0:T(8,128)(2,1)S(1)}, bf16[1024,256]{1,0:T(8,128)(2,1)S(1)}, u32[]{:S(2)}, u32[]{:S(2)}) %collective-permute-start.16) | collective-permute-done | bytes 524320 | tf_op jit(solution)/shard_map/ppermute | solution.py:26
  273.0 22.9 %attend.3 = (f32[2048,256]{1,0:T(8,128)}, bf16[2048,256]{1,0:T(8,128)(2,1)}, f32[2048,4]{1,0:T(8,128)}) custom-call(s32[8]{0:T(128)} %get-tuple-element.336.first, bf16[2048,256]{1,0:T(8,128)(2,1)} %get-tuple-element.217.q_ref, bf16[2048,256]{1,0:T(8,128)(2,1)} %get-tuple-element.220.k_ref, bf16[2048,256]{1,0:T(8,128)(2,1)} %get-tuple-element.221.v_ref, ...), custom_call_target="tpu_custom_call" | custom-call | flops 154618822656 | bytes 41943040 | tf_op jit(solution)/shard_map/attend/pallas_call | solution.py:856
  304.6 13.0 %out_project.2 = (bf16[8,256,256]{2,1,0:T(8,128)(2,1)}, f32[256,2048]{1,0:T(8,128)}, bf16[256,2048]{1,0:T(8,128)(2,1)}) custom-call(s32[8]{0:T(128)} %copy-done.66, bf16[8,256,256]{2,1,0:T(8,128)(2,1)} %all-to-all-done.3.came_ref, bf16[4,4,8,64,256]{4,3,2,1,0:T(8,128)(2,1)} %bitcast.212, bf16[4,4,8,64,256]{4,3,2,1,0:T(8,128)(2,1)} %bitcast.21.odd_ref, ...), custom_call_target="tpu_custom_call" | custom-call | flops 17179869184 | bytes 117440512 | tf_op jit(solution)/shard_map/out_project/pallas_call | solution.py:436
  327.0 13.1 %out_project.3 = (bf16[8,256,256]{2,1,0:T(8,128)(2,1)}, f32[256,2048]{1,0:T(8,128)}, bf16[256,2048]{1,0:T(8,128)(2,1)}) custom-call(s32[8]{0:T(128)} %copy-done.66, bf16[8,256,256]{2,1,0:T(8,128)(2,1)} %copy-done.24, bf16[4,4,8,64,256]{4,3,2,1,0:T(8,128)(2,1)} %bitcast.213, bf16[4,4,8,64,256]{4,3,2,1,0:T(8,128)(2,1)} %bitcast.21.odd_ref, ...), custom_call_target="tpu_custom_call" | custom-call | flops 17179869184 | bytes 117440512 | tf_op jit(solution)/shard_map/out_project/pallas_call | solution.py:436
  341.8 8.7 ffn_grad.2.refs_1_.t_ref
  355.2 8.7 ffn_grad.3.refs_1_.t_ref
  363.8 16.2 %collective-permute-done.26.refs_4_ = bf16[128,2048]{1,0:T(8,128)(2,1)S(1)} collective-permute-done((bf16[128,2048]{1,0:T(8,128)(2,1)S(1)}, bf16[128,2048]{1,0:T(8,128)(2,1)S(1)}, u32[]{:S(2)}, u32[]{:S(2)}) %collective-permute-start.26) | collective-permute-done | bytes 524320 | tf_op jit(solution)/shard_map/ppermute | solution.py:26
  390.9 11.1 %ffn_in.4 = (f32[1024,1024]{1,0:T(8,128)}, bf16[1024,1024]{1,0:T(8,128)(2,1)}, f32[1024,4]{1,0:T(8,128)}) custom-call(bf16[1024,2048]{1,0:T(8,128)(2,1)} %join.11.refs_0_.refs_4_, bf16[1024,1024]{1,0:T(8,128)(2,1)} %ffn_grad.2.refs_1_.t_ref, bf16[4,2048,256]{2,1,0:T(8,128)(2,1)} %bitcast.273), custom_call_target="tpu_custom_call" | custom-call | flops 34359738368 | bytes 201326592 | tf_op jit(solution)/shard_map/ffn_in/pallas_call | solution.py:632
  403.3 8.1 collective-permute-done.33.refs_2_
  416.8 7.2 collective-permute-done.31.refs_4_
  427.5 11.3 %ffn_in.5 = (f32[1024,1024]{1,0:T(8,128)}, bf16[1024,1024]{1,0:T(8,128)(2,1)}, f32[1024,4]{1,0:T(8,128)}) custom-call(bf16[1024,2048]{1,0:T(8,128)(2,1)} %collective-permute-done.29.refs_0_.refs_5_, bf16[1024,1024]{1,0:T(8,128)(2,1)} %ffn_grad.3.refs_1_.t_ref, bf16[4,2048,256]{2,1,0:T(8,128)(2,1)} %bitcast.274), custom_call_target="tpu_custom_call" | custom-call | flops 34359738368 | bytes 201326592 | tf_op jit(solution)/shard_map/ffn_in/pallas_call | solution.py:632
  445.6 16.7 %ffn_in.6 = (f32[1024,1024]{1,0:T(8,128)}, bf16[1024,1024]{1,0:T(8,128)(2,1)}, f32[1024,4]{1,0:T(8,128)}, bf16[1024,1024]{1,0:T(8,128)(2,1)}) custom-call(bf16[1024,2048]{1,0:T(8,128)(2,1)} %join.13.refs_0_.refs_6_, bf16[1024,2048]{1,0:T(8,128)(2,1)} %join.12.refs_1_.refs_6_, bf16[4,2048,256]{2,1,0:T(8,128)(2,1)} %bitcast.275, ...), custom_call_target="tpu_custom_call" | custom-call | flops 68719476736 | bytes 201326592 | tf_op jit(solution)/shard_map/ffn_in/pallas_call | solution.py:632
  464.9 16.7 %ffn_in.7 = (f32[1024,1024]{1,0:T(8,128)}, bf16[1024,1024]{1,0:T(8,128)(2,1)}, f32[1024,4]{1,0:T(8,128)}, bf16[1024,1024]{1,0:T(8,128)(2,1)}) custom-call(bf16[1024,2048]{1,0:T(8,128)(2,1)} %collective-permute-done.38.refs_0_.refs_7_, bf16[1024,2048]{1,0:T(8,128)(2,1)} %collective-permute-done.39.refs_1_.refs_7_, bf16[4,2048,256]{2,1,0:T(8,128)(2,1)} %bitcast.276, ...), custom_call_target="tpu_custom_call" | custom-call | flops 68719476736 | bytes 201326592 | tf_op jit(solution)/shard_map/ffn_in/pallas_call | solution.py:632
  488.4 17.7 %ffn_out.4 = (bf16[1024,1024]{1,0:T(8,128)(2,1)}, bf16[1024,1024]{1,0:T(8,128)(2,1)}, bf16[1024,2048]{1,0:T(8,128)(2,1)}, bf16[1024,2048]{1,0:T(8,128)(2,1)}, f32[1,1024]{1,0:T(1,128)}) custom-call(f32[1024,1024]{1,0:T(8,128)} %get-tuple-element.264.a_ref, bf16[1024,1024]{1,0:T(8,128)(2,1)} %get-tuple-element.265.p_ref, ...), custom_call_target="tpu_custom_call" | custom-call | flops 68719476736 | bytes 234881024 | tf_op jit(solution)/shard_map/ffn_out/pallas_call | solution.py:685
  507.0 18.2 %ffn_out.5 = (bf16[1024,1024]{1,0:T(8,128)(2,1)}, bf16[1024,1024]{1,0:T(8,128)(2,1)}, bf16[1024,2048]{1,0:T(8,128)(2,1)}, bf16[1024,2048]{1,0:T(8,128)(2,1)}, f32[1,1024]{1,0:T(1,128)}) custom-call(f32[1024,1024]{1,0:T(8,128)} %get-tuple-element.247.a_ref, bf16[1024,1024]{1,0:T(8,128)(2,1)} %get-tuple-element.248.p_ref, ...), custom_call_target="tpu_custom_call" | custom-call | flops 68719476736 | bytes 234881024 | tf_op jit(solution)/shard_map/ffn_out/pallas_call | solution.py:685
  534.6 17.6 %ffn_out.6 = (bf16[1024,1024]{1,0:T(8,128)(2,1)}, bf16[1024,1024]{1,0:T(8,128)(2,1)}, bf16[1024,2048]{1,0:T(8,128)(2,1)}, bf16[1024,2048]{1,0:T(8,128)(2,1)}, f32[1,1024]{1,0:T(1,128)}) custom-call(f32[1024,1024]{1,0:T(8,128)} %get-tuple-element.279.a_ref, bf16[1024,1024]{1,0:T(8,128)(2,1)} %get-tuple-element.280.p_ref, ...), custom_call_target="tpu_custom_call" | custom-call | flops 68719476736 | bytes 234881024 | tf_op jit(solution)/shard_map/ffn_out/pallas_call | solution.py:685
  558.8 17.8 %ffn_out.7 = (bf16[1024,1024]{1,0:T(8,128)(2,1)}, bf16[1024,1024]{1,0:T(8,128)(2,1)}, bf16[1024,2048]{1,0:T(8,128)(2,1)}, bf16[1024,2048]{1,0:T(8,128)(2,1)}, f32[1,1024]{1,0:T(1,128)}) custom-call(f32[1024,1024]{1,0:T(8,128)} %get-tuple-element.273.a_ref, bf16[1024,1024]{1,0:T(8,128)(2,1)} %get-tuple-element.274.p_ref, ...), custom_call_target="tpu_custom_call" | custom-call | flops 68719476736 | bytes 234881024 | tf_op jit(solution)/shard_map/ffn_out/pallas_call | solution.py:685
  576.6 5.0 collective-permute-done.50
  582.2 3.9 add_add_fusion.1.grad_ref
  592.3 24.4 %weight_grad.3 = bf16[1024,2048]{1,0:T(8,128)(2,1)} custom-call(bf16[1024,1024]{1,0:T(8,128)(2,1)} %get-tuple-element.294.refs_0_, bf16[1024,1024]{1,0:T(8,128)(2,1)} %get-tuple-element.296.refs_1_, bf16[1024,1024]{1,0:T(8,128)(2,1)} %get-tuple-element.298.refs_2_, bf16[1024,1024]{1,0:T(8,128)(2,1)} %get-tuple-element.300.refs_3_, ...), custom_call_target="tpu_custom_call" | custom-call | flops 137438953472 | bytes 234881024 | tf_op jit(solution)/shard_map/weight_grad/pallas_call | solution.py:763
  623.7 16.3 %out_back.2 = (f32[256,2048]{1,0:T(8,128)}, bf16[256,2048]{1,0:T(8,128)(2,1)}, bf16[8,256,256]{2,1,0:T(8,128)(2,1)}, f32[1,2048]{1,0:T(1,128)}, f32[8,1,256]{2,1,0:T(1,128)}) custom-call(s32[8]{0:T(128)} %copy-done.66, f32[256,2048]{1,0:T(8,128)} %add_add_fusion.1.grad_ref, f32[256,2048]{1,0:T(8,128)} %get-tuple-element.227.res_ref, ...), custom_call_target="tpu_custom_call" | custom-call | flops 17179869184 | bytes 150994944 | tf_op jit(solution)/shard_map/out_back/pallas_call | solution.py:533
  640.0 3.7 all-to-all-start.5
  649.1 24.5 %weight_grad.4 = bf16[1024,2048]{1,0:T(8,128)(2,1)} custom-call(bf16[1024,1024]{1,0:T(8,128)(2,1)} %get-tuple-element.308.refs_0_, bf16[1024,1024]{1,0:T(8,128)(2,1)} %get-tuple-element.310.refs_1_, bf16[1024,1024]{1,0:T(8,128)(2,1)} %get-tuple-element.312.refs_2_, bf16[1024,1024]{1,0:T(8,128)(2,1)} %get-tuple-element.314.refs_3_, ...), custom_call_target="tpu_custom_call" | custom-call | flops 137438953472 | bytes 234881024 | tf_op jit(solution)/shard_map/weight_grad/pallas_call | solution.py:763
  674.5 3.6 add_convert_fusion.21
  686.7 4.2 add_add_fusion.grad_ref
  690.9 16.2 %out_back.3 = (f32[256,2048]{1,0:T(8,128)}, bf16[256,2048]{1,0:T(8,128)(2,1)}, bf16[8,256,256]{2,1,0:T(8,128)(2,1)}, f32[1,2048]{1,0:T(1,128)}, f32[8,1,256]{2,1,0:T(1,128)}) custom-call(s32[8]{0:T(128)} %copy-done.66, f32[256,2048]{1,0:T(8,128)} %add_add_fusion.grad_ref, f32[256,2048]{1,0:T(8,128)} %get-tuple-element.234.res_ref, ...), custom_call_target="tpu_custom_call" | custom-call | flops 17179869184 | bytes 150994944 | tf_op jit(solution)/shard_map/out_back/pallas_call | solution.py:533
  707.0 4.2 all-to-all-start.6
  711.3 11.0 %out_grad.1 = bf16[8,4,8,64,256]{4,3,2,1,0:T(8,128)(2,1)} custom-call(bf16[8,256,256]{2,1,0:T(8,128)(2,1)} %get-tuple-element.321.refs_0_, bf16[8,256,256]{2,1,0:T(8,128)(2,1)} %get-tuple-element.323.refs_1_, bf16[256,2048]{1,0:T(8,128)(2,1)} %get-tuple-element.324.refs_2_, bf16[256,2048]{1,0:T(8,128)(2,1)} %get-tuple-element.325.refs_3_), custom_call_target="tpu_custom_call" | custom-call | flops 34359738368 | bytes 100663296 | tf_op jit(solution)/shard_map/out_grad/pallas_call | solution.py:351
  728.6 31.6 %attend_back.2.x_ref.refs_0_.refs_1_ = bf16[2048,768]{1,0:T(8,128)(2,1)} custom-call(s32[8]{0:T(128)} %get-tuple-element.328.first, s32[8]{0:T(128)} %shift-right-arithmetic_add_fusion.spot, bf16[2048,256]{1,0:T(8,128)(2,1)} %get-tuple-element.203.q_ref, bf16[2048,256]{1,0:T(8,128)(2,1)} %get-tuple-element.206.k_ref, ...), custom_call_target="tpu_custom_call" | custom-call | flops 206158430208 | bytes 83886080 | tf_op jit(solution)/shard_map/attend_back/pallas_call | solution.py:972
  765.5 7.4 multiply.81
  780.1 7.3 multiply.82
  791.3 28.5 %attend_back.3.x_ref.refs_2_.refs_3_ = bf16[2048,768]{1,0:T(8,128)(2,1)} custom-call(s32[8]{0:T(128)} %get-tuple-element.336.first, s32[8]{0:T(128)} %shift-right-arithmetic_add_fusion.spot, bf16[2048,256]{1,0:T(8,128)(2,1)} %get-tuple-element.217.q_ref, bf16[2048,256]{1,0:T(8,128)(2,1)} %get-tuple-element.220.k_ref, ...), custom_call_target="tpu_custom_call" | custom-call | flops 206158430208 | bytes 83886080 | tf_op jit(solution)/shard_map/attend_back/pallas_call | solution.py:972
  825.1 7.5 multiply.83
  849.1 7.3 multiply.84
  862.2 19.8 %weight_grad.5 = (bf16[768,2048]{1,0:T(8,128)(2,1)}, f32[1,2048]{1,0:T(1,128)}) custom-call(bf16[2048,768]{1,0:T(8,128)(2,1)} %attend_back.2.x_ref.refs_0_.refs_1_, bf16[2048,768]{1,0:T(8,128)(2,1)} %attend_back.2.x_ref.refs_0_.refs_1_, bf16[2048,768]{1,0:T(8,128)(2,1)} %attend_back.3.x_ref.refs_2_.refs_3_, ...), custom_call_target="tpu_custom_call" | custom-call | flops 103079215104 | bytes 209715200 | tf_op jit(solution)/shard_map/weight_grad/pallas_call | solution.py:763
  896.0 3.7 fusion.24
  900.8 6.7 all-to-all-done.9
  912.0 3.6 fusion.25
  923.7 7.0 all-to-all-done.8
  933.8 8.6 collective-permute-done.70
  942.5 3.6 add_convert_fusion.5
  956.7 12.5 %all-reduce.1 = (f32[3,256]{1,0:T(4,128)S(1)}, f32[4,256]{1,0:T(4,128)S(1)}) all-reduce(f32[3,256]{1,0:T(4,128)S(1)} %copy.279, f32[4,256]{1,0:T(4,128)S(1)} %reshape.402), channel_id=1, replica_groups=mesh['seq'=8,'tensor'=4] {'tensor'}, use_global_device_ids=true, to_apply=%region_17.18 | all-reduce | flops 1792 | bytes 14336 | tf_op jit(solution)/shard_map/psum | solution.py:1358
  972.3 14.6 %collective-permute-done.73 = bf16[256,2048]{1,0:T(8,128)(2,1)} collective-permute-done((bf16[256,2048]{1,0:T(8,128)(2,1)}, bf16[256,2048]{1,0:T(8,128)(2,1)}, u32[]{:S(2)}, u32[]{:S(2)}) %collective-permute-start.73) | collective-permute-done | bytes 1048608 | tf_op jit(solution)/shard_map/ppermute | solution.py:26
  987.0 5.4 fusion.31
  992.4 9.7 reduce-scatter.13.cloned.1.call-done
  1004.5 3.7 all-to-all-start.7
  1008.2 4.2 fusion.9
  1014.7 6.2 all-to-all-done.7
  (492 shorter events, 298.7 us)
Async XLA Ops:
  15.0 117.4 %all-gather.11.cloned.1.call-start = ((), (), s32[]{:S(2)}) async-start(), calls=%async_computation.23 | async-start | bytes 3932160 | tf_op jit(solution)/shard_map/all_gather | solution.py:1080
  38.8 25.6 %collective-permute-start = (bf16[256,2048]{1,0:T(8,128)(2,1)S(1)}, bf16[256,2048]{1,0:T(8,128)(2,1)}, u32[]{:S(2)}, u32[]{:S(2)}) collective-permute-start(bf16[256,2048]{1,0:T(8,128)(2,1)S(1)} %get-tuple-element.188.refs_0_), channel_id=1, source_target_pairs={{0,16},{4,20},{8,24},{12,28},{16,0},{20,4},{24,8},{28,12},{1,17},{... | collective-permute-start | bytes 3145736 | tf_op jit(solution)/shard_map/ppermute | solution.py:26
  86.6 67.0 %collective-permute-start.9 = (bf16[1024,2048]{1,0:T(8,128)(2,1)}, bf16[1024,2048]{1,0:T(8,128)(2,1)}, u32[]{:S(2)}, u32[]{:S(2)}) collective-permute-start(bf16[1024,2048]{1,0:T(8,128)(2,1)} %join.7.x_ref.refs_4_), channel_id=1, source_target_pairs={{0,4},{4,0},{8,12},{12,8},{16,20},{20,16},{24,28},{28,24},{1,5},{5... | collective-permute-start | bytes 12582920 | tf_op jit(solution)/shard_map/ppermute | solution.py:26
  87.1 51.0 %collective-permute-start.8 = (bf16[256,2048]{1,0:T(8,128)(2,1)}, bf16[256,2048]{1,0:T(8,128)(2,1)}, u32[]{:S(2)}, u32[]{:S(2)}) collective-permute-start(bf16[256,2048]{1,0:T(8,128)(2,1)} %get-tuple-element.204.refs_0_), channel_id=1, source_target_pairs={{0,16},{4,20},{8,24},{12,28},{16,0},{20,4},{24,8},{28,12},{1,17},{... | collective-permute-start | bytes 3145736 | tf_op jit(solution)/shard_map/ppermute | solution.py:26
  88.8 49.3 %collective-permute-start.7 = (bf16[256,2048]{1,0:T(8,128)(2,1)}, bf16[256,2048]{1,0:T(8,128)(2,1)}, u32[]{:S(2)}, u32[]{:S(2)}) collective-permute-start(bf16[256,2048]{1,0:T(8,128)(2,1)} %get-tuple-element.204.refs_0_), channel_id=1, source_target_pairs={{0,8},{4,12},{8,0},{12,4},{16,24},{20,28},{24,16},{28,20},{1,9},{5... | collective-permute-start | bytes 3145736 | tf_op jit(solution)/shard_map/ppermute | solution.py:26
  100.1 32.3 %all-to-all-start.1 = ((bf16[8,256,256]{2,1,0:T(8,128)(2,1)}), bf16[8,256,256]{2,1,0:T(8,128)(2,1)S(1)}, u32[]{:S(2)}, u32[]{:S(2)}) async-start(bf16[8,256,256]{2,1,0:T(8,128)(2,1)} %copy.245), calls=%async_computation.1 | async-start | bytes 2097152 | tf_op jit(solution)/shard_map/all_to_all | solution.py:1092
  103.6 49.9 %all-gather.7.cloned.1.call-start = ((), (), s32[]{:S(2)}) async-start(), calls=%async_computation.16 | async-start | bytes 1310720 | tf_op jit(solution)/shard_map/all_gather | solution.py:1087
  104.9 236.9 %all-gather.9.cloned.1.call-start = ((), (), s32[]{:S(2)}) async-start(), calls=%async_computation.17 | async-start | bytes 5242880 | tf_op jit(solution)/shard_map/all_gather | solution.py:1169
  162.2 228.8 %all-gather.13.cloned.1.call-start = ((), (), s32[]{:S(2)}) async-start(), calls=%async_computation.24 | async-start | bytes 5242880 | tf_op jit(solution)/shard_map/all_gather | solution.py:1160
  175.9 49.6 %collective-permute-start.13 = (bf16[2048,256]{1,0:T(8,128)(2,1)}, bf16[2048,256]{1,0:T(8,128)(2,1)}, u32[]{:S(2)}, u32[]{:S(2)}) collective-permute-start(bf16[2048,256]{1,0:T(8,128)(2,1)} %all-gather.7.cloned.1.call-done.refs_0_), channel_id=1, source_target_pairs={{0,16},{4,20},{8,24},{12,28},{16,0},{20,4},{24,8},{28,12},{1,17},{... | collective-permute-start | bytes 3145736 | tf_op jit(solution)/shard_map/ppermute | solution.py:26
  177.2 48.3 %collective-permute-start.12 = (bf16[2048,256]{1,0:T(8,128)(2,1)}, bf16[2048,256]{1,0:T(8,128)(2,1)}, u32[]{:S(2)}, u32[]{:S(2)}) collective-permute-start(bf16[2048,256]{1,0:T(8,128)(2,1)} %all-gather.7.cloned.1.call-done.refs_0_), channel_id=1, source_target_pairs={{0,8},{4,12},{8,0},{12,4},{16,24},{20,28},{24,16},{28,20},{1,9},{5... | collective-permute-start | bytes 3145736 | tf_op jit(solution)/shard_map/ppermute | solution.py:26
  192.9 49.9 %collective-permute-start.14 = (bf16[1024,2048]{1,0:T(8,128)(2,1)}, bf16[1024,2048]{1,0:T(8,128)(2,1)}, u32[]{:S(2)}, u32[]{:S(2)}) collective-permute-start(bf16[1024,2048]{1,0:T(8,128)(2,1)} %join.8.x_ref.refs_6_), channel_id=1, source_target_pairs={{0,4},{4,0},{8,12},{12,8},{16,20},{20,16},{24,28},{28,24},{1,5},{5... | collective-permute-start | bytes 12582920 | tf_op jit(solution)/shard_map/ppermute | solution.py:26
  219.3 76.6 %collective-permute-start.18 = (bf16[256,2048]{1,0:T(8,128)(2,1)}, bf16[256,2048]{1,0:T(8,128)(2,1)}, u32[]{:S(2)}, u32[]{:S(2)}) collective-permute-start(bf16[256,2048]{1,0:T(8,128)(2,1)} %get-tuple-element.230.refs_0_.cot_ref), channel_id=1, source_target_pairs={{0,16},{4,20},{8,24},{12,28},{16,0},{20,4},{24,8},{28,12},{1,17},{... | collective-permute-start | bytes 3145736 | tf_op jit(solution)/shard_map/ppermute | solution.py:26
  219.9 76.0 %collective-permute-start.17 = (bf16[256,2048]{1,0:T(8,128)(2,1)}, bf16[256,2048]{1,0:T(8,128)(2,1)}, u32[]{:S(2)}, u32[]{:S(2)}) collective-permute-start(bf16[256,2048]{1,0:T(8,128)(2,1)} %get-tuple-element.230.refs_0_.cot_ref), channel_id=1, source_target_pairs={{0,8},{4,12},{8,0},{12,4},{16,24},{20,28},{24,16},{28,20},{1,9},{5... | collective-permute-start | bytes 3145736 | tf_op jit(solution)/shard_map/ppermute | solution.py:26
  221.2 79.6 %all-to-all-start.3 = ((bf16[8,256,256]{2,1,0:T(8,128)(2,1)}), bf16[8,256,256]{2,1,0:T(8,128)(2,1)}, u32[]{:S(2)}, u32[]{:S(2)}) async-start(bf16[8,256,256]{2,1,0:T(8,128)(2,1)} %bitcast.231), calls=%async_computation.3 | async-start | bytes 2097152 | tf_op jit(solution)/shard_map/all_to_all | solution.py:1132
  227.6 40.4 %collective-permute-start.16 = (bf16[1024,256]{1,0:T(8,128)(2,1)S(1)}, bf16[1024,256]{1,0:T(8,128)(2,1)S(1)}, u32[]{:S(2)}, u32[]{:S(2)}) collective-permute-start(bf16[1024,256]{1,0:T(8,128)(2,1)S(1)} %slice.530), channel_id=1, source_target_pairs={{0,8},{4,12},{8,0},{12,4},{16,24},{20,28},{24,16},{28,20},{1,9},{5... | collective-permute-start | bytes 1572872 | tf_op jit(solution)/shard_map/ppermute | solution.py:26
  229.6 38.4 %collective-permute-start.15 = (bf16[1024,256]{1,0:T(8,128)(2,1)S(1)}, bf16[1024,256]{1,0:T(8,128)(2,1)S(1)}, u32[]{:S(2)}, u32[]{:S(2)}) collective-permute-start(bf16[1024,256]{1,0:T(8,128)(2,1)S(1)} %slice.529), channel_id=1, source_target_pairs={{0,16},{4,20},{8,24},{12,28},{16,0},{20,4},{24,8},{28,12},{1,17},{... | collective-permute-start | bytes 1572872 | tf_op jit(solution)/shard_map/ppermute | solution.py:26
  272.9 31.7 %collective-permute-start.19 = (bf16[8192,256]{1,0:T(8,128)(2,1)}, bf16[8192,256]{1,0:T(8,128)(2,1)}, u32[]{:S(2)}, u32[]{:S(2)}) collective-permute-start(bf16[8192,256]{1,0:T(8,128)(2,1)} %join.9), channel_id=1, source_target_pairs={{0,4},{4,0},{8,12},{12,8},{16,20},{20,16},{24,28},{28,24},{1,5},{5... | collective-permute-start | bytes 12582920 | tf_op jit(solution)/shard_map/ppermute | solution.py:26
  304.4 461.1 %reduce-scatter.9.cloned.1.call-start = ((), (), s32[]{:S(2)}) async-start(), calls=%async_computation.18 | async-start | bytes 5242880 | tf_op jit(solution)/shard_map/reduce_scatter | solution.py:1260
  317.6 32.9 %collective-permute-start.24 = (bf16[256,2048]{1,0:T(8,128)(2,1)}, bf16[256,2048]{1,0:T(8,128)(2,1)}, u32[]{:S(2)}, u32[]{:S(2)}) collective-permute-start(bf16[256,2048]{1,0:T(8,128)(2,1)} %get-tuple-element.242.refs_0_), channel_id=1, source_target_pairs={{0,16},{4,20},{8,24},{12,28},{16,0},{20,4},{24,8},{28,12},{1,17},{... | collective-permute-start | bytes 3145736 | tf_op jit(solution)/shard_map/ppermute | solution.py:26
  319.5 31.0 %collective-permute-start.23 = (bf16[256,2048]{1,0:T(8,128)(2,1)}, bf16[256,2048]{1,0:T(8,128)(2,1)}, u32[]{:S(2)}, u32[]{:S(2)}) collective-permute-start(bf16[256,2048]{1,0:T(8,128)(2,1)} %get-tuple-element.242.refs_0_), channel_id=1, source_target_pairs={{0,8},{4,12},{8,0},{12,4},{16,24},{20,28},{24,16},{28,20},{1,9},{5... | collective-permute-start | bytes 3145736 | tf_op jit(solution)/shard_map/ppermute | solution.py:26
  325.8 29.3 %collective-permute-start.22 = (bf16[1024,2048]{1,0:T(8,128)(2,1)}, bf16[1024,2048]{1,0:T(8,128)(2,1)}, u32[]{:S(2)}, u32[]{:S(2)}) collective-permute-start(bf16[1024,2048]{1,0:T(8,128)(2,1)} %join.10.c_ref.refs_4_), channel_id=1, source_target_pairs={{0,4},{4,0},{8,12},{12,8},{16,20},{20,16},{24,28},{28,24},{1,5},{5... | collective-permute-start | bytes 12582920 | tf_op jit(solution)/shard_map/ppermute | solution.py:26
  340.1 47.5 %collective-permute-start.28 = (bf16[256,2048]{1,0:T(8,128)(2,1)S(1)}, bf16[256,2048]{1,0:T(8,128)(2,1)S(1)}, u32[]{:S(2)}, u32[]{:S(2)}) collective-permute-start(bf16[256,2048]{1,0:T(8,128)(2,1)S(1)} %copy-done.15), channel_id=1, source_target_pairs={{0,16},{4,20},{8,24},{12,28},{16,0},{20,4},{24,8},{28,12},{1,17},{... | collective-permute-start | bytes 3145736 | tf_op jit(solution)/shard_map/ppermute | solution.py:26
  341.0 46.6 %collective-permute-start.27 = (bf16[256,2048]{1,0:T(8,128)(2,1)S(1)}, bf16[256,2048]{1,0:T(8,128)(2,1)S(1)}, u32[]{:S(2)}, u32[]{:S(2)}) collective-permute-start(bf16[256,2048]{1,0:T(8,128)(2,1)S(1)} %copy-done.15), channel_id=1, source_target_pairs={{0,8},{4,12},{8,0},{12,4},{16,24},{20,28},{24,16},{28,20},{1,9},{5... | collective-permute-start | bytes 3145736 | tf_op jit(solution)/shard_map/ppermute | solution.py:26
  352.7 27.3 %collective-permute-start.26 = (bf16[128,2048]{1,0:T(8,128)(2,1)S(1)}, bf16[128,2048]{1,0:T(8,128)(2,1)S(1)}, u32[]{:S(2)}, u32[]{:S(2)}) collective-permute-start(bf16[128,2048]{1,0:T(8,128)(2,1)S(1)} %slice.539), channel_id=1, source_target_pairs={{0,8},{4,12},{8,0},{12,4},{16,24},{20,28},{24,16},{28,20},{1,9},{5... | collective-permute-start | bytes 1572872 | tf_op jit(solution)/shard_map/ppermute | solution.py:26
  354.0 26.9 %collective-permute-start.25 = (bf16[128,2048]{1,0:T(8,128)(2,1)S(1)}, bf16[128,2048]{1,0:T(8,128)(2,1)S(1)}, u32[]{:S(2)}, u32[]{:S(2)}) collective-permute-start(bf16[128,2048]{1,0:T(8,128)(2,1)S(1)} %slice.538), channel_id=1, source_target_pairs={{0,16},{4,20},{8,24},{12,28},{16,0},{20,4},{24,8},{28,12},{1,17},{... | collective-permute-start | bytes 1572872 | tf_op jit(solution)/shard_map/ppermute | solution.py:26
  384.9 42.6 %collective-permute-start.29 = (bf16[1024,2048]{1,0:T(8,128)(2,1)}, bf16[1024,2048]{1,0:T(8,128)(2,1)}, u32[]{:S(2)}, u32[]{:S(2)}) collective-permute-start(bf16[1024,2048]{1,0:T(8,128)(2,1)} %join.11.refs_0_.refs_4_), channel_id=1, source_target_pairs={{0,4},{4,0},{8,12},{12,8},{16,20},{20,16},{24,28},{28,24},{1,5},{5... | collective-permute-start | bytes 12582920 | tf_op jit(solution)/shard_map/ppermute | solution.py:26
  385.0 26.3 %collective-permute-start.33 = (bf16[256,2048]{1,0:T(8,128)(2,1)}, bf16[256,2048]{1,0:T(8,128)(2,1)}, u32[]{:S(2)}, u32[]{:S(2)}) collective-permute-start(bf16[256,2048]{1,0:T(8,128)(2,1)} %get-tuple-element.256.refs_0_), channel_id=1, source_target_pairs={{0,16},{4,20},{8,24},{12,28},{16,0},{20,4},{24,8},{28,12},{1,17},{... | collective-permute-start | bytes 3145736 | tf_op jit(solution)/shard_map/ppermute | solution.py:26
  386.4 26.3 %collective-permute-start.32 = (bf16[256,2048]{1,0:T(8,128)(2,1)}, bf16[256,2048]{1,0:T(8,128)(2,1)}, u32[]{:S(2)}, u32[]{:S(2)}) collective-permute-start(bf16[256,2048]{1,0:T(8,128)(2,1)} %get-tuple-element.256.refs_0_), channel_id=1, source_target_pairs={{0,8},{4,12},{8,0},{12,4},{16,24},{20,28},{24,16},{28,20},{1,9},{5... | collective-permute-start | bytes 3145736 | tf_op jit(solution)/shard_map/ppermute | solution.py:26
  389.4 34.6 %collective-permute-start.31 = (bf16[128,2048]{1,0:T(8,128)(2,1)}, bf16[128,2048]{1,0:T(8,128)(2,1)}, u32[]{:S(2)}, u32[]{:S(2)}) collective-permute-start(bf16[128,2048]{1,0:T(8,128)(2,1)} %slice.541), channel_id=1, source_target_pairs={{0,8},{4,12},{8,0},{12,4},{16,24},{20,28},{24,16},{28,20},{1,9},{5... | collective-permute-start | bytes 1572872 | tf_op jit(solution)/shard_map/ppermute | solution.py:26
  390.3 33.7 %collective-permute-start.30 = (bf16[128,2048]{1,0:T(8,128)(2,1)}, bf16[128,2048]{1,0:T(8,128)(2,1)}, u32[]{:S(2)}, u32[]{:S(2)}) collective-permute-start(bf16[128,2048]{1,0:T(8,128)(2,1)} %slice.540), channel_id=1, source_target_pairs={{0,16},{4,20},{8,24},{12,28},{16,0},{20,4},{24,8},{28,12},{1,17},{... | collective-permute-start | bytes 1572872 | tf_op jit(solution)/shard_map/ppermute | solution.py:26
  414.9 25.7 %collective-permute-start.36 = (bf16[128,2048]{1,0:T(8,128)(2,1)S(1)}, bf16[128,2048]{1,0:T(8,128)(2,1)S(1)}, u32[]{:S(2)}, u32[]{:S(2)}) collective-permute-start(bf16[128,2048]{1,0:T(8,128)(2,1)S(1)} %slice.543), channel_id=1, source_target_pairs={{0,8},{4,12},{8,0},{12,4},{16,24},{20,28},{24,16},{28,20},{1,9},{5... | collective-permute-start | bytes 1572872 | tf_op jit(solution)/shard_map/ppermute | solution.py:26
  427.5 37.4 %collective-permute-start.39 = (bf16[1024,2048]{1,0:T(8,128)(2,1)}, bf16[1024,2048]{1,0:T(8,128)(2,1)}, u32[]{:S(2)}, u32[]{:S(2)}) collective-permute-start(bf16[1024,2048]{1,0:T(8,128)(2,1)} %join.12.refs_1_.refs_6_), channel_id=1, source_target_pairs={{0,4},{4,0},{8,12},{12,8},{16,20},{20,16},{24,28},{28,24},{1,5},{5... | collective-permute-start | bytes 12582920 | tf_op jit(solution)/shard_map/ppermute | solution.py:26
  527.5 116.2 %collective-permute-start.52 = (bf16[1024,2048]{1,0:T(8,128)(2,1)}, bf16[1024,2048]{1,0:T(8,128)(2,1)}, u32[]{:S(2)}, u32[]{:S(2)}) collective-permute-start(bf16[1024,2048]{1,0:T(8,128)(2,1)} %get-tuple-element.306), channel_id=1, source_target_pairs={{0,4},{4,0},{8,12},{12,8},{16,20},{20,16},{24,28},{28,24},{1,5},{5... | collective-permute-start | bytes 12582920 | tf_op jit(solution)/shard_map/ppermute | solution.py:26
  552.3 33.8 %collective-permute-start.47 = (bf16[1024,2048]{1,0:T(8,128)(2,1)}, bf16[1024,2048]{1,0:T(8,128)(2,1)S(1)}, u32[]{:S(2)}, u32[]{:S(2)}) collective-permute-start(bf16[1024,2048]{1,0:T(8,128)(2,1)} %get-tuple-element.293), channel_id=1, source_target_pairs={{0,4},{4,0},{8,12},{12,8},{16,20},{20,16},{24,28},{28,24},{1,5},{5... | collective-permute-start | bytes 12582920 | tf_op jit(solution)/shard_map/ppermute | solution.py:26
  552.4 170.0 %collective-permute-start.59 = (bf16[1024,2048]{1,0:T(8,128)(2,1)}, bf16[1024,2048]{1,0:T(8,128)(2,1)}, u32[]{:S(2)}, u32[]{:S(2)}) collective-permute-start(bf16[1024,2048]{1,0:T(8,128)(2,1)} %get-tuple-element.327), channel_id=1, source_target_pairs={{0,4},{4,0},{8,12},{12,8},{16,20},{20,16},{24,28},{28,24},{1,5},{5... | collective-permute-start | bytes 12582920 | tf_op jit(solution)/shard_map/ppermute | solution.py:26
  556.3 25.3 %collective-permute-start.50 = (bf16[256,2048]{1,0:T(8,128)(2,1)S(1)}, bf16[256,2048]{1,0:T(8,128)(2,1)}, u32[]{:S(2)}, u32[]{:S(2)}) collective-permute-start(bf16[256,2048]{1,0:T(8,128)(2,1)S(1)} %pad_maximum_fusion.2), channel_id=1, source_target_pairs={{0,8},{4,12},{8,0},{12,4},{16,24},{20,28},{24,16},{28,20},{1,9},{5... | collective-permute-start | bytes 3145736 | tf_op jit(solution)/shard_map/ppermute | solution.py:26
  589.7 27.1 %collective-permute-start.49 = (bf16[128,2048]{1,0:T(8,128)(2,1)S(1)}, bf16[128,2048]{1,0:T(8,128)(2,1)S(1)}, u32[]{:S(2)}, u32[]{:S(2)}) collective-permute-start(bf16[128,2048]{1,0:T(8,128)(2,1)S(1)} %get-tuple-element.484), channel_id=1, source_target_pairs={{0,8},{4,12},{8,0},{12,4},{16,24},{20,28},{24,16},{28,20},{1,9},{5... | collective-permute-start | bytes 1572872 | tf_op jit(solution)/shard_map/ppermute | solution.py:26
  590.9 25.9 %collective-permute-start.48 = (bf16[128,2048]{1,0:T(8,128)(2,1)S(1)}, bf16[128,2048]{1,0:T(8,128)(2,1)S(1)}, u32[]{:S(2)}, u32[]{:S(2)}) collective-permute-start(bf16[128,2048]{1,0:T(8,128)(2,1)S(1)} %get-tuple-element.485), channel_id=1, source_target_pairs={{0,16},{4,20},{8,24},{12,28},{16,0},{20,4},{24,8},{28,12},{1,17},{... | collective-permute-start | bytes 1572872 | tf_op jit(solution)/shard_map/ppermute | solution.py:26
  621.1 65.6 %collective-permute-start.57 = (bf16[256,2048]{1,0:T(8,128)(2,1)}, bf16[256,2048]{1,0:T(8,128)(2,1)}, u32[]{:S(2)}, u32[]{:S(2)}) collective-permute-start(bf16[256,2048]{1,0:T(8,128)(2,1)} %pad_maximum_fusion.4), channel_id=1, source_target_pairs={{0,8},{4,12},{8,0},{12,4},{16,24},{20,28},{24,16},{28,20},{1,9},{5... | collective-permute-start | bytes 3145736 | tf_op jit(solution)/shard_map/ppermute | solution.py:26
  623.0 63.7 %collective-permute-start.58 = (bf16[256,2048]{1,0:T(8,128)(2,1)}, bf16[256,2048]{1,0:T(8,128)(2,1)}, u32[]{:S(2)}, u32[]{:S(2)}) collective-permute-start(bf16[256,2048]{1,0:T(8,128)(2,1)} %pad_maximum_fusion.5), channel_id=1, source_target_pairs={{0,16},{4,20},{8,24},{12,28},{16,0},{20,4},{24,8},{28,12},{1,17},{... | collective-permute-start | bytes 3145736 | tf_op jit(solution)/shard_map/ppermute | solution.py:26
  640.0 40.3 %all-to-all-start.5 = ((bf16[8,256,256]{2,1,0:T(8,128)(2,1)}), bf16[8,256,256]{2,1,0:T(8,128)(2,1)S(1)}, u32[]{:S(2)}, u32[]{:S(2)}) async-start(bf16[8,256,256]{2,1,0:T(8,128)(2,1)} %get-tuple-element.304), calls=%async_computation.5 | async-start | bytes 2097152 | tf_op jit(solution)/shard_map/all_to_all | solution.py:1275
  643.6 181.5 %reduce-scatter.11.cloned.1.call-start = ((), (), s32[]{:S(2)}) async-start(), calls=%async_computation.19 | async-start | bytes 5242880 | tf_op jit(solution)/shard_map/reduce_scatter | solution.py:1311
  645.6 28.1 %collective-permute-start.55 = (bf16[128,2048]{1,0:T(8,128)(2,1)S(1)}, bf16[128,2048]{1,0:T(8,128)(2,1)S(1)}, u32[]{:S(2)}, u32[]{:S(2)}) collective-permute-start(bf16[128,2048]{1,0:T(8,128)(2,1)S(1)} %get-tuple-element.478), channel_id=1, source_target_pairs={{0,8},{4,12},{8,0},{12,4},{16,24},{20,28},{24,16},{28,20},{1,9},{5... | collective-permute-start | bytes 1572872 | tf_op jit(solution)/shard_map/ppermute | solution.py:26
  647.7 26.8 %collective-permute-start.53 = (bf16[128,2048]{1,0:T(8,128)(2,1)S(1)}, bf16[128,2048]{1,0:T(8,128)(2,1)}, u32[]{:S(2)}, u32[]{:S(2)}) collective-permute-start(bf16[128,2048]{1,0:T(8,128)(2,1)S(1)} %get-tuple-element.479), channel_id=1, source_target_pairs={{0,16},{4,20},{8,24},{12,28},{16,0},{20,4},{24,8},{28,12},{1,17},{... | collective-permute-start | bytes 1572872 | tf_op jit(solution)/shard_map/ppermute | solution.py:26
  707.0 58.4 %all-to-all-start.6 = ((bf16[8,256,256]{2,1,0:T(8,128)(2,1)}), bf16[8,256,256]{2,1,0:T(8,128)(2,1)}, u32[]{:S(2)}, u32[]{:S(2)}) async-start(bf16[8,256,256]{2,1,0:T(8,128)(2,1)} %get-tuple-element.320), calls=%async_computation.7 | async-start | bytes 2097152 | tf_op jit(solution)/shard_map/all_to_all | solution.py:1275
  711.3 148.0 %reduce-scatter.15.cloned.1.call-start = ((), (), s32[]{:S(2)}) async-start(), calls=%async_computation.21 | async-start | bytes 9437184 | tf_op jit(solution)/shard_map/reduce_scatter | solution.py:1320
  725.2 35.0 %collective-permute-start.60 = (bf16[128,2048]{1,0:T(8,128)(2,1)}, bf16[128,2048]{1,0:T(8,128)(2,1)}, u32[]{:S(2)}, u32[]{:S(2)}) collective-permute-start(bf16[128,2048]{1,0:T(8,128)(2,1)} %get-tuple-element.472), channel_id=1, source_target_pairs={{0,16},{4,20},{8,24},{12,28},{16,0},{20,4},{24,8},{28,12},{1,17},{... | collective-permute-start | bytes 1572872 | tf_op jit(solution)/shard_map/ppermute | solution.py:26
  727.1 33.1 %collective-permute-start.62 = (bf16[128,2048]{1,0:T(8,128)(2,1)}, bf16[128,2048]{1,0:T(8,128)(2,1)}, u32[]{:S(2)}, u32[]{:S(2)}) collective-permute-start(bf16[128,2048]{1,0:T(8,128)(2,1)} %get-tuple-element.473), channel_id=1, source_target_pairs={{0,8},{4,12},{8,0},{12,4},{16,24},{20,28},{24,16},{28,20},{1,9},{5... | collective-permute-start | bytes 1572872 | tf_op jit(solution)/shard_map/ppermute | solution.py:26
  790.7 29.1 %collective-permute-start.65 = (bf16[128,2048]{1,0:T(8,128)(2,1)}, bf16[128,2048]{1,0:T(8,128)(2,1)}, u32[]{:S(2)}, u32[]{:S(2)}) collective-permute-start(bf16[128,2048]{1,0:T(8,128)(2,1)} %get-tuple-element.466), channel_id=1, source_target_pairs={{0,16},{4,20},{8,24},{12,28},{16,0},{20,4},{24,8},{28,12},{1,17},{... | collective-permute-start | bytes 1572872 | tf_op jit(solution)/shard_map/ppermute | solution.py:26
  791.3 28.5 %collective-permute-start.67 = (bf16[128,2048]{1,0:T(8,128)(2,1)}, bf16[128,2048]{1,0:T(8,128)(2,1)}, u32[]{:S(2)}, u32[]{:S(2)}) collective-permute-start(bf16[128,2048]{1,0:T(8,128)(2,1)} %get-tuple-element.467), channel_id=1, source_target_pairs={{0,8},{4,12},{8,0},{12,4},{16,24},{20,28},{24,16},{28,20},{1,9},{5... | collective-permute-start | bytes 1572872 | tf_op jit(solution)/shard_map/ppermute | solution.py:26
  832.7 26.7 %collective-permute-start.69 = (bf16[1024,2048]{1,0:T(8,128)(2,1)}, bf16[1024,2048]{1,0:T(8,128)(2,1)}, u32[]{:S(2)}, u32[]{:S(2)}) collective-permute-start(bf16[1024,2048]{1,0:T(8,128)(2,1)} %multiply.83), channel_id=1, source_target_pairs={{0,4},{4,0},{8,12},{12,8},{16,20},{20,16},{24,28},{28,24},{1,5},{5... | collective-permute-start | bytes 12582920 | tf_op jit(solution)/shard_map/ppermute | solution.py:26
  839.8 56.2 %collective-permute-start.54 = (bf16[256,2048]{1,0:T(8,128)(2,1)}, bf16[256,2048]{1,0:T(8,128)(2,1)}, u32[]{:S(2)}, u32[]{:S(2)}) collective-permute-start(bf16[256,2048]{1,0:T(8,128)(2,1)} %pad_maximum_fusion.6), channel_id=1, source_target_pairs={{0,8},{4,12},{8,0},{12,4},{16,24},{20,28},{24,16},{28,20},{1,9},{5... | collective-permute-start | bytes 3145736 | tf_op jit(solution)/shard_map/ppermute | solution.py:26
  841.4 54.6 %collective-permute-start.56 = (bf16[256,2048]{1,0:T(8,128)(2,1)}, bf16[256,2048]{1,0:T(8,128)(2,1)}, u32[]{:S(2)}, u32[]{:S(2)}) collective-permute-start(bf16[256,2048]{1,0:T(8,128)(2,1)} %pad_maximum_fusion.7), channel_id=1, source_target_pairs={{0,16},{4,20},{8,24},{12,28},{16,0},{20,4},{24,8},{28,12},{1,17},{... | collective-permute-start | bytes 3145736 | tf_op jit(solution)/shard_map/ppermute | solution.py:26
  842.9 69.1 %collective-permute-start.63 = (bf16[256,2048]{1,0:T(8,128)(2,1)}, bf16[256,2048]{1,0:T(8,128)(2,1)}, u32[]{:S(2)}, u32[]{:S(2)}) collective-permute-start(bf16[256,2048]{1,0:T(8,128)(2,1)} %pad_maximum_fusion.9), channel_id=1, source_target_pairs={{0,16},{4,20},{8,24},{12,28},{16,0},{20,4},{24,8},{28,12},{1,17},{... | collective-permute-start | bytes 3145736 | tf_op jit(solution)/shard_map/ppermute | solution.py:26
  843.7 68.3 %collective-permute-start.61 = (bf16[256,2048]{1,0:T(8,128)(2,1)}, bf16[256,2048]{1,0:T(8,128)(2,1)}, u32[]{:S(2)}, u32[]{:S(2)}) collective-permute-start(bf16[256,2048]{1,0:T(8,128)(2,1)} %pad_maximum_fusion.8), channel_id=1, source_target_pairs={{0,8},{4,12},{8,0},{12,4},{16,24},{20,28},{24,16},{28,20},{1,9},{5... | collective-permute-start | bytes 3145736 | tf_op jit(solution)/shard_map/ppermute | solution.py:26
  845.3 62.2 %all-to-all-start.9 = ((bf16[8,256,256]{2,1,0:T(8,128)(2,1)}), bf16[8,256,256]{2,1,0:T(8,128)(2,1)S(1)}, u32[]{:S(2)}, u32[]{:S(2)}) async-start(bf16[8,256,256]{2,1,0:T(8,128)(2,1)} %bitcast.195), calls=%async_computation.14 | async-start | bytes 2097152 | tf_op jit(solution)/shard_map/all_to_all | solution.py:1363
  848.8 104.1 %reduce-scatter.17.cloned.1.call-start = ((), (), s32[]{:S(2)}) async-start(), calls=%async_computation.22 | async-start | bytes 1310720 | tf_op jit(solution)/shard_map/reduce_scatter | solution.py:1319
  859.3 96.4 %reduce-scatter.19.cloned.1.call-start = ((), (), s32[]{:S(2)}) async-start(), calls=%async_computation.25 | async-start | bytes 1179648
  891.6 110.5 %reduce-scatter.13.cloned.1.call-start = ((), (), s32[]{:S(2)}) async-start(), calls=%async_computation.20 | async-start | bytes 3932160 | tf_op jit(solution)/shard_map/reduce_scatter | solution.py:1373
  932.6 39.6 %collective-permute-start.68 = (bf16[256,2048]{1,0:T(8,128)(2,1)}, bf16[256,2048]{1,0:T(8,128)(2,1)S(1)}, u32[]{:S(2)}, u32[]{:S(2)}) collective-permute-start(bf16[256,2048]{1,0:T(8,128)(2,1)} %pad_maximum_fusion.11), channel_id=1, source_target_pairs={{0,16},{4,20},{8,24},{12,28},{16,0},{20,4},{24,8},{28,12},{1,17},{... | collective-permute-start | bytes 3145736 | tf_op jit(solution)/shard_map/ppermute | solution.py:26
  933.2 39.1 %collective-permute-start.66 = (bf16[256,2048]{1,0:T(8,128)(2,1)}, bf16[256,2048]{1,0:T(8,128)(2,1)}, u32[]{:S(2)}, u32[]{:S(2)}) collective-permute-start(bf16[256,2048]{1,0:T(8,128)(2,1)} %pad_maximum_fusion.10), channel_id=1, source_target_pairs={{0,8},{4,12},{8,0},{12,4},{16,24},{20,28},{24,16},{28,20},{1,9},{5... | collective-permute-start | bytes 3145736 | tf_op jit(solution)/shard_map/ppermute | solution.py:26
  947.2 39.7 %collective-permute-start.73 = (bf16[256,2048]{1,0:T(8,128)(2,1)}, bf16[256,2048]{1,0:T(8,128)(2,1)}, u32[]{:S(2)}, u32[]{:S(2)}) collective-permute-start(bf16[256,2048]{1,0:T(8,128)(2,1)} %pad_maximum_fusion.13), channel_id=1, source_target_pairs={{0,16},{4,20},{8,24},{12,28},{16,0},{20,4},{24,8},{28,12},{1,17},{... | collective-permute-start | bytes 3145736 | tf_op jit(solution)/shard_map/ppermute | solution.py:26
  949.8 37.1 %collective-permute-start.71 = (bf16[256,2048]{1,0:T(8,128)(2,1)}, bf16[256,2048]{1,0:T(8,128)(2,1)}, u32[]{:S(2)}, u32[]{:S(2)}) collective-permute-start(bf16[256,2048]{1,0:T(8,128)(2,1)} %pad_maximum_fusion.12), channel_id=1, source_target_pairs={{0,8},{4,12},{8,0},{12,4},{16,24},{20,28},{24,16},{28,20},{1,9},{5... | collective-permute-start | bytes 3145736 | tf_op jit(solution)/shard_map/ppermute | solution.py:26
  (101 other events, 1378.2 us)
Sparse Core Ops, SparseCore 0:
  28.6 62.9 all-gather.10
  106.0 29.5 all-gather.6
  162.3 80.1 all-gather.8
  244.0 79.2 all-gather.12
  616.9 77.8 reduce-scatter.8
  697.1 77.2 reduce-scatter.10
  777.8 81.4 reduce-scatter.14
  861.7 28.6 reduce-scatter.16
  893.5 45.0 reduce-scatter.18
  941.3 60.7 reduce-scatter.12
